TPU v7x, 32 devices: a whole 2x2x4 slice. The times are simulated.
32 devices in a mesh: ns: 8 (over y, x, core), ew: 4 (over z).
Axes of the slice: x: 2, y: 2, z: 4, core: 2. Of those that a mesh axis runs over, the one named last changes fastest.
Arguments:
- tokens: bfloat16 [64, 512, 512], P('ns', 'ew'), may hold values from -6 to 6
- conv_gain: float32 [512], replicated, may hold values from 0.1 to 1.9
- w_expand: bfloat16 [512, 2048], replicated, may hold values from -0.25 to 0.25
- dw_kernel: float32 [3, 3, 2048], replicated, may hold values from -2 to 2
- w_project: bfloat16 [2048, 512], replicated, may hold values from -0.375 to 0.375
- block_gain: float32 [512], replicated, may hold values from 0.1 to 1.9
- block_qkv: bfloat16 [512, 1536], replicated, may hold values from -2 to 2
- block_out: bfloat16 [512, 512], replicated, may hold values from -0.25 to 0.25
- grid_gain: float32 [512], replicated, may hold values from 0.1 to 1.9
- grid_qkv: bfloat16 [512, 1536], replicated, may hold values from -2 to 2
- grid_out: bfloat16 [512, 512], replicated, may hold values from -0.25 to 0.25
Outputs:
- block_output: bfloat16 [64, 512, 512], P('ns', 'ew')
All inputs are finite; a program needn't handle non-finite values.
Results may differ from a plain program's by a relative error of at most 0.017.
Values may be sent and summed in bfloat16 or wider, within the bound.
No kernel may reach another device: no remote copies, remote signals or barrier semaphores. Data moves between devices by JAX's collectives and lax.ppermute only.
A program may use at most 128 MiB of HBM per device.

v0:
```python
import jax
import jax.numpy as jnp
from jax import lax
from jax.sharding import PartitionSpec as P

HEADS = 16
WINDOW = 8


def with_halo(block, sides, width):
    for axis, dim in sides:
        count = lax.axis_size(axis)
        forward = [(i, i + 1) for i in range(count - 1)]
        backward = [(target, source) for source, target in forward]
        low = lax.ppermute(
            lax.slice_in_dim(block, block.shape[dim] - width, None, axis=dim), axis, forward
        )
        high = lax.ppermute(lax.slice_in_dim(block, 0, width, axis=dim), axis, backward)
        block = jnp.concatenate([low, block, high], axis=dim)
    return block


def normalize(tokens, scale_gain):
    floats = tokens.astype(jnp.float32)
    center = floats - jnp.mean(floats, axis=-1, keepdims=True)
    spread = jnp.mean(center * center, axis=-1, keepdims=True)
    return (center * lax.rsqrt(spread + 1e-05) * scale_gain).astype(jnp.bfloat16)


def expand_rows(tokens, scale_gain, w_expand):
    normed = normalize(tokens, scale_gain)
    flat_tokens = normed.reshape(-1, normed.shape[-1])
    hidden = jax.nn.gelu(jnp.dot(flat_tokens, w_expand, preferred_element_type=jnp.float32))
    return hidden.astype(jnp.bfloat16).reshape(tokens.shape[:-1] + (w_expand.shape[1],))


def depthwise(padded, dw_kernel, tile_rows, tile_cols):
    summed = jnp.zeros((tile_rows, tile_cols, padded.shape[-1]), jnp.float32)
    for offset_row in range(3):
        for offset_col in range(3):
            summed = (
                summed
                + padded[
                    offset_row : offset_row + tile_rows, offset_col : offset_col + tile_cols
                ].astype(jnp.float32)
                * dw_kernel[offset_row, offset_col]
            )
    return jax.nn.gelu(summed).astype(jnp.bfloat16)


def attend(tokens, scale_gain, w_qkv, w_out):
    layout = tokens.shape
    dim_p, dim_w, dim_q, dim_s, channels = layout
    head_dim = channels // HEADS
    normed = normalize(tokens, scale_gain).reshape(-1, channels)
    packed = jnp.dot(normed, w_qkv, preferred_element_type=jnp.float32).astype(jnp.bfloat16)
    packed = packed.reshape(dim_p, dim_w, dim_q, dim_s, 3, HEADS, head_dim)
    moved = jnp.transpose(packed, (4, 1, 3, 5, 0, 2, 6)).reshape(
        3, dim_w * dim_s, HEADS, dim_p * dim_q, head_dim
    )
    queries = moved[0]
    key_rows = moved[1]
    value_rows = moved[2]
    scores = jnp.einsum(
        "nhqd,nhkd->nhqk", queries, key_rows, preferred_element_type=jnp.float32
    ) * head_dim ** (-0.5)
    weights = jax.nn.softmax(scores, axis=-1).astype(jnp.bfloat16)
    blended = jnp.einsum(
        "nhqk,nhkd->nhqd", weights, value_rows, preferred_element_type=jnp.float32
    ).astype(jnp.bfloat16)
    blended = blended.reshape(dim_w, dim_s, HEADS, dim_p, dim_q, head_dim)
    blended = jnp.transpose(blended, (3, 0, 4, 1, 2, 5)).reshape(-1, channels)
    result = tokens.astype(jnp.float32).reshape(-1, channels) + jnp.dot(
        blended, w_out, preferred_element_type=jnp.float32
    )
    return result.astype(jnp.bfloat16).reshape(layout)


def on_device(
    tokens,
    conv_gain,
    w_expand,
    dw_kernel,
    w_project,
    block_gain,
    block_qkv,
    block_out,
    grid_gain,
    grid_qkv,
    grid_out,
):
    tile_rows, tile_cols, channels = tokens.shape
    band_count = lax.axis_size("ns")
    strip_count = lax.axis_size("ew")
    bordered = with_halo(tokens, (("ns", 0), ("ew", 1)), 1)
    hidden = expand_rows(bordered, conv_gain, w_expand)
    row_place = lax.axis_index("ns") * tile_rows - 1 + jnp.arange(tile_rows + 2, dtype=jnp.int32)
    col_place = lax.axis_index("ew") * tile_cols - 1 + jnp.arange(tile_cols + 2, dtype=jnp.int32)
    row_inside = (row_place >= 0) & (row_place < tile_rows * band_count)
    col_inside = (col_place >= 0) & (col_place < tile_cols * strip_count)
    inside = row_inside[:, None] & col_inside[None, :]
    padded = jnp.where(inside[:, :, None], hidden, jnp.zeros_like(hidden))
    active = depthwise(padded, dw_kernel, tile_rows, tile_cols)
    update = jnp.dot(
        active.reshape(-1, active.shape[-1]), w_project, preferred_element_type=jnp.float32
    )
    after_conv = (
        tokens.astype(jnp.float32) + update.reshape(tile_rows, tile_cols, channels)
    ).astype(jnp.bfloat16)
    shaped = after_conv.reshape(tile_rows, tile_cols // WINDOW, WINDOW, 1, channels)
    after_block = attend(shaped, block_gain, block_qkv, block_out)
    stride_cols = tile_cols * strip_count // WINDOW
    per_strip = WINDOW // strip_count
    shared = stride_cols // band_count
    local_rows = tile_rows // strip_count
    sectioned = after_block.reshape(1, tile_rows, per_strip, stride_cols, channels)
    grouped = lax.all_to_all(
        lax.all_to_all(sectioned, "ns", split_axis=3, concat_axis=0, tiled=True),
        "ew",
        split_axis=1,
        concat_axis=2,
        tiled=True,
    )
    windows = grouped.reshape(WINDOW, band_count // WINDOW * local_rows, WINDOW, shared, channels)
    attended = attend(windows, grid_gain, grid_qkv, grid_out)
    attended = attended.reshape(band_count, local_rows, WINDOW, shared, channels)
    returned = lax.all_to_all(
        lax.all_to_all(attended, "ns", split_axis=0, concat_axis=3, tiled=True),
        "ew",
        split_axis=2,
        concat_axis=1,
        tiled=True,
    )
    return returned.reshape(tile_rows, tile_cols, channels)


def solution(mesh):
    in_specs = (P("ns", "ew", None), P(), P(), P(), P(), P(), P(), P(), P(), P(), P())
    out_specs = P("ns", "ew", None)
    return jax.shard_map(
        on_device, mesh=mesh, in_specs=in_specs, out_specs=out_specs, check_vma=False
    )
```

profile of v0, /device:TPU:0, one launch (start us, length us, event | category | flops | bytes accessed | tf_op | source)
XLA Modules:
  0.0 310.2 jit_solution(17202727372299461342)
XLA Ops:
  0.0 1.8 fusion.63
  1.8 1.3 collective-permute-start.1
  3.1 3.7 %collective-permute-start = (bf16[1,128,512]{2,1,0:T(8,128)(2,1)S(1)}, bf16[1,128,512]{2,1,0:T(8,128)(2,1)}, u32[]{:S(2)}, u32[]{:S(2)}) collective-permute-start(bf16[1,128,512]{2,1,0:T(8,128)(2,1)S(1)} %get-tuple-element.11), channel_id=1, source_target_pairs={{0,4},{4,8},{8,12},{12,16},{16,20},{20,24},{24,28},{1,5},{5,9},{9,... | collective-permute-start | bytes 393224 | tf_op jit(solution)/shard_map/ppermute | solution.py:15
  6.8 1.6 fusion.64
  8.4 0.5 compare_and_fusion.1
  8.9 0.9 constant_dynamic-update-slice_fusion.2
  9.8 1.3 constant_dynamic-update-slice_fusion.1
  11.3 4.9 %collective-permute-start.2 = (bf16[10,1,512]{2,1,0:T(2,128)(2,1)S(1)}, bf16[10,1,512]{2,1,0:T(2,128)(2,1)S(1)}, u32[]{:S(2)}, u32[]{:S(2)}) collective-permute-start(bf16[10,1,512]{2,1,0:T(2,128)(2,1)S(1)} %get-tuple-element.8), channel_id=1, source_target_pairs={{0,1},{1,2},{2,3},{4,5},{5,6},{6,7},{8,9},{9,10},{10,11},{12,13},{... | collective-permute-start | bytes 30728 | tf_op jit(solution)/shard_map/ppermute | solution.py:15
  16.2 1.3 collective-permute-start.3
  17.5 0.7 broadcast_and_fusion
  18.2 3.7 %collective-permute-done.3 = bf16[10,1,512]{2,1,0:T(2,128)(2,1)S(1)} collective-permute-done((bf16[10,1,512]{2,1,0:T(2,128)(2,1)S(1)}, bf16[10,1,512]{2,1,0:T(2,128)(2,1)S(1)}, u32[]{:S(2)}, u32[]{:S(2)}) %collective-permute-start.3) | collective-permute-done | bytes 10272 | tf_op jit(solution)/shard_map/ppermute | solution.py:18
  21.9 0.5 fusion.60
  22.4 0.1 div.41
  22.5 1.3 multiply_reduce_fusion.2
  23.7 0.1 rsqrt.34
  23.9 2.0 maximum_convert_fusion
  25.9 4.0 %reshape.233 = f32[1300,512]{1,0:T(8,128)} reshape(f32[10,130,512]{2,1,0:T(8,128)} %maximum_convert_fusion) | data formatting | bytes 5324800 | tf_op jit(solution)/shard_map/convert_element_type | solution.py:24
  29.8 8.4 %fusion.9 = bf16[1300,2048]{1,0:T(8,128)(2,1)} fusion(bf16[512,2048]{1,0:T(8,128)(2,1)S(1)} %copy-done, f32[1300,512]{1,0:T(8,128)} %reshape.233, f32[512]{0:T(512)S(1)} %copy-done.15, f32[1300]{0:T(1024)S(1)} %rsqrt.34, f32[1300]{0:T(1024)S(1)} %div.41), kind=kOutput, calls=%fused_computation.13 | convolution fusion | flops 2752921600 | bytes 10096800 | tf_op jit(solution)/shard_map/dot_general | solution.py:33
  38.2 5.4 %reshape.224 = bf16[10,130,2048]{2,1,0:T(8,128)(2,1)} reshape(bf16[1300,2048]{1,0:T(8,128)(2,1)} %fusion.9) | data formatting | bytes 10649600 | tf_op jit(solution)/shard_map/reshape | solution.py:34
  43.7 3.1 %broadcast_select_fusion = bf16[10,130,2048]{2,1,0:T(8,128)(2,1)S(1)} fusion(bf16[10,130,2048]{2,1,0:T(8,128)(2,1)} %reshape.224, pred[10,130]{1,0:T(8,128)(4,1)S(1)} %broadcast_and_fusion), kind=kLoop, calls=%fused_computation.30 | loop fusion | flops 2662400 | bytes 10650900 | tf_op jit(solution)/shard_map/jit(_where)/select_n | solution.py:102
  46.9 0.0 copy-start.11
  46.9 13.7 %convert_reduce_fusion = (f32[8,128]{1,0:T(8,128)S(1)}, bf16[8,128,512]{2,1,0:T(8,128)(2,1)S(1)}) fusion(bf16[2048,512]{1,0:T(8,128)(2,1)} %param.15, bf16[10,130,2048]{2,1,0:T(8,128)(2,1)S(1)} %broadcast_select_fusion, f32[2048]{0:T(1024)S(1)} %bitcast.135, f32[2048]{0:T(1024)S(1)} %bitcast.136, f32[2048]{0:T(1024)S(1)} %bitcast.129, ...), kind=kOutput, calls=%fused_computation.53 | convolution fusion | flops 2223504384 | bytes 42020864 | tf_op jit(solution)/shard_map/dot_general | solution.py:104
  60.7 0.5 fusion.36
  61.2 0.4 fusion.39
  61.6 4.9 %convolution_convert_fusion.1 = bf16[1024,1536]{1,0:T(8,128)(2,1)} fusion(bf16[1024,512]{1,0:T(8,128)(2,1)S(1)} %fusion.39, bf16[512,1536]{1,0:T(8,128)(2,1)} %param.17), kind=kOutput, calls=%fused_computation.41 | convolution fusion | flops 1612185600 | bytes 5767168 | tf_op jit(solution)/shard_map/dot_general | solution.py:56
  66.5 14.6 %reshape.225 = bf16[8,16,8,1,3,16,32]{6,5,4,2,1,0,3:T(8,128)(2,1)} reshape(bf16[1024,1536]{1,0:T(8,128)(2,1)} %convolution_convert_fusion.1) | data formatting | bytes 6291456 | tf_op jit(solution)/shard_map/reshape | solution.py:57
  81.1 8.8 %copy.126 = bf16[8,16,8,1,3,16,32]{6,2,0,5,1,3,4:T(8,128)(2,1)S(1)} copy(bf16[8,16,8,1,3,16,32]{6,5,4,2,1,0,3:T(8,128)(2,1)} %reshape.225) | data formatting | bytes 6291456 | tf_op jit(solution)/shard_map/reshape | solution.py:57
  89.8 6.3 %fusion.25 = f32[16,16,64,64]{2,3,1,0:T(8,128)} fusion(bf16[3,16,1,16,8,8,32]{6,5,4,3,1,2,0:T(8,128)(2,1)S(1)} %bitcast.113), kind=kOutput, calls=%fused_computation.34 | convolution fusion | flops 67108864 | bytes 12582912 | tf_op jit(solution)/shard_map/nhqd,nhkd->nhqk/dot_general | solution.py:64
  96.1 0.9 copy-done.2
  97.1 11.6 %fusion.65 = (f32[16,16,64]{2,1,0:T(8,128)S(1)}, f32[16,16,64,64]{2,3,1,0:T(8,128)}) fusion(f32[16,16,64,64]{2,3,1,0:T(8,128)} %fusion.25), kind=kOutput, calls=%fused_computation.97 | output fusion | flops 4194367 | bytes 8454144 | tf_op jit(solution)/shard_map/sub | solution.py:67
  108.6 7.2 %fusion.43 = bf16[16,16,64,32]{2,3,1,0:T(8,128)(2,1)} fusion(bf16[3,16,1,16,8,8,32]{6,5,4,3,1,2,0:T(8,128)(2,1)} %bitcast.114, f32[16,16,64,64]{2,3,1,0:T(8,128)} %get-tuple-element.26, f32[16,16,64]{2,1,0:T(8,128)S(1)} %get-tuple-element.25), kind=kOutput, calls=%fused_computation.64 | convolution fusion | flops 69730304 | bytes 13697024 | tf_op jit(solution)/shard_map/nhqk,nhkd->nhqd/dot_general | solution.py:68
  115.9 5.3 %copy.84 = bf16[16,16,64,32]{3,2,1,0:T(8,128)(2,1)} copy(bf16[16,16,64,32]{2,3,1,0:T(8,128)(2,1)} %fusion.43) | data formatting | bytes 2097152 | tf_op jit(solution)/shard_map/convert_element_type | solution.py:70
  121.2 9.0 %copy.85 = bf16[8,16,8,1,16,32]{5,4,2,1,0,3:T(8,128)(2,1)} copy(bf16[8,16,8,1,16,32]{5,2,0,4,1,3:T(8,128)(2,1)} %bitcast.117) | data formatting | bytes 2097152 | tf_op jit(solution)/shard_map/transpose | solution.py:72
  130.2 6.0 %reshape.227 = bf16[1024,512]{1,0:T(8,128)(2,1)S(1)} reshape(bf16[8,16,8,1,16,32]{5,4,2,1,0,3:T(8,128)(2,1)} %copy.85) | data formatting | bytes 2097152 | tf_op jit(solution)/shard_map/reshape | solution.py:72
  136.2 0.7 fusion.40
  136.9 1.1 copy.86
  138.0 20.9 %all_to_all.60 = bf16[1,8,2,64,512]{4,2,1,0,3:T(2,128)(2,1)S(1)} all-to-all(bf16[1,8,2,64,512]{4,2,1,0,3:T(2,128)(2,1)S(1)} %copy.86), channel_id=1, replica_groups=mesh['ns'=8,'ew'=4] {'ns'}, dimensions={3} | all-to-all | bytes 2097152 | tf_op jit(solution)/shard_map/all_to_all | solution.py:118
  158.9 0.6 copy.128
  159.5 28.9 %all_to_all.61 = bf16[8,8,2,8,512]{4,3,0,2,1:T(8,128)(2,1)S(1)} all-to-all(bf16[8,8,2,8,512]{4,3,0,2,1:T(8,128)(2,1)S(1)} %bitcast.120), channel_id=1, replica_groups=mesh['ns'=8,'ew'=4] {'ew'}, dimensions={1} | all-to-all | bytes 2097152 | tf_op jit(solution)/shard_map/all_to_all | solution.py:117
  188.4 0.3 copy.88
  188.7 0.3 reduce_sum.77
  189.1 0.5 multiply_reduce_fusion.3
  189.7 0.1 rsqrt.38
  189.8 0.1 div.49
  190.0 0.3 convert_element_type.165
  190.3 0.2 copy.89
  190.5 0.4 fusion.33
  190.9 0.8 copy-done.13
  191.7 3.5 %convolution_convert_fusion = bf16[1024,1536]{1,0:T(8,128)(2,1)} fusion(bf16[1024,512]{1,0:T(8,128)(2,1)S(1)} %fusion.33, bf16[512,1536]{1,0:T(8,128)(2,1)S(1)} %copy-done.13), kind=kOutput, calls=%fused_computation.40 | convolution fusion | flops 1612185600 | bytes 5767168 | tf_op jit(solution)/shard_map/dot_general | solution.py:56
  195.1 14.6 %reshape.228 = bf16[8,2,8,8,3,16,32]{6,5,4,3,2,1,0:T(8,128)(2,1)} reshape(bf16[1024,1536]{1,0:T(8,128)(2,1)} %convolution_convert_fusion) | data formatting | bytes 6291456 | tf_op jit(solution)/shard_map/reshape | solution.py:57
  209.7 11.5 %copy.125 = bf16[8,2,8,8,3,16,32]{6,2,0,5,3,1,4:T(8,128)(2,1)S(1)} copy(bf16[8,2,8,8,3,16,32]{6,5,4,3,2,1,0:T(8,128)(2,1)} %reshape.228) | data formatting | bytes 6291456 | tf_op jit(solution)/shard_map/reshape | solution.py:57
  221.2 5.4 %fusion.61 = (bf16[1,2,8,16,8,8,32]{6,5,4,3,2,1,0:T(8,128)(2,1)}, bf16[1,2,8,16,8,8,32]{6,5,4,3,2,1,0:T(8,128)(2,1)}, bf16[1,2,8,16,8,8,32]{6,5,4,3,2,1,0:T(8,128)(2,1)}) fusion(bf16[3,2,8,16,8,8,32]{6,5,4,3,2,1,0:T(8,128)(2,1)S(1)} %bitcast.112), kind=kLoop, calls=%fused_computation.93 | loop fusion | bytes 6291456 | tf_op jit(solution)/shard_map/slice | solution.py:62
  226.6 9.5 %fusion.66 = (f32[16,16,64]{2,1,0:T(8,128)S(1)}, f32[16,16,64,64]{2,3,1,0:T(8,128)}) fusion(bf16[16,16,64,32]{3,2,1,0:T(8,128)(2,1)} %bitcast.126, bf16[16,16,64,32]{3,2,1,0:T(8,128)(2,1)} %bitcast.125), kind=kOutput, calls=%fused_computation.98 | convolution fusion | flops 70254656 | bytes 6356992 | tf_op jit(solution)/shard_map/sub | solution.py:67
  236.1 7.3 %fusion.42 = bf16[16,16,64,32]{2,3,1,0:T(8,128)(2,1)} fusion(bf16[16,16,64,32]{3,2,1,0:T(8,128)(2,1)} %bitcast.124, f32[16,16,64,64]{2,3,1,0:T(8,128)} %get-tuple-element.28, f32[16,16,64]{2,1,0:T(8,128)S(1)} %get-tuple-element.27), kind=kOutput, calls=%fused_computation.63 | convolution fusion | flops 69730304 | bytes 6356992 | tf_op jit(solution)/shard_map/nhqk,nhkd->nhqd/dot_general | solution.py:68
  243.4 5.0 %copy.100 = bf16[16,16,64,32]{3,2,1,0:T(8,128)(2,1)} copy(bf16[16,16,64,32]{2,3,1,0:T(8,128)(2,1)} %fusion.42) | data formatting | bytes 2097152 | tf_op jit(solution)/shard_map/convert_element_type | solution.py:70
  248.4 6.9 %copy.101 = bf16[8,2,8,8,16,32]{5,4,3,2,1,0:T(8,128)(2,1)} copy(bf16[8,2,8,8,16,32]{5,2,0,4,3,1:T(8,128)(2,1)} %bitcast.118) | data formatting | bytes 2097152 | tf_op jit(solution)/shard_map/transpose | solution.py:72
  255.2 5.9 %reshape.230 = bf16[1024,512]{1,0:T(8,128)(2,1)S(1)} reshape(bf16[8,2,8,8,16,32]{5,4,3,2,1,0:T(8,128)(2,1)} %copy.101) | data formatting | bytes 2097152 | tf_op jit(solution)/shard_map/reshape | solution.py:72
  261.2 1.8 fusion.34
  262.9 17.8 %all_to_all.62 = bf16[8,2,8,8,512]{4,3,2,1,0:T(8,128)(2,1)S(1)} all-to-all(bf16[8,2,8,8,512]{4,3,2,1,0:T(8,128)(2,1)S(1)} %bitcast.123), channel_id=1, replica_groups=mesh['ns'=8,'ew'=4] {'ns'}, dimensions={0} | all-to-all | bytes 2097152 | tf_op jit(solution)/shard_map/all_to_all | solution.py:128
  280.7 0.1 copy.127
  280.8 0.1 copy.103
  280.9 27.9 %all_to_all.63 = bf16[1,2,8,64,512]{4,3,1,0,2:T(8,128)(2,1)S(1)} all-to-all(bf16[1,2,8,64,512]{4,3,1,0,2:T(8,128)(2,1)S(1)} %copy.103), channel_id=1, replica_groups=mesh['ns'=8,'ew'=4] {'ew'}, dimensions={2} | all-to-all | bytes 2097152 | tf_op jit(solution)/shard_map/all_to_all | solution.py:127
  308.8 0.1 copy.104
  308.9 1.1 copy.105
  (44 shorter events, 0.3 us)
Async XLA Ops:
  0.0 29.8 %copy-start = (bf16[512,2048]{1,0:T(8,128)(2,1)S(1)}, bf16[512,2048]{1,0:T(8,128)(2,1)}, u32[]{:S(2)}) copy-start(bf16[512,2048]{1,0:T(8,128)(2,1)} %param.13) | copy-start | bytes 6291460
  1.8 9.4 %collective-permute-start.1 = (bf16[1,128,512]{2,1,0:T(8,128)(2,1)}, bf16[1,128,512]{2,1,0:T(8,128)(2,1)S(1)}, u32[]{:S(2)}, u32[]{:S(2)}) collective-permute-start(bf16[1,128,512]{2,1,0:T(8,128)(2,1)} %get-tuple-element.10), channel_id=1, source_target_pairs={{4,0},{8,4},{12,8},{16,12},{20,16},{24,20},{28,24},{5,1},{9,5},{13... | collective-permute-start | bytes 393224 | tf_op jit(solution)/shard_map/ppermute | solution.py:18
  3.1 5.8 %collective-permute-start = (bf16[1,128,512]{2,1,0:T(8,128)(2,1)S(1)}, bf16[1,128,512]{2,1,0:T(8,128)(2,1)}, u32[]{:S(2)}, u32[]{:S(2)}) collective-permute-start(bf16[1,128,512]{2,1,0:T(8,128)(2,1)S(1)} %get-tuple-element.11), channel_id=1, source_target_pairs={{0,4},{4,8},{8,12},{12,16},{16,20},{20,24},{24,28},{1,5},{5,9},{9,... | collective-permute-start | bytes 393224 | tf_op jit(solution)/shard_map/ppermute | solution.py:15
  11.3 6.9 %collective-permute-start.2 = (bf16[10,1,512]{2,1,0:T(2,128)(2,1)S(1)}, bf16[10,1,512]{2,1,0:T(2,128)(2,1)S(1)}, u32[]{:S(2)}, u32[]{:S(2)}) collective-permute-start(bf16[10,1,512]{2,1,0:T(2,128)(2,1)S(1)} %get-tuple-element.8), channel_id=1, source_target_pairs={{0,1},{1,2},{2,3},{4,5},{5,6},{6,7},{8,9},{9,10},{10,11},{12,13},{... | collective-permute-start | bytes 30728 | tf_op jit(solution)/shard_map/ppermute | solution.py:15
  16.2 5.7 %collective-permute-start.3 = (bf16[10,1,512]{2,1,0:T(2,128)(2,1)S(1)}, bf16[10,1,512]{2,1,0:T(2,128)(2,1)S(1)}, u32[]{:S(2)}, u32[]{:S(2)}) collective-permute-start(bf16[10,1,512]{2,1,0:T(2,128)(2,1)S(1)} %get-tuple-element.9), channel_id=1, source_target_pairs={{1,0},{2,1},{3,2},{5,4},{6,5},{7,6},{9,8},{10,9},{11,10},{13,12},{... | collective-permute-start | bytes 30728 | tf_op jit(solution)/shard_map/ppermute | solution.py:18
  23.8 6.0 %copy-start.15 = (f32[512]{0:T(512)S(1)}, f32[512]{0:T(512)}, u32[]{:S(2)}) copy-start(f32[512]{0:T(512)} %param.12) | copy-start | bytes 6148
  43.7 3.2 %copy-start.3 = (bf16[8,128,512]{2,1,0:T(8,128)(2,1)S(1)}, bf16[8,128,512]{2,1,0:T(8,128)(2,1)}, u32[]{:S(2)}) copy-start(bf16[8,128,512]{2,1,0:T(8,128)(2,1)} %param.11) | copy-start | bytes 3145732
  43.7 3.2 %copy-start.4 = (f32[1,1,2048]{2,1,0:T(1,128)S(1)}, f32[1,1,2048]{2,1,0:T(1,128)}, u32[]{:S(2)}) copy-start(f32[1,1,2048]{2,1,0:T(1,128)} %get-tuple-element.14) | copy-start | bytes 24580
  43.7 3.2 %copy-start.5 = (f32[1,1,2048]{2,1,0:T(1,128)S(1)}, f32[1,1,2048]{2,1,0:T(1,128)}, u32[]{:S(2)}) copy-start(f32[1,1,2048]{2,1,0:T(1,128)} %get-tuple-element.15) | copy-start | bytes 24580
  43.7 3.2 %copy-start.6 = (f32[1,1,2048]{2,1,0:T(1,128)S(1)}, f32[1,1,2048]{2,1,0:T(1,128)}, u32[]{:S(2)}) copy-start(f32[1,1,2048]{2,1,0:T(1,128)} %get-tuple-element.16) | copy-start | bytes 24580
  43.7 3.2 %copy-start.7 = (f32[1,1,2048]{2,1,0:T(1,128)S(1)}, f32[1,1,2048]{2,1,0:T(1,128)}, u32[]{:S(2)}) copy-start(f32[1,1,2048]{2,1,0:T(1,128)} %get-tuple-element.17) | copy-start | bytes 24580
  43.7 3.2 %copy-start.8 = (f32[1,1,2048]{2,1,0:T(1,128)S(1)}, f32[1,1,2048]{2,1,0:T(1,128)}, u32[]{:S(2)}) copy-start(f32[1,1,2048]{2,1,0:T(1,128)} %get-tuple-element.18) | copy-start | bytes 24580
  43.7 3.2 %copy-start.9 = (f32[1,1,2048]{2,1,0:T(1,128)S(1)}, f32[1,1,2048]{2,1,0:T(1,128)}, u32[]{:S(2)}) copy-start(f32[1,1,2048]{2,1,0:T(1,128)} %get-tuple-element.19) | copy-start | bytes 24580
  43.7 3.2 %copy-start.10 = (f32[1,1,2048]{2,1,0:T(1,128)S(1)}, f32[1,1,2048]{2,1,0:T(1,128)}, u32[]{:S(2)}) copy-start(f32[1,1,2048]{2,1,0:T(1,128)} %get-tuple-element.20) | copy-start | bytes 24580
  46.9 14.3 %copy-start.11 = (f32[512]{0:T(512)S(1)}, f32[512]{0:T(512)}, u32[]{:S(2)}) copy-start(f32[512]{0:T(512)} %param.16) | copy-start | bytes 6148
  89.8 7.2 %copy-start.2 = (bf16[8,16,8,1,3,16,32]{6,2,0,5,1,3,4:T(8,128)(2,1)}, bf16[8,16,8,1,3,16,32]{6,2,0,5,1,3,4:T(8,128)(2,1)S(1)}, u32[]{:S(2)}) copy-start(bf16[8,16,8,1,3,16,32]{6,2,0,5,1,3,4:T(8,128)(2,1)S(1)} %copy.126) | copy-start | bytes 9437188
  130.2 6.0 %copy-start.14 = (bf16[512,512]{1,0:T(8,128)(2,1)S(1)}, bf16[512,512]{1,0:T(8,128)(2,1)}, u32[]{:S(2)}) copy-start(bf16[512,512]{1,0:T(8,128)(2,1)} %param.18) | copy-start | bytes 1572868
  189.6 0.9 copy-start.12
  190.3 1.4 copy-start.13
  280.8 29.2 %copy-start.1 = (bf16[512,2048]{1,0:T(8,128)(2,1)S(1)}, bf16[512,2048]{1,0:T(8,128)(2,1)}, u32[]{:S(2)}) copy-start(bf16[512,2048]{1,0:T(8,128)(2,1)} %param.13) | copy-start | bytes 6291460
where the time goes:
time: 315 us; the launch traced here: 310 us
  local copies, waits for them, and re-layouts  114 us (36%)
  blocking collectives  95.5 us (30%)
  matrix products  63.2 us (20%)
  other arithmetic  22 us (7%)
  starting transfers between devices  11.2 us (4%)
  waiting for transfers between devices  3.71 us (1%)
    reshape x4, local copies, waits for them, and re-layouts, attend(): packed = packed.reshape(dim_p, dim_w, dim_q, dim_s, 3, HEADS, head_dim)  49.4 us
    all_to_all x1, blocking collectives, on_device(): lax.all_to_all(lax.all_to_all(sectioned, 'ns', split_axis=3, concat_axis=...  28.9 us
    all_to_all x1, blocking collectives, on_device(): lax.all_to_all(lax.all_to_all(attended, 'ns', split_axis=0, concat_axis=3...  27.9 us
    all_to_all x1, blocking collectives, on_device(): lax.all_to_all(sectioned, 'ns', split_axis=3, concat_axis=0, tiled=True)  20.9 us
    all_to_all x1, blocking collectives, on_device(): lax.all_to_all(attended, 'ns', split_axis=0, concat_axis=3, tiled=True)  17.8 us
    transpose x2, local copies, waits for them, and re-layouts, attend(): blended = jnp.transpose(blended, (3, 0, 4, 1, 2, 5)).reshape(-1, channels)  15.9 us
    dot_general x2, matrix products, attend(): jnp.einsum('nhqk,nhkd->nhqd', weights, value_rows, preferred_element_type...  14.5 us
    dot_general x1, matrix products, on_device(): jnp.dot(active.reshape(-1, active.shape[-1]), w_project, preferred_elemen...  13.7 us
  transfers between devices with their start and end apart: 4, of which 1 were waited for; matrix products, arithmetic and copies ran while one was open for 2% of the time, Pallas kernels for 0%

commit v1 on v0

v1 whole, which is shorter than its diff:
```python
import functools
import math

import jax
import jax.numpy as jnp
from jax import lax
from jax.experimental import pallas as pl
from jax.experimental.pallas import tpu as pltpu
from jax.sharding import PartitionSpec as P

HEADS = 16
WINDOW = 8
FEATURES = 256
LANES = 128
GROUP = 4
VMEM_LIMIT = 56 * 1024 * 1024

NT = (((1,), (1,)), ((), ()))


def normalize(floats, scale_gain):
    center = floats - jnp.mean(floats, axis=-1, keepdims=True)
    spread = jnp.mean(center * center, axis=-1, keepdims=True)
    return center * lax.rsqrt(spread + 1e-05) * scale_gain


def gelu(v):
    inner = v * (math.sqrt(2 / math.pi) + (math.sqrt(2 / math.pi) * 0.044715) * (v * v))
    half = 0.5 * v
    return half + half * jnp.tanh(inner)


def tiles(value):
    return [value[:, t : t + LANES] for t in range(0, value.shape[1], LANES)]


def strided(ref, start, size, stride):
    return jnp.concatenate([ref[t, pl.ds(start, size, stride=stride), :] for t in range(ref.shape[0])], axis=1)


def conv_kernel(
    slot_of, x_ref, edge_ref, side_ref, gain_ref, w1_ref, dw_ref, w2_ref, out_ref, n_ref, tmp_ref, e_ref, acc_ref
):
    step = pl.program_id(0)
    rows, cols, _ = x_ref.shape
    strips = cols // WINDOW
    features = w1_ref.shape[1]
    side_count = side_ref.shape[0] // 2
    gain = gain_ref[...]

    @pl.when(step == 0)
    def _():
        def place(slot, block):
            for t, part in enumerate(tiles(normalize(block.astype(jnp.float32), gain))):
                tmp_ref[t] = part
            for b in range(WINDOW):
                start = pl.multiple_of(slot * cols + b * strips, strips)
                n_ref[pl.ds(start, strips), :] = strided(tmp_ref, b, strips, WINDOW).astype(jnp.bfloat16)

        @pl.loop(0, rows)
        def _(i):
            place(i + 1, x_ref[i])

        place(0, edge_ref[0])
        place(rows + 1, edge_ref[1])
        n_ref[pl.ds((rows + 2) * cols, 2 * side_count), :] = normalize(
            side_ref[...].astype(jnp.float32), gain
        ).astype(jnp.bfloat16)
        acc_ref[...] = jnp.zeros_like(acc_ref)

    w1 = w1_ref[...]
    w2 = w2_ref[...]
    taps = [[dw_ref[3 * a + b : 3 * a + b + 1, :].astype(jnp.bfloat16) for b in range(3)] for a in range(3)]
    sides = gelu(
        jnp.dot(n_ref[pl.ds((rows + 2) * cols, 2 * side_count), :], w1, preferred_element_type=jnp.float32)
    )
    place_in_strip = lax.broadcasted_iota(jnp.int32, (strips, features), 0)

    def expand(i):
        hidden = gelu(
            jnp.dot(n_ref[pl.ds(i * cols, cols), :], w1, preferred_element_type=jnp.float32).astype(jnp.bfloat16)
        )
        e_ref[i, 1 : WINDOW + 1] = hidden.reshape(WINDOW, strips, features)
        last = pltpu.roll(hidden[(WINDOW - 1) * strips :].astype(jnp.float32), 1, axis=0)
        first = pltpu.roll(hidden[:strips].astype(jnp.float32), strips - 1, axis=0)
        low = jnp.where(place_in_strip == 0, sides[i : i + 1], last)
        high = jnp.where(place_in_strip == strips - 1, sides[side_count + i : side_count + i + 1], first)
        e_ref[i, 0] = low.astype(jnp.bfloat16)
        e_ref[i, WINDOW + 1] = high.astype(jnp.bfloat16)

    def contract(i):
        pieces = []
        for b in range(WINDOW):
            parts = []
            for da in range(3):
                t = [e_ref[i + da, b + db] * taps[da][db] for db in range(3)]
                parts.append(t[0] + t[1] + t[2])
            pieces.append(gelu(parts[0] + parts[1] + parts[2]))
        active = jnp.concatenate(pieces, axis=0)
        for t, part in enumerate(tiles(jnp.dot(active, w2, preferred_element_type=jnp.float32))):
            acc_ref[t, i * cols : (i + 1) * cols, :] += part

    for i in range(rows + 2):
        expand(i)
        if i >= 2:
            contract(i - 2)

    @pl.when(step == pl.num_programs(0) - 1)
    def _():
        for pair in range(strips // 2):
            tokens = x_ref[:, pair * 2 * WINDOW : (pair + 1) * 2 * WINDOW, :].astype(jnp.float32)
            for odd in range(2):
                window = 2 * pair + odd
                own = tokens[:, odd * WINDOW : (odd + 1) * WINDOW, :].reshape(rows * WINDOW, -1)
                summed = own + strided(acc_ref, window, rows * WINDOW, strips)
                out_ref[slot_of(window)] = summed.astype(jnp.bfloat16)


def conv_block(tokens, edge, side, gain, w_expand, dw_kernel, w_project, slot_of):
    rows, cols, channels = tokens.shape
    width = w_expand.shape[1]
    features = min(FEATURES, width)
    strips = cols // WINDOW
    whole = lambda *shape: pl.BlockSpec(shape, lambda f: (0,) * len(shape))
    return pl.pallas_call(
        functools.partial(conv_kernel, slot_of),
        grid=(width // features,),
        out_shape=jax.ShapeDtypeStruct((strips, rows * WINDOW, channels), jnp.bfloat16),
        in_specs=[
            whole(*tokens.shape),
            whole(*edge.shape),
            whole(*side.shape),
            whole(1, channels),
            pl.BlockSpec((channels, features), lambda f: (0, f)),
            pl.BlockSpec((9, features), lambda f: (0, f)),
            pl.BlockSpec((features, channels), lambda f: (f, 0)),
        ],
        out_specs=whole(strips, rows * WINDOW, channels),
        scratch_shapes=[
            pltpu.VMEM(((rows + 2) * cols + side.shape[0], channels), jnp.bfloat16),
            pltpu.VMEM((channels // LANES, cols, LANES), jnp.float32),
            pltpu.VMEM((rows + 2, WINDOW + 2, strips, features), jnp.bfloat16),
            pltpu.VMEM((channels // LANES, rows * cols, LANES), jnp.float32),
        ],
        compiler_params=pltpu.CompilerParams(
            dimension_semantics=("arbitrary",), vmem_limit_bytes=VMEM_LIMIT
        ),
        cost_estimate=pl.CostEstimate(
            flops=4 * rows * cols * channels * width,
            bytes_accessed=4 * channels * width + 4 * rows * cols * channels,
            transcendentals=2 * rows * cols * width,
        ),
        name="conv_block",
    )(
        tokens,
        edge,
        side,
        gain.reshape(1, channels),
        w_expand,
        dw_kernel.reshape(9, width),
        w_project,
    )


def attend_windows(x, gain, wqk, wvt, wout):
    tokens, channels = x.shape
    head_dim = channels // HEADS
    group = LANES // head_dim
    size = WINDOW * WINDOW
    scale = math.log2(math.e) / math.sqrt(head_dim)
    normed = normalize(x, gain).astype(jnp.bfloat16)
    queries = (jnp.dot(normed, wqk[:, :channels], preferred_element_type=jnp.float32) * scale).astype(jnp.bfloat16)
    keys = jnp.dot(normed, wqk[:, channels : 2 * channels], preferred_element_type=jnp.float32).astype(jnp.bfloat16)
    values = lax.dot_general(wvt, normed, NT, preferred_element_type=jnp.float32).astype(jnp.bfloat16)
    lane = lax.broadcasted_iota(jnp.int32, (size, LANES), 1)
    head_lanes = [lane // head_dim == h for h in range(group)]
    half = lax.broadcasted_iota(jnp.int32, (LANES, 2 * size), 1) // size
    block_row = lax.broadcasted_iota(jnp.int32, (2 * LANES, group * size), 0) % LANES // head_dim
    block_col = lax.broadcasted_iota(jnp.int32, (2 * LANES, group * size), 1) // size
    own_block = block_row == block_col
    pick = (
        lax.broadcasted_iota(jnp.int32, (size, group * size), 0)
        == lax.broadcasted_iota(jnp.int32, (size, group * size), 1) % size
    ).astype(jnp.bfloat16)
    zero = jnp.zeros((), jnp.bfloat16)
    blended = []
    for pair in range(tokens // (2 * size)):
        parts = []
        for g in range(channels // LANES):
            weights = []
            for odd in range(2):
                at = (2 * pair + odd) * size
                q = queries[at : at + size, g * LANES : (g + 1) * LANES]
                k = keys[at : at + size, g * LANES : (g + 1) * LANES]
                q_heads = jnp.concatenate([jnp.where(m, q, zero) for m in head_lanes], axis=0)
                scores = lax.dot_general(k, q_heads, NT, preferred_element_type=jnp.float32)
                raised = jnp.exp2(scores - jnp.max(scores, axis=0, keepdims=True))
                weights.append(
                    (raised * (1.0 / jnp.sum(raised, axis=0, keepdims=True))).astype(jnp.bfloat16)
                )
            v = values[g * LANES : (g + 1) * LANES, pair * 2 * size : (pair + 1) * 2 * size]
            v_halves = jnp.concatenate([jnp.where(half == 0, v, zero), jnp.where(half == 1, v, zero)], axis=0)
            mixed = jnp.dot(v_halves, jnp.concatenate(weights, axis=0), preferred_element_type=jnp.float32)
            mixed = jnp.where(own_block, mixed, 0.0).astype(jnp.bfloat16)
            parts.append(lax.dot_general(pick, mixed, NT, preferred_element_type=jnp.float32).astype(jnp.bfloat16))
        for odd in range(2):
            blended.append(
                jnp.concatenate([part[:, odd * LANES : (odd + 1) * LANES] for part in parts], axis=1)
            )
    return x + jnp.dot(jnp.concatenate(blended, axis=0), wout, preferred_element_type=jnp.float32)


def window_kernel(x_ref, gain_ref, wqk_ref, wvt_ref, wout_ref, out_ref):
    count, size, channels = x_ref.shape
    _, places, shares, side, _ = out_ref.shape
    x = x_ref[...].astype(jnp.float32).reshape(count * size, channels)
    result = attend_windows(x, gain_ref[...], wqk_ref, wvt_ref[...], wout_ref[...]).astype(jnp.bfloat16)
    result = result.reshape(places, shares, size // side, side, channels)
    for j in range(places):
        for share in range(shares):
            out_ref[:, j, share] = result[j, share]


def attention_call(kernel, name, grid, x, x_spec, gain, weights, out_shape, out_spec, scratch):
    channels = x.shape[-1]
    tokens = x.size // channels
    whole = lambda array: pl.BlockSpec(array.shape, lambda step: (0,) * array.ndim)
    gain = gain.reshape(1, channels)
    return pl.pallas_call(
        kernel,
        grid=(grid,),
        out_shape=jax.ShapeDtypeStruct(out_shape, jnp.bfloat16),
        in_specs=[x_spec, whole(gain)] + [whole(w) for w in weights],
        out_specs=out_spec,
        scratch_shapes=scratch,
        compiler_params=pltpu.CompilerParams(
            dimension_semantics=("arbitrary",), vmem_limit_bytes=VMEM_LIMIT
        ),
        cost_estimate=pl.CostEstimate(
            flops=16 * tokens * channels * channels,
            bytes_accessed=8 * channels * channels + 4 * tokens * channels,
            transcendentals=HEADS * tokens * WINDOW * WINDOW,
        ),
        name=name,
    )(x, gain, *weights)


def window_attention(x, chunk, chunks, shares, gain, weights):
    windows, size, channels = x.shape
    per_chunk = windows // chunks
    block = min(GROUP, per_chunk)
    steps = per_chunk // block
    return attention_call(
        window_kernel,
        "window_attention",
        steps,
        x,
        pl.BlockSpec((block, size, channels), lambda step: (chunk * steps + step, 0, 0)),
        gain,
        weights,
        (size // WINDOW, per_chunk // shares, shares, WINDOW, channels),
        pl.BlockSpec((size // WINDOW, block // shares, shares, WINDOW, channels), lambda step: (0, step, 0, 0, 0)),
        [],
    )


def grid_kernel(x_ref, gain_ref, wqk_ref, wvt_ref, wout_ref, out_ref, floats_ref):
    step = pl.program_id(0)
    tokens, channels = x_ref.shape
    size = WINDOW * WINDOW
    windows = tokens // size
    block = windows // pl.num_programs(0)

    @pl.when(step == 0)
    def _():
        for t, part in enumerate(tiles(x_ref[...])):
            floats_ref[t] = part.astype(jnp.float32)

    first = step * block
    x = jnp.concatenate([strided(floats_ref, first + w, size, windows) for w in range(block)], axis=0)
    result = attend_windows(x, gain_ref[...], wqk_ref, wvt_ref[...], wout_ref[...])
    for t, part in enumerate(tiles(result)):
        for w in range(block):
            floats_ref[t, pl.ds(first + w, size, stride=windows), :] = part[w * size : (w + 1) * size]

    @pl.when(step == pl.num_programs(0) - 1)
    def _():
        for t in range(floats_ref.shape[0]):
            out_ref[:, t * LANES : (t + 1) * LANES] = floats_ref[t].astype(jnp.bfloat16)


def grid_attention(x, gain, weights):
    tokens, channels = x.shape
    windows = tokens // (WINDOW * WINDOW)
    spec = pl.BlockSpec((tokens, channels), lambda step: (0, 0))
    return attention_call(
        grid_kernel,
        "grid_attention",
        windows // min(GROUP, windows),
        x,
        spec,
        gain,
        weights,
        (tokens, channels),
        spec,
        [pltpu.VMEM((channels // LANES, tokens, LANES), jnp.float32)],
    )


def halo(tokens):
    rows, cols, channels = tokens.shape
    bands = [(i, i + 1) for i in range(lax.axis_size("ns") - 1)]
    strips = [(i, i + 1) for i in range(lax.axis_size("ew") - 1)]
    back = lambda pairs: [(target, source) for source, target in pairs]
    north = lax.ppermute(tokens[rows - 1], "ns", bands)
    south = lax.ppermute(tokens[0], "ns", back(bands))
    west = lax.ppermute(
        jnp.concatenate([north[None, cols - 1], tokens[:, cols - 1], south[None, cols - 1]]), "ew", strips
    )
    east = lax.ppermute(jnp.concatenate([north[None, 0], tokens[:, 0], south[None, 0]]), "ew", back(strips))
    pad = ((0, -(rows + 2) % 16), (0, 0))
    return jnp.stack([north, south]), jnp.concatenate([jnp.pad(west, pad), jnp.pad(east, pad)])


def exchange(x):
    bands, strips = lax.axis_size("ns"), lax.axis_size("ew")
    if bands == WINDOW:
        return lax.all_to_all(x, ("ns", "ew"), 0, 0, tiled=True)
    inner = bands // WINDOW
    groups = [[a * inner + p for a in range(WINDOW)] for p in range(inner)]
    shape = x.shape
    x = x.reshape(WINDOW, strips, *shape[1:])
    x = lax.all_to_all(x, "ns", 0, 0, axis_index_groups=groups, tiled=True)
    x = lax.all_to_all(x, "ew", 1, 1, tiled=True)
    return x.reshape(shape)


def attention_weights(w_qkv, w_out):
    channels = w_out.shape[0]
    return w_qkv[:, : 2 * channels], w_qkv[:, 2 * channels :].T, w_out


def on_device(
    tokens,
    conv_gain,
    w_expand,
    dw_kernel,
    w_project,
    block_gain,
    block_qkv,
    block_out,
    grid_gain,
    grid_qkv,
    grid_out,
):
    rows, cols, channels = tokens.shape
    shares = WINDOW // lax.axis_size("ew")
    group = WINDOW * lax.axis_size("ew")
    across = cols // shares // WINDOW
    places = group // rows
    chunks = across // places

    def slot_of(window):
        share, at = divmod(window, across)
        chunk, place = divmod(at, places)
        return (chunk * places + place) * shares + share

    edge, side = halo(tokens)
    after_conv = conv_block(tokens, edge, side, conv_gain, w_expand, dw_kernel, w_project, slot_of)
    block_weights = attention_weights(block_qkv, block_out)
    grid_weights = attention_weights(grid_qkv, grid_out)
    sent = []
    for chunk in range(chunks):
        x = window_attention(after_conv, chunk, chunks, shares, block_gain, block_weights)
        sent.append(exchange(x.reshape(group, shares * WINDOW, channels)))
    returned = []
    for x in sent:
        y = grid_attention(x.reshape(-1, channels), grid_gain, grid_weights)
        returned.append(exchange(y.reshape(group, shares * WINDOW, channels)))
    pieces = [y.reshape(rows, places, shares, WINDOW, channels) for y in returned]
    joined = jnp.stack(pieces)
    return jnp.transpose(joined, (1, 3, 0, 2, 4, 5)).reshape(rows, cols, channels)


def solution(mesh):
    in_specs = (P("ns", "ew", None), P(), P(), P(), P(), P(), P(), P(), P(), P(), P())
    out_specs = P("ns", "ew", None)
    return jax.shard_map(
        on_device, mesh=mesh, in_specs=in_specs, out_specs=out_specs, check_vma=False
    )
```

time: 315 us -> 125 us (0.40); the launches traced: 310 us -> 124 us
  local copies, waits for them, and re-layouts: 114 us -> 8.18 us
  blocking collectives: 95.5 us -> 18.5 us
  matrix products: 63.2 us -> 0 us
  Pallas kernels: 0 us -> 55.7 us
  other arithmetic: 22 us -> 1.47 us
  starting transfers between devices: 11.2 us -> 27.6 us
  waiting for transfers between devices: 3.71 us -> 12.4 us
    all_to_all x4 -> x1, blocking collectives: 95.5 us -> 18.5 us  [exchange(): return lax.all_to_all(x, ('ns', 'ew'), 0, 0, tiled=True)]
    reshape x7 -> x1, local copies, waits for them, and re-layouts: 66.7 us -> 0.69 us  [conv_block(): dw_kernel.reshape(9, width)]
    pallas_call x0 -> x5, Pallas kernels: none -> 55.7 us  [the longest x4 38.7 us: attention_call(): pl.pallas_call(kernel, grid=(grid,), out_shape=jax.ShapeDtypeStruct(out_s...]
    dot_general x9 -> x0, matrix products: 53.7 us -> none  [the longest x2 14.5 us: attend(): jnp.einsum('nhqk,nhkd->nhqd', weights, value_rows, preferred_element_type...]
    all_to_all x0 -> x3, starting transfers between devices: none -> 17.9 us  [exchange(): return lax.all_to_all(x, ('ns', 'ew'), 0, 0, tiled=True)]
    transpose x2 -> x0, local copies, waits for them, and re-layouts: 15.9 us -> none  [attend(): blended = jnp.transpose(blended, (3, 0, 4, 1, 2, 5)).reshape(-1, channels)]
    convert_element_type x5 -> x0, local copies, waits for them, and re-layouts: 14.8 us -> none  [the longest x2 10.3 us: attend(): blended = jnp.einsum('nhqk,nhkd->nhqd', weights, value_rows, preferred_el...]
    sub x1 -> x0, other arithmetic: 11.6 us -> none  [attend(): weights = jax.nn.softmax(scores, axis=-1).astype(jnp.bfloat16)]
  transfers between devices with their start and end apart: 4 -> 7, of which waited for: 1 -> 5; matrix products, arithmetic and copies ran while one was open for 2% -> 5% of each run, Pallas kernels for 0% -> 24%
where the time goes in v1:
time: 125 us; the launch traced here: 124 us
  Pallas kernels  55.7 us (45%)
  starting transfers between devices  27.6 us (22%)
  blocking collectives  18.5 us (15%)
  waiting for transfers between devices  12.4 us (10%)
  local copies, waits for them, and re-layouts  8.18 us (7%)
  other arithmetic  1.47 us (1%)
    pallas_call x4, Pallas kernels, attention_call(): pl.pallas_call(kernel, grid=(grid,), out_shape=jax.ShapeDtypeStruct(out_s...  38.7 us
    all_to_all x1, blocking collectives, exchange(): return lax.all_to_all(x, ('ns', 'ew'), 0, 0, tiled=True)  18.5 us
    all_to_all x3, starting transfers between devices, exchange(): return lax.all_to_all(x, ('ns', 'ew'), 0, 0, tiled=True)  17.9 us
    pallas_call x1, Pallas kernels, conv_block(): pl.pallas_call(functools.partial(conv_kernel, slot_of), grid=(width // fe...  17 us
    all_to_all x3, waiting for transfers between devices, exchange(): return lax.all_to_all(x, ('ns', 'ew'), 0, 0, tiled=True)  11.5 us
    ppermute x1, starting transfers between devices, halo(): lax.ppermute(jnp.concatenate([north[None, cols - 1], tokens[:, cols - 1],...  4.73 us
  transfers between devices with their start and end apart: 7, of which 5 were waited for; matrix products, arithmetic and copies ran while one was open for 5% of the time, Pallas kernels for 24%

profile of v1, /device:TPU:0, one launch (start us, length us, event | category | flops | bytes accessed | tf_op | source)
XLA Modules:
  0.0 124.0 jit_solution(14373722277728057448)
XLA Ops:
  0.0 0.0 copy-start
  0.0 0.0 slice-start
  0.0 0.0 copy-start.4
  0.0 1.1 slice_bitcast_fusion.1
  1.1 2.4 %collective-permute-start = (bf16[128,512]{1,0:T(8,128)(2,1)S(1)}, bf16[128,512]{1,0:T(8,128)(2,1)S(1)}, u32[]{:S(2)}, u32[]{:S(2)}) collective-permute-start(bf16[128,512]{1,0:T(8,128)(2,1)S(1)} %get-tuple-element.7), channel_id=1, source_target_pairs={{0,4},{4,8},{8,12},{12,16},{16,20},{20,24},{24,28},{1,5},{5,9},{9,... | collective-permute-start | bytes 393224 | tf_op jit(solution)/shard_map/ppermute | solution.py:315
  3.5 1.3 %collective-permute-start.1 = (bf16[128,512]{1,0:T(8,128)(2,1)S(1)}, bf16[128,512]{1,0:T(8,128)(2,1)S(1)}, u32[]{:S(2)}, u32[]{:S(2)}) collective-permute-start(bf16[128,512]{1,0:T(8,128)(2,1)S(1)} %get-tuple-element.8), channel_id=1, source_target_pairs={{4,0},{8,4},{12,8},{16,12},{20,16},{24,20},{28,24},{5,1},{9,5},{13... | collective-permute-start | bytes 393224 | tf_op jit(solution)/shard_map/ppermute | solution.py:316
  4.8 0.0 copy-done
  4.8 1.2 slice.44.wqk_ref
  6.0 0.9 fusion.3
  6.9 0.0 copy-done.4
  6.9 0.7 reshape.36.dw_ref
  7.6 0.0 slice-done
  7.6 1.0 copy.21
  8.6 0.0 collective-permute-done
  8.7 0.2 collective-permute-done.1
  8.9 1.3 %collective-permute-start.3 = (bf16[10,512]{1,0:T(8,128)(2,1)S(1)}, bf16[10,512]{1,0:T(8,128)(2,1)S(1)}, u32[]{:S(2)}, u32[]{:S(2)}) collective-permute-start(bf16[10,512]{1,0:T(8,128)(2,1)S(1)} %pad_maximum_fusion.3), channel_id=1, source_target_pairs={{1,0},{2,1},{3,2},{5,4},{6,5},{7,6},{9,8},{10,9},{11,10},{13,12},{... | collective-permute-start | bytes 30728 | tf_op jit(solution)/shard_map/ppermute | solution.py:320
  10.2 4.7 %collective-permute-start.2 = (bf16[10,512]{1,0:T(8,128)(2,1)S(1)}, bf16[10,512]{1,0:T(8,128)(2,1)S(1)}, u32[]{:S(2)}, u32[]{:S(2)}) collective-permute-start(bf16[10,512]{1,0:T(8,128)(2,1)S(1)} %pad_maximum_fusion.2), channel_id=1, source_target_pairs={{0,1},{1,2},{2,3},{4,5},{5,6},{6,7},{8,9},{9,10},{10,11},{12,13},{... | collective-permute-start | bytes 30728 | tf_op jit(solution)/shard_map/ppermute | solution.py:317
  15.0 0.7 pad_maximum_fusion.1.edge_ref
  15.7 0.0 collective-permute-done.3
  15.7 0.7 collective-permute-done.2
  16.4 0.6 fusion.2.side_ref
  17.0 17.0 %conv_block.1.x_ref = bf16[16,64,512]{2,1,0:T(8,128)(2,1)} custom-call(bf16[8,128,512]{2,1,0:T(8,128)(2,1)} %x_ref.1, bf16[2,128,512]{2,1,0:T(8,128)(2,1)} %pad_maximum_fusion.1.edge_ref, bf16[32,512]{1,0:T(8,128)(2,1)} %fusion.2.side_ref, f32[1,512]{1,0:T(1,128)} %bitcast.44, bf16[512,2048]{1,0:T(8,128)(2,1)} %w1_ref.1, f32[9,2048]{1,0:T(8,128)} %reshape.36.dw_ref, ...), custom_call_target="tpu_custom_call" | custom-call | flops 4294967296 | bytes 6291456 | tf_op jit(solution)/shard_map/conv_block/pallas_call | solution.py:125
  34.0 9.5 %window_attention.3 = bf16[8,4,2,8,512]{4,3,2,1,0:T(8,128)(2,1)} custom-call(bf16[16,64,512]{2,1,0:T(8,128)(2,1)} %conv_block.1.x_ref, f32[1,512]{1,0:T(1,128)} %bitcast.45, bf16[512,1024]{1,0:T(8,128)(2,1)} %slice.44.wqk_ref, bf16[512,512]{1,0:T(8,128)(2,1)} %bitcast.30, bf16[512,512]{1,0:T(8,128)(2,1)} %wout_ref.6), custom_call_target="tpu_custom_call" | custom-call | flops 4294967296 | bytes 4194304 | tf_op jit(solution)/shard_map/window_attention/pallas_call | solution.py:229
  43.5 9.5 %all-to-all-start.2 = ((bf16[32,16,512]{2,1,0:T(8,128)(2,1)}), bf16[32,16,512]{2,1,0:T(8,128)(2,1)S(1)}, u32[]{:S(2)}, u32[]{:S(2)}) async-start(bf16[32,16,512]{2,1,0:T(8,128)(2,1)} %bitcast.38), calls=%async_computation.2 | async-start | bytes 1048576 | tf_op jit(solution)/shard_map/all_to_all | solution.py:328
  53.0 9.5 %window_attention.2 = bf16[8,4,2,8,512]{4,3,2,1,0:T(8,128)(2,1)} custom-call(bf16[16,64,512]{2,1,0:T(8,128)(2,1)} %conv_block.1.x_ref, f32[1,512]{1,0:T(1,128)} %bitcast.46, bf16[512,1024]{1,0:T(8,128)(2,1)} %slice.44.wqk_ref, bf16[512,512]{1,0:T(8,128)(2,1)} %bitcast.31, bf16[512,512]{1,0:T(8,128)(2,1)} %wout_ref.6), custom_call_target="tpu_custom_call" | custom-call | flops 4294967296 | bytes 4194304 | tf_op jit(solution)/shard_map/window_attention/pallas_call | solution.py:229
  62.5 0.0 copy-start.1
  62.5 4.9 %all-to-all-done.2 = bf16[32,16,512]{2,1,0:T(8,128)(2,1)S(1)} async-done(((bf16[32,16,512]{2,1,0:T(8,128)(2,1)}), bf16[32,16,512]{2,1,0:T(8,128)(2,1)S(1)}, u32[]{:S(2)}, u32[]{:S(2)}) %all-to-all-start.2) | async-done | bytes 524320 | tf_op jit(solution)/shard_map/all_to_all | solution.py:328
  67.4 0.0 copy-start.2
  67.4 0.0 slice-start.1
  67.4 4.3 %all-to-all-start = ((bf16[32,16,512]{2,1,0:T(8,128)(2,1)}), bf16[32,16,512]{2,1,0:T(8,128)(2,1)S(1)}, u32[]{:S(2)}, u32[]{:S(2)}) async-start(bf16[32,16,512]{2,1,0:T(8,128)(2,1)} %bitcast.34), calls=%async_computation | async-start | bytes 1048576 | tf_op jit(solution)/shard_map/all_to_all | solution.py:328
  71.7 0.0 copy-done.1
  71.7 1.1 slice.46.wqk_ref
  72.8 0.0 copy-done.2
  72.8 0.0 slice-done.1
  72.8 1.0 copy.22
  73.8 9.9 %grid_attention.3 = bf16[512,512]{1,0:T(8,128)(2,1)} custom-call(bf16[512,512]{1,0:T(8,128)(2,1)} %bitcast.32, f32[1,512]{1,0:T(1,128)} %bitcast.47, bf16[512,1024]{1,0:T(8,128)(2,1)} %slice.46.wqk_ref, bf16[512,512]{1,0:T(8,128)(2,1)} %bitcast.35, bf16[512,512]{1,0:T(8,128)(2,1)} %wout_ref.7), custom_call_target="tpu_custom_call" | custom-call | flops 2147483648 | bytes 3145728 | tf_op jit(solution)/shard_map/grid_attention/pallas_call | solution.py:229
  83.7 2.1 %all-to-all-done = bf16[32,16,512]{2,1,0:T(8,128)(2,1)S(1)} async-done(((bf16[32,16,512]{2,1,0:T(8,128)(2,1)}), bf16[32,16,512]{2,1,0:T(8,128)(2,1)S(1)}, u32[]{:S(2)}, u32[]{:S(2)}) %all-to-all-start) | async-done | bytes 524320 | tf_op jit(solution)/shard_map/all_to_all | solution.py:328
  85.9 0.0 copy-start.3
  85.9 4.1 %all-to-all-start.3 = ((bf16[32,16,512]{2,1,0:T(8,128)(2,1)}), bf16[32,16,512]{2,1,0:T(8,128)(2,1)S(1)}, u32[]{:S(2)}, u32[]{:S(2)}) async-start(bf16[32,16,512]{2,1,0:T(8,128)(2,1)} %bitcast.37), calls=%async_computation.3 | async-start | bytes 1048576 | tf_op jit(solution)/shard_map/all_to_all | solution.py:328
  89.9 0.0 copy-done.3
  90.0 9.9 %grid_attention.2 = bf16[512,512]{1,0:T(8,128)(2,1)} custom-call(bf16[512,512]{1,0:T(8,128)(2,1)} %bitcast.33, f32[1,512]{1,0:T(1,128)} %bitcast.48, bf16[512,1024]{1,0:T(8,128)(2,1)} %slice.46.wqk_ref, bf16[512,512]{1,0:T(8,128)(2,1)} %bitcast.36, bf16[512,512]{1,0:T(8,128)(2,1)} %wout_ref.7), custom_call_target="tpu_custom_call" | custom-call | flops 2147483648 | bytes 3145728 | tf_op jit(solution)/shard_map/grid_attention/pallas_call | solution.py:229
  99.9 4.5 %all-to-all-done.3 = bf16[32,16,512]{2,1,0:T(8,128)(2,1)S(1)} async-done(((bf16[32,16,512]{2,1,0:T(8,128)(2,1)}), bf16[32,16,512]{2,1,0:T(8,128)(2,1)S(1)}, u32[]{:S(2)}, u32[]{:S(2)}) %all-to-all-start.3) | async-done | bytes 524320 | tf_op jit(solution)/shard_map/all_to_all | solution.py:328
  104.3 18.5 %all_to_all.20 = bf16[32,16,512]{2,1,0:T(8,128)(2,1)S(1)} all-to-all(bf16[32,16,512]{2,1,0:T(8,128)(2,1)} %bitcast.39), channel_id=1, replica_groups=mesh['ns'=8,'ew'=4] {'ns','ew'}, dimensions={0} | all-to-all | bytes 1048576 | tf_op jit(solution)/shard_map/all_to_all | solution.py:328
  122.8 0.1 pad_maximum_fusion
  122.9 1.1 copy.18
  (6 shorter events, 0.1 us)
Async XLA Ops:
  0.0 4.8 %copy-start = (bf16[512,1536]{1,0:T(8,128)(2,1)S(1)}, bf16[512,1536]{1,0:T(8,128)(2,1)}, u32[]{:S(2)}) copy-start(bf16[512,1536]{1,0:T(8,128)(2,1)} %param.17) | copy-start | bytes 4718596
  0.0 7.6 %slice-start = ((bf16[512,1536]{1,0:T(8,128)(2,1)}), bf16[512,512]{1,0:T(8,128)(2,1)S(1)}, s32[]{:S(2)}) async-start(bf16[512,1536]{1,0:T(8,128)(2,1)} %param.17), calls=%async_computation.4 | async-start | bytes 1048576 | tf_op jit(solution)/shard_map/slice | solution.py:340
  0.0 6.9 %copy-start.4 = (f32[3,3,2048]{2,1,0:T(4,128)S(1)}, f32[3,3,2048]{2,1,0:T(4,128)}, u32[]{:S(2)}) copy-start(f32[3,3,2048]{2,1,0:T(4,128)} %param.14) | copy-start | bytes 221188
  1.1 7.5 %collective-permute-start = (bf16[128,512]{1,0:T(8,128)(2,1)S(1)}, bf16[128,512]{1,0:T(8,128)(2,1)S(1)}, u32[]{:S(2)}, u32[]{:S(2)}) collective-permute-start(bf16[128,512]{1,0:T(8,128)(2,1)S(1)} %get-tuple-element.7), channel_id=1, source_target_pairs={{0,4},{4,8},{8,12},{12,16},{16,20},{20,24},{24,28},{1,5},{5,9},{9,... | collective-permute-start | bytes 393224 | tf_op jit(solution)/shard_map/ppermute | solution.py:315
  3.5 5.3 %collective-permute-start.1 = (bf16[128,512]{1,0:T(8,128)(2,1)S(1)}, bf16[128,512]{1,0:T(8,128)(2,1)S(1)}, u32[]{:S(2)}, u32[]{:S(2)}) collective-permute-start(bf16[128,512]{1,0:T(8,128)(2,1)S(1)} %get-tuple-element.8), channel_id=1, source_target_pairs={{4,0},{8,4},{12,8},{16,12},{20,16},{24,20},{28,24},{5,1},{9,5},{13... | collective-permute-start | bytes 393224 | tf_op jit(solution)/shard_map/ppermute | solution.py:316
  8.9 6.8 %collective-permute-start.3 = (bf16[10,512]{1,0:T(8,128)(2,1)S(1)}, bf16[10,512]{1,0:T(8,128)(2,1)S(1)}, u32[]{:S(2)}, u32[]{:S(2)}) collective-permute-start(bf16[10,512]{1,0:T(8,128)(2,1)S(1)} %pad_maximum_fusion.3), channel_id=1, source_target_pairs={{1,0},{2,1},{3,2},{5,4},{6,5},{7,6},{9,8},{10,9},{11,10},{13,12},{... | collective-permute-start | bytes 30728 | tf_op jit(solution)/shard_map/ppermute | solution.py:320
  10.2 6.2 %collective-permute-start.2 = (bf16[10,512]{1,0:T(8,128)(2,1)S(1)}, bf16[10,512]{1,0:T(8,128)(2,1)S(1)}, u32[]{:S(2)}, u32[]{:S(2)}) collective-permute-start(bf16[10,512]{1,0:T(8,128)(2,1)S(1)} %pad_maximum_fusion.2), channel_id=1, source_target_pairs={{0,1},{1,2},{2,3},{4,5},{5,6},{6,7},{8,9},{9,10},{10,11},{12,13},{... | collective-permute-start | bytes 30728 | tf_op jit(solution)/shard_map/ppermute | solution.py:317
  43.5 23.9 %all-to-all-start.2 = ((bf16[32,16,512]{2,1,0:T(8,128)(2,1)}), bf16[32,16,512]{2,1,0:T(8,128)(2,1)S(1)}, u32[]{:S(2)}, u32[]{:S(2)}) async-start(bf16[32,16,512]{2,1,0:T(8,128)(2,1)} %bitcast.38), calls=%async_computation.2 | async-start | bytes 1048576 | tf_op jit(solution)/shard_map/all_to_all | solution.py:328
  62.5 9.2 %copy-start.1 = (bf16[512,1536]{1,0:T(8,128)(2,1)S(1)}, bf16[512,1536]{1,0:T(8,128)(2,1)}, u32[]{:S(2)}) copy-start(bf16[512,1536]{1,0:T(8,128)(2,1)} %param.20) | copy-start | bytes 4718596
  67.4 5.4 %copy-start.2 = (bf16[32,16,512]{2,1,0:T(8,128)(2,1)}, bf16[32,16,512]{2,1,0:T(8,128)(2,1)S(1)}, u32[]{:S(2)}) copy-start(bf16[32,16,512]{2,1,0:T(8,128)(2,1)S(1)} %all-to-all-done.2) | copy-start | bytes 1572868
  67.4 5.4 %slice-start.1 = ((bf16[512,1536]{1,0:T(8,128)(2,1)}), bf16[512,512]{1,0:T(8,128)(2,1)S(1)}, s32[]{:S(2)}) async-start(bf16[512,1536]{1,0:T(8,128)(2,1)} %param.20), calls=%async_computation.5 | async-start | bytes 1048576 | tf_op jit(solution)/shard_map/slice | solution.py:340
  67.4 18.5 %all-to-all-start = ((bf16[32,16,512]{2,1,0:T(8,128)(2,1)}), bf16[32,16,512]{2,1,0:T(8,128)(2,1)S(1)}, u32[]{:S(2)}, u32[]{:S(2)}) async-start(bf16[32,16,512]{2,1,0:T(8,128)(2,1)} %bitcast.34), calls=%async_computation | async-start | bytes 1048576 | tf_op jit(solution)/shard_map/all_to_all | solution.py:328
  85.9 4.1 %copy-start.3 = (bf16[32,16,512]{2,1,0:T(8,128)(2,1)}, bf16[32,16,512]{2,1,0:T(8,128)(2,1)S(1)}, u32[]{:S(2)}) copy-start(bf16[32,16,512]{2,1,0:T(8,128)(2,1)S(1)} %all-to-all-done) | copy-start | bytes 1572868
  85.9 18.5 %all-to-all-start.3 = ((bf16[32,16,512]{2,1,0:T(8,128)(2,1)}), bf16[32,16,512]{2,1,0:T(8,128)(2,1)S(1)}, u32[]{:S(2)}, u32[]{:S(2)}) async-start(bf16[32,16,512]{2,1,0:T(8,128)(2,1)} %bitcast.37), calls=%async_computation.3 | async-start | bytes 1048576 | tf_op jit(solution)/shard_map/all_to_all | solution.py:328

commit v2 on v1

v2 whole, which is shorter than its diff:
```python
import functools
import math

import jax
import jax.numpy as jnp
from jax import lax
from jax.experimental import pallas as pl
from jax.experimental.pallas import tpu as pltpu
from jax.sharding import PartitionSpec as P

HEADS = 16
WINDOW = 8
FEATURES = 1024
LANES = 128
GROUP = 8
SENDS = 1
MIB = 1024 * 1024

NT = (((1,), (1,)), ((), ()))


def normalize(floats, scale_gain):
    center = floats - jnp.mean(floats, axis=-1, keepdims=True)
    spread = jnp.mean(center * center, axis=-1, keepdims=True)
    return center * lax.rsqrt(spread + 1e-05) * scale_gain


def gelu(v):
    inner = v * (math.sqrt(2 / math.pi) + (math.sqrt(2 / math.pi) * 0.044715) * (v * v))
    half = 0.5 * v
    return half + half * jnp.tanh(inner)


def tiles(value):
    return [value[:, t : t + LANES] for t in range(0, value.shape[1], LANES)]


def strided(ref, start, size, stride):
    return jnp.concatenate([ref[t, pl.ds(start, size, stride=stride), :] for t in range(ref.shape[0])], axis=1)


def conv_kernel(
    slot_of, x_ref, ns0_ref, ns1_ref, ew0_ref, ew1_ref, gain_ref, w1_ref, dw_ref, w2_ref, out_ref,
    n_ref, tmp_ref, e_ref, acc_ref
):
    step = pl.program_id(0)
    rows, cols, _ = x_ref.shape
    strips = cols // WINDOW
    features = w1_ref.shape[1]
    side_rows = ew0_ref.shape[0]
    side_count = side_rows + -side_rows % 16
    gain = gain_ref[...]

    @pl.when(step == 0)
    def _():
        def place(slot, block):
            for t, part in enumerate(tiles(normalize(block, gain))):
                tmp_ref[t] = part
            for b in range(WINDOW):
                start = slot * cols + b * strips
                n_ref[start : start + strips, :] = strided(tmp_ref, b, strips, WINDOW).astype(jnp.bfloat16)

        def sorted_pair(first_ref, second_ref, axis):
            first, second = first_ref[...].astype(jnp.float32), second_ref[...].astype(jnp.float32)
            even = lax.rem(lax.axis_index(axis), 2) == 0
            return jnp.where(even, second, first), jnp.where(even, first, second)

        for i in range(rows):
            place(i + 1, x_ref[i].astype(jnp.float32))
        north, south = sorted_pair(ns0_ref, ns1_ref, "ns")
        place(0, north)
        place(rows + 1, south)
        pad = jnp.zeros((side_count - side_rows, x_ref.shape[2]), jnp.float32)
        for k, block in enumerate(sorted_pair(ew0_ref, ew1_ref, "ew")):
            start = (rows + 2) * cols + k * side_count
            n_ref[start : start + side_count, :] = normalize(
                jnp.concatenate([block, pad], axis=0), gain
            ).astype(jnp.bfloat16)
        acc_ref[...] = jnp.zeros_like(acc_ref)

    w1 = w1_ref[...]
    w2 = w2_ref[...]
    taps = [[dw_ref[3 * a + b : 3 * a + b + 1, :].astype(jnp.bfloat16) for b in range(3)] for a in range(3)]
    sides = gelu(
        jnp.dot(n_ref[pl.ds((rows + 2) * cols, 2 * side_count), :], w1, preferred_element_type=jnp.float32)
    )
    place_in_strip = lax.broadcasted_iota(jnp.int32, (strips, features), 0)

    def expand(i):
        hidden = gelu(
            jnp.dot(n_ref[pl.ds(i * cols, cols), :], w1, preferred_element_type=jnp.float32).astype(jnp.bfloat16)
        )
        e_ref[i, 1 : WINDOW + 1] = hidden.reshape(WINDOW, strips, features)
        last = pltpu.roll(hidden[(WINDOW - 1) * strips :].astype(jnp.float32), 1, axis=0)
        first = pltpu.roll(hidden[:strips].astype(jnp.float32), strips - 1, axis=0)
        low = jnp.where(place_in_strip == 0, sides[i : i + 1], last)
        high = jnp.where(place_in_strip == strips - 1, sides[side_count + i : side_count + i + 1], first)
        e_ref[i, 0] = low.astype(jnp.bfloat16)
        e_ref[i, WINDOW + 1] = high.astype(jnp.bfloat16)

    def contract(i):
        pieces = []
        for b in range(WINDOW):
            parts = []
            for da in range(3):
                t = [e_ref[i + da, b + db] * taps[da][db] for db in range(3)]
                parts.append(t[0] + t[1] + t[2])
            pieces.append(gelu(parts[0] + parts[1] + parts[2]))
        active = jnp.concatenate(pieces, axis=0)
        for t, part in enumerate(tiles(jnp.dot(active, w2, preferred_element_type=jnp.float32))):
            acc_ref[t, i * cols : (i + 1) * cols, :] += part

    for i in range(rows + 2):
        expand(i)
    for i in range(rows):
        contract(i)

    @pl.when(step == pl.num_programs(0) - 1)
    def _():
        for pair in range(strips // 2):
            tokens = x_ref[:, pair * 2 * WINDOW : (pair + 1) * 2 * WINDOW, :].astype(jnp.float32)
            for odd in range(2):
                window = 2 * pair + odd
                own = tokens[:, odd * WINDOW : (odd + 1) * WINDOW, :].reshape(rows * WINDOW, -1)
                summed = own + strided(acc_ref, window, rows * WINDOW, strips)
                out_ref[slot_of(window)] = summed.astype(jnp.bfloat16)


def conv_block(tokens, swaps, gain, w_expand, dw_kernel, w_project, slot_of):
    rows, cols, channels = tokens.shape
    width = w_expand.shape[1]
    features = min(FEATURES, width)
    strips = cols // WINDOW
    side_count = swaps[2].shape[0] + -swaps[2].shape[0] % 16
    whole = lambda *shape: pl.BlockSpec(shape, lambda f: (0,) * len(shape))
    return pl.pallas_call(
        functools.partial(conv_kernel, slot_of),
        grid=(width // features,),
        out_shape=jax.ShapeDtypeStruct((strips, rows * WINDOW, channels), jnp.bfloat16),
        in_specs=[
            whole(*tokens.shape),
            *[whole(*swap.shape) for swap in swaps],
            whole(1, channels),
            pl.BlockSpec((channels, features), lambda f: (0, f)),
            pl.BlockSpec((9, features), lambda f: (0, f)),
            pl.BlockSpec((features, channels), lambda f: (f, 0)),
        ],
        out_specs=whole(strips, rows * WINDOW, channels),
        scratch_shapes=[
            pltpu.VMEM(((rows + 2) * cols + 2 * side_count, channels), jnp.bfloat16),
            pltpu.VMEM((channels // LANES, cols, LANES), jnp.float32),
            pltpu.VMEM((rows + 2, WINDOW + 2, strips, features), jnp.bfloat16),
            pltpu.VMEM((channels // LANES, rows * cols, LANES), jnp.float32),
        ],
        compiler_params=pltpu.CompilerParams(
            dimension_semantics=("arbitrary",), vmem_limit_bytes=40 * MIB
        ),
        cost_estimate=pl.CostEstimate(
            flops=4 * rows * cols * channels * width,
            bytes_accessed=4 * channels * width + 4 * rows * cols * channels,
            transcendentals=2 * rows * cols * width,
        ),
        name="conv_block",
    )(
        tokens,
        *swaps,
        gain.reshape(1, channels),
        w_expand,
        dw_kernel.reshape(9, width),
        w_project,
    )


def attend_windows(x, gain, wqkv_ref, wout_ref):
    tokens, channels = x.shape
    head_dim = channels // HEADS
    group = LANES // head_dim
    size = WINDOW * WINDOW
    two = 2 * head_dim
    pairs, groups = tokens // (2 * size), channels // LANES
    units = [(p, g) for p in range(pairs) for g in range(groups)]
    scale = math.log2(math.e) / math.sqrt(head_dim)
    normed = normalize(x, gain).astype(jnp.bfloat16)

    def project(first):
        return jnp.dot(normed, wqkv_ref[:, first : first + channels], preferred_element_type=jnp.float32)

    queries = (project(0) * scale).astype(jnp.bfloat16)
    keys = project(channels).astype(jnp.bfloat16)
    values = lax.dot_general(
        wqkv_ref[:, 2 * channels :].T, normed, NT, preferred_element_type=jnp.float32
    ).astype(jnp.bfloat16)
    lane = lax.broadcasted_iota(jnp.int32, (1, LANES), 1)
    head_lanes = [(lane // head_dim == h).astype(jnp.float32).astype(jnp.bfloat16) for h in range(group)]
    halves = [(lane // size == h).astype(jnp.float32).astype(jnp.bfloat16) for h in range(2)]
    pick = (
        (
            lax.broadcasted_iota(jnp.int32, (size, 2 * size), 0)
            == lax.broadcasted_iota(jnp.int32, (size, 2 * size), 1) % size
        )
        .astype(jnp.float32)
        .astype(jnp.bfloat16)
    )
    scores = {}
    for p, g in units:
        for odd in range(2):
            at = (2 * p + odd) * size
            q = queries[at : at + size, g * LANES : (g + 1) * LANES]
            k = keys[at : at + size, g * LANES : (g + 1) * LANES]
            q_heads = jnp.concatenate([q * m for m in head_lanes], axis=0)
            scores[p, g, odd] = lax.dot_general(k, q_heads, NT, preferred_element_type=jnp.float32)
    weights = {}
    for unit, s in scores.items():
        raised = jnp.exp2(s - jnp.max(s, axis=0, keepdims=True))
        weights[unit] = (raised * (1.0 / jnp.sum(raised, axis=0, keepdims=True))).astype(jnp.bfloat16)
    mixed = {}
    for p, g in units:
        both = jnp.concatenate([weights[p, g, 0], weights[p, g, 1]], axis=0)
        for t in range(group // 2):
            at = g * LANES + t * two
            v = values[at : at + two, p * 2 * size : (p + 1) * 2 * size]
            v_halves = jnp.concatenate([v * m for m in halves], axis=0)
            mixed[p, g, t] = jnp.dot(
                v_halves, both[:, t * 2 * size : (t + 1) * 2 * size], preferred_element_type=jnp.float32
            ).astype(jnp.bfloat16)
    parts = {}
    for p, g in units:
        own = [
            mixed[p, g, t][odd * two + h * head_dim : odd * two + (h + 1) * head_dim] * halves[h]
            for odd in range(2)
            for t in range(group // 2)
            for h in range(2)
        ]
        parts[p, g] = lax.dot_general(
            pick, jnp.concatenate(own, axis=0), NT, preferred_element_type=jnp.float32
        ).astype(jnp.bfloat16)
    blended = [
        jnp.concatenate([parts[p, g][:, odd * LANES : (odd + 1) * LANES] for g in range(groups)], axis=1)
        for p in range(pairs)
        for odd in range(2)
    ]
    return x + jnp.dot(jnp.concatenate(blended, axis=0), wout_ref[...], preferred_element_type=jnp.float32)


def window_kernel(x_ref, gain_ref, wqkv_ref, wout_ref, out_ref):
    count, size, channels = x_ref.shape
    _, places, shares, parts, side, _ = out_ref.shape
    x = x_ref[...].astype(jnp.float32).reshape(count * size, channels)
    result = attend_windows(x, gain_ref[...], wqkv_ref, wout_ref).astype(jnp.bfloat16)
    result = result.reshape(places, shares, parts, size // side, side, channels)
    for j in range(places):
        for share in range(shares):
            for part in range(parts):
                out_ref[:, j, share, part] = result[j, share, part]


def attention_call(kernel, name, grid, x, x_spec, gain, weights, out_shape, out_spec, scratch):
    channels = x.shape[-1]
    tokens = x.size // channels
    whole = lambda array: pl.BlockSpec(array.shape, lambda step: (0,) * array.ndim)
    gain = gain.reshape(1, channels)
    return pl.pallas_call(
        kernel,
        grid=(grid,),
        out_shape=jax.ShapeDtypeStruct(out_shape, jnp.bfloat16),
        in_specs=[x_spec, whole(gain)] + [whole(w) for w in weights],
        out_specs=out_spec,
        scratch_shapes=scratch,
        compiler_params=pltpu.CompilerParams(
            dimension_semantics=("arbitrary",), vmem_limit_bytes=24 * MIB
        ),
        cost_estimate=pl.CostEstimate(
            flops=16 * tokens * channels * channels,
            bytes_accessed=8 * channels * channels + 4 * tokens * channels,
            transcendentals=HEADS * tokens * WINDOW * WINDOW,
        ),
        name=name,
    )(x, gain, *weights)


def window_attention(x, send, sends, places, shares, gain, weights):
    windows, size, channels = x.shape
    per_send = windows // sends
    parts = per_send // (places * shares)
    block_places = max(1, min(places, GROUP // (shares * parts)))
    block = block_places * shares * parts
    steps = per_send // block
    return attention_call(
        window_kernel,
        "window_attention",
        steps,
        x,
        pl.BlockSpec((block, size, channels), lambda step: (send * steps + step, 0, 0)),
        gain,
        weights,
        (size // WINDOW, places, shares, parts, WINDOW, channels),
        pl.BlockSpec(
            (size // WINDOW, block_places, shares, parts, WINDOW, channels), lambda step: (0, step, 0, 0, 0, 0)
        ),
        [],
    )


def grid_kernel(x_ref, gain_ref, wqkv_ref, wout_ref, out_ref, floats_ref):
    step = pl.program_id(0)
    tokens, channels = x_ref.shape
    size = WINDOW * WINDOW
    windows = tokens // size
    block = windows // pl.num_programs(0)

    @pl.when(step == 0)
    def _():
        for t, part in enumerate(tiles(x_ref[...])):
            floats_ref[t] = part.astype(jnp.float32)

    first = step * block
    x = jnp.concatenate([strided(floats_ref, first + w, size, windows) for w in range(block)], axis=0)
    result = attend_windows(x, gain_ref[...], wqkv_ref, wout_ref)
    for t, part in enumerate(tiles(result)):
        for w in range(block):
            floats_ref[t, pl.ds(first + w, size, stride=windows), :] = part[w * size : (w + 1) * size]

    @pl.when(step == pl.num_programs(0) - 1)
    def _():
        for t in range(floats_ref.shape[0]):
            out_ref[:, t * LANES : (t + 1) * LANES] = floats_ref[t].astype(jnp.bfloat16)


def grid_attention(x, gain, weights):
    tokens, channels = x.shape
    windows = tokens // (WINDOW * WINDOW)
    spec = pl.BlockSpec((tokens, channels), lambda step: (0, 0))
    return attention_call(
        grid_kernel,
        "grid_attention",
        windows // min(GROUP, windows),
        x,
        spec,
        gain,
        weights,
        (tokens, channels),
        spec,
        [pltpu.VMEM((channels // LANES, tokens, LANES), jnp.float32)],
    )


def swap(low_edge, high_edge, axis, first):
    pairs = [(a, a + 1) for a in range(first, lax.axis_size(axis) - 1, 2)]
    lower = lax.rem(lax.axis_index(axis), 2) == first
    return lax.ppermute(
        jnp.where(lower, high_edge, low_edge), axis, pairs + [(target, source) for source, target in pairs]
    )


def halo(tokens):
    rows, cols, _ = tokens.shape
    ns0, ns1 = [swap(tokens[0], tokens[rows - 1], "ns", first) for first in range(2)]
    even = lax.rem(lax.axis_index("ns"), 2) == 0

    def column(c):
        north, south = jnp.where(even, ns1[c], ns0[c]), jnp.where(even, ns0[c], ns1[c])
        return jnp.concatenate([north[None], tokens[:, c], south[None]])

    ew0, ew1 = [swap(column(0), column(cols - 1), "ew", first) for first in range(2)]
    return ns0, ns1, ew0, ew1


def exchange(x):
    bands, strips = lax.axis_size("ns"), lax.axis_size("ew")
    if bands == WINDOW:
        return lax.all_to_all(x, ("ns", "ew"), 0, 0, tiled=True)
    inner = bands // WINDOW
    groups = [[a * inner + p for a in range(WINDOW)] for p in range(inner)]
    shape = x.shape
    x = x.reshape(WINDOW, strips, *shape[1:])
    x = lax.all_to_all(x, "ns", 0, 0, axis_index_groups=groups, tiled=True)
    x = lax.all_to_all(x, "ew", 1, 1, tiled=True)
    return x.reshape(shape)


def on_device(
    tokens,
    conv_gain,
    w_expand,
    dw_kernel,
    w_project,
    block_gain,
    block_qkv,
    block_out,
    grid_gain,
    grid_qkv,
    grid_out,
):
    rows, cols, channels = tokens.shape
    shares = WINDOW // lax.axis_size("ew")
    group = WINDOW * lax.axis_size("ew")
    across = cols // shares // WINDOW
    places = group // rows
    parts = across // places
    sends = min(SENDS, parts)
    per_send = parts // sends

    def slot_of(window):
        share, at = divmod(window, across)
        part, place = divmod(at, places)
        send, part = divmod(part, per_send)
        return ((send * places + place) * shares + share) * per_send + part

    after_conv = conv_block(tokens, halo(tokens), conv_gain, w_expand, dw_kernel, w_project, slot_of)
    sent = []
    for send in range(sends):
        x = window_attention(after_conv, send, sends, places, shares, block_gain, (block_qkv, block_out))
        sent.append(exchange(x.reshape(group, -1, channels)))
    returned = []
    for x in sent:
        y = grid_attention(x.reshape(-1, channels), grid_gain, (grid_qkv, grid_out))
        returned.append(exchange(y.reshape(group, -1, channels)))
    pieces = [y.reshape(rows, places, shares, per_send, WINDOW, channels) for y in returned]
    return jnp.transpose(jnp.stack(pieces), (1, 3, 0, 4, 2, 5, 6)).reshape(rows, cols, channels)


def solution(mesh):
    in_specs = (P("ns", "ew", None), P(), P(), P(), P(), P(), P(), P(), P(), P(), P())
    out_specs = P("ns", "ew", None)
    return jax.shard_map(
        on_device, mesh=mesh, in_specs=in_specs, out_specs=out_specs, check_vma=False
    )
```

time: 125 us -> 108 us (0.86)
  blocking collectives: 18.5 us -> 61.5 us
  Pallas kernels: 55.7 us -> 24.7 us
  starting transfers between devices: 27.6 us -> 10.2 us
  waiting for transfers between devices: 12.4 us -> 0.84 us
    all_to_all x1 -> x2, blocking collectives: 18.5 us -> 61.5 us  [exchange(): return lax.all_to_all(x, ('ns', 'ew'), 0, 0, tiled=True)]
    pallas_call x4 -> x2, Pallas kernels: 38.7 us -> 14 us  [attention_call(): pl.pallas_call(kernel, grid=(grid,), out_shape=jax.ShapeDtypeStruct(out_s...]
    all_to_all x3 -> x0, starting transfers between devices: 17.9 us -> none  [exchange(): return lax.all_to_all(x, ('ns', 'ew'), 0, 0, tiled=True)]
    all_to_all x3 -> x0, waiting for transfers between devices: 11.5 us -> none  [exchange(): return lax.all_to_all(x, ('ns', 'ew'), 0, 0, tiled=True)]
    pallas_call x1, Pallas kernels: 17 us -> 10.7 us  [conv_block(): pl.pallas_call(functools.partial(conv_kernel, slot_of), grid=(width // fe...]
    unnamed x14 -> x20, local copies, waits for them, and re-layouts: 2.04 us -> 5.12 us
    slice x9 -> x1, local copies, waits for them, and re-layouts: 3.2 us -> 0.9 us  [column(): return jnp.concatenate([north[None], tokens[:, c], south[None]])]
  transfers between devices with their start and end apart: 7 -> 4, of which waited for: 5 -> 2; matrix products, arithmetic and copies ran while one was open for 5% -> 2% of each run, Pallas kernels for 24% -> 0%
where the time goes in v2:
time: 108 us; the launch traced here: 106 us
  blocking collectives  61.5 us (57%)
  Pallas kernels  24.7 us (23%)
  starting transfers between devices  10.2 us (9%)
  local copies, waits for them, and re-layouts  8.07 us (7%)
    all_to_all x2, blocking collectives, exchange(): return lax.all_to_all(x, ('ns', 'ew'), 0, 0, tiled=True)  61.5 us
    pallas_call x2, Pallas kernels, attention_call(): pl.pallas_call(kernel, grid=(grid,), out_shape=jax.ShapeDtypeStruct(out_s...  14 us
    pallas_call x1, Pallas kernels, conv_block(): pl.pallas_call(functools.partial(conv_kernel, slot_of), grid=(width // fe...  10.7 us
    ppermute x4, starting transfers between devices, swap(): lax.ppermute(jnp.where(lower, high_edge, low_edge), axis, pairs + [(targe...  10.2 us
    unnamed x20, local copies, waits for them, and re-layouts  5.12 us
  transfers between devices with their start and end apart: 4, of which 2 were waited for; matrix products, arithmetic and copies ran while one was open for 2% of the time, Pallas kernels for 0%

profile of v2, /device:TPU:0, one launch (start us, length us, event | category | flops | bytes accessed | tf_op | source)
XLA Modules:
  0.0 106.5 jit_solution(5210193288455805144)
XLA Ops:
  0.0 1.0 select_bitcast_fusion
  1.0 0.7 collective-permute-start.1
  1.7 4.4 %collective-permute-start = (bf16[128,512]{1,0:T(8,128)(2,1)S(1)}, bf16[128,512]{1,0:T(8,128)(2,1)S(1)}, u32[]{:S(2)}, u32[]{:S(2)}) collective-permute-start(bf16[128,512]{1,0:T(8,128)(2,1)S(1)} %get-tuple-element.8), channel_id=1, source_target_pairs={{0,4},{8,12},{16,20},{24,28},{4,0},{12,8},{20,16},{28,24},{1,5},{9... | collective-permute-start | bytes 393224 | tf_op jit(solution)/shard_map/ppermute | solution.py:350
  6.0 0.9 fusion
  6.9 0.0 collective-permute-done.1.ns1_ref
  7.0 0.1 collective-permute-done.ns0_ref
  7.1 0.7 collective-permute-start.3
  7.7 4.5 %collective-permute-start.2 = (bf16[10,512]{1,0:T(8,128)(2,1)S(1)}, bf16[10,512]{1,0:T(8,128)(2,1)S(1)}, u32[]{:S(2)}, u32[]{:S(2)}) collective-permute-start(bf16[10,512]{1,0:T(8,128)(2,1)S(1)} %get-tuple-element.14), channel_id=1, source_target_pairs={{0,1},{2,3},{1,0},{3,2},{4,5},{6,7},{5,4},{7,6},{8,9},{10,11},{9,8... | collective-permute-start | bytes 30728 | tf_op jit(solution)/shard_map/ppermute | solution.py:350
  12.2 0.9 reshape.29.dw_ref
  13.1 0.0 collective-permute-done.3.ew1_ref
  13.1 0.8 collective-permute-done.2.ew0_ref
  13.9 0.0 copy-start
  13.9 1.2 %copy-done = bf16[8,128,512]{2,1,0:T(8,128)(2,1)S(1)} copy-done((bf16[8,128,512]{2,1,0:T(8,128)(2,1)S(1)}, bf16[8,128,512]{2,1,0:T(8,128)(2,1)}, u32[]{:S(2)}) %copy-start) | copy-done | bytes 1048600
  15.1 0.0 copy-start.1
  15.1 1.6 %copy-done.1 = bf16[512,2048]{1,0:T(8,128)(2,1)S(1)} copy-done((bf16[512,2048]{1,0:T(8,128)(2,1)S(1)}, bf16[512,2048]{1,0:T(8,128)(2,1)}, u32[]{:S(2)}) %copy-start.1) | copy-done | bytes 2097176
  16.7 0.0 copy-start.2
  16.7 1.6 %copy-done.2 = bf16[2048,512]{1,0:T(8,128)(2,1)S(1)} copy-done((bf16[2048,512]{1,0:T(8,128)(2,1)S(1)}, bf16[2048,512]{1,0:T(8,128)(2,1)}, u32[]{:S(2)}) %copy-start.2) | copy-done | bytes 2097176
  18.3 0.0 copy-start.7
  18.3 0.7 copy-done.7
  19.0 0.0 copy-start.3
  19.0 0.0 copy-start.5
  19.0 0.0 copy-start.8
  19.0 10.7 %conv_block.1.x_ref = bf16[16,64,512]{2,1,0:T(8,128)(2,1)S(1)} custom-call(bf16[8,128,512]{2,1,0:T(8,128)(2,1)S(1)} %copy-done, bf16[128,512]{1,0:T(8,128)(2,1)S(1)} %collective-permute-done.ns0_ref, bf16[128,512]{1,0:T(8,128)(2,1)S(1)} %collective-permute-done.1.ns1_ref, bf16[10,512]{1,0:T(8,128)(2,1)S(1)} %collective-permute-done.2.ew0_ref, ...), custom_call_target="tpu_custom_call" | custom-call | flops 4294967296 | bytes 6291456 | tf_op jit(solution)/shard_map/conv_block/pallas_call | solution.py:136
  29.7 0.0 copy-done.3
  29.7 0.0 copy-done.5
  29.8 0.0 copy-done.8
  29.8 6.1 %window_attention.1 = bf16[8,4,2,2,8,512]{5,4,3,2,1,0:T(8,128)(2,1)S(1)} custom-call(bf16[16,64,512]{2,1,0:T(8,128)(2,1)S(1)} %conv_block.1.x_ref, f32[1,512]{1,0:T(1,128)S(1)} %bitcast.22, bf16[512,1536]{1,0:T(8,128)(2,1)S(1)} %copy-done.3, bf16[512,512]{1,0:T(8,128)(2,1)S(1)} %copy-done.5), custom_call_target="tpu_custom_call" | custom-call | flops 4294967296 | bytes 4194304 | tf_op jit(solution)/shard_map/window_attention/pallas_call | solution.py:262
  35.8 0.0 copy-start.4
  35.9 0.0 copy-start.6
  35.9 0.0 copy-start.9
  35.9 32.2 %all_to_all.10 = bf16[32,32,512]{2,1,0:T(8,128)(2,1)S(1)} all-to-all(bf16[32,32,512]{2,1,0:T(8,128)(2,1)S(1)} %bitcast.18), channel_id=1, replica_groups=mesh['ns'=8,'ew'=4] {'ns','ew'}, dimensions={0} | all-to-all | bytes 2097152 | tf_op jit(solution)/shard_map/all_to_all | solution.py:371
  68.1 0.0 copy-done.4
  68.1 0.0 copy-done.6
  68.1 0.0 copy-done.9
  68.1 7.9 %grid_attention.1 = bf16[1024,512]{1,0:T(8,128)(2,1)S(1)} custom-call(bf16[1024,512]{1,0:T(8,128)(2,1)S(1)} %bitcast.19, f32[1,512]{1,0:T(1,128)S(1)} %bitcast.23, bf16[512,1536]{1,0:T(8,128)(2,1)S(1)} %copy-done.4, bf16[512,512]{1,0:T(8,128)(2,1)S(1)} %copy-done.6), custom_call_target="tpu_custom_call" | custom-call | flops 4294967296 | bytes 4194304 | tf_op jit(solution)/shard_map/grid_attention/pallas_call | solution.py:262
  76.0 29.3 %all_to_all.11 = bf16[32,32,512]{2,1,0:T(8,128)(2,1)S(1)} all-to-all(bf16[32,32,512]{2,1,0:T(8,128)(2,1)S(1)} %bitcast.20), channel_id=1, replica_groups=mesh['ns'=8,'ew'=4] {'ns','ew'}, dimensions={0} | all-to-all | bytes 2097152 | tf_op jit(solution)/shard_map/all_to_all | solution.py:371
  105.3 1.1 %copy.14 = bf16[1,8,4,2,2,8,512]{6,5,2,4,3,1,0:T(8,128)(2,1)} copy(bf16[1,8,4,2,2,8,512]{6,5,4,3,2,1,0:T(8,128)(2,1)S(1)} %bitcast.24) | data formatting | bytes 2097152 | tf_op jit(solution)/shard_map/stack;reshape | solution.py:419
  (3 shorter events, 0.0 us)
Async XLA Ops:
  1.0 6.0 %collective-permute-start.1 = (bf16[128,512]{1,0:T(8,128)(2,1)S(1)}, bf16[128,512]{1,0:T(8,128)(2,1)S(1)}, u32[]{:S(2)}, u32[]{:S(2)}) collective-permute-start(bf16[128,512]{1,0:T(8,128)(2,1)S(1)} %get-tuple-element.7), channel_id=1, source_target_pairs={{4,8},{12,16},{20,24},{8,4},{16,12},{24,20},{5,9},{13,17},{21,25},... | collective-permute-start | bytes 393224 | tf_op jit(solution)/shard_map/ppermute | solution.py:350
  1.7 5.3 %collective-permute-start = (bf16[128,512]{1,0:T(8,128)(2,1)S(1)}, bf16[128,512]{1,0:T(8,128)(2,1)S(1)}, u32[]{:S(2)}, u32[]{:S(2)}) collective-permute-start(bf16[128,512]{1,0:T(8,128)(2,1)S(1)} %get-tuple-element.8), channel_id=1, source_target_pairs={{0,4},{8,12},{16,20},{24,28},{4,0},{12,8},{20,16},{28,24},{1,5},{9... | collective-permute-start | bytes 393224 | tf_op jit(solution)/shard_map/ppermute | solution.py:350
  7.1 6.1 %collective-permute-start.3 = (bf16[10,512]{1,0:T(8,128)(2,1)S(1)}, bf16[10,512]{1,0:T(8,128)(2,1)S(1)}, u32[]{:S(2)}, u32[]{:S(2)}) collective-permute-start(bf16[10,512]{1,0:T(8,128)(2,1)S(1)} %get-tuple-element.13), channel_id=1, source_target_pairs={{1,2},{2,1},{5,6},{6,5},{9,10},{10,9},{13,14},{14,13},{17,18},{18,... | collective-permute-start | bytes 30728 | tf_op jit(solution)/shard_map/ppermute | solution.py:350
  7.7 6.2 %collective-permute-start.2 = (bf16[10,512]{1,0:T(8,128)(2,1)S(1)}, bf16[10,512]{1,0:T(8,128)(2,1)S(1)}, u32[]{:S(2)}, u32[]{:S(2)}) collective-permute-start(bf16[10,512]{1,0:T(8,128)(2,1)S(1)} %get-tuple-element.14), channel_id=1, source_target_pairs={{0,1},{2,3},{1,0},{3,2},{4,5},{6,7},{5,4},{7,6},{8,9},{10,11},{9,8... | collective-permute-start | bytes 30728 | tf_op jit(solution)/shard_map/ppermute | solution.py:350
  13.9 1.2 %copy-start = (bf16[8,128,512]{2,1,0:T(8,128)(2,1)S(1)}, bf16[8,128,512]{2,1,0:T(8,128)(2,1)}, u32[]{:S(2)}) copy-start(bf16[8,128,512]{2,1,0:T(8,128)(2,1)} %x_ref.1) | copy-start | bytes 3145732
  15.1 1.6 %copy-start.1 = (bf16[512,2048]{1,0:T(8,128)(2,1)S(1)}, bf16[512,2048]{1,0:T(8,128)(2,1)}, u32[]{:S(2)}) copy-start(bf16[512,2048]{1,0:T(8,128)(2,1)} %w1_ref.1) | copy-start | bytes 6291460
  16.7 1.6 %copy-start.2 = (bf16[2048,512]{1,0:T(8,128)(2,1)S(1)}, bf16[2048,512]{1,0:T(8,128)(2,1)}, u32[]{:S(2)}) copy-start(bf16[2048,512]{1,0:T(8,128)(2,1)} %w2_ref.1) | copy-start | bytes 6291460
  18.3 0.7 copy-start.7
  19.0 10.7 %copy-start.3 = (bf16[512,1536]{1,0:T(8,128)(2,1)S(1)}, bf16[512,1536]{1,0:T(8,128)(2,1)}, u32[]{:S(2)}) copy-start(bf16[512,1536]{1,0:T(8,128)(2,1)} %wqkv_ref.2) | copy-start | bytes 4718596
  19.0 10.7 %copy-start.5 = (bf16[512,512]{1,0:T(8,128)(2,1)S(1)}, bf16[512,512]{1,0:T(8,128)(2,1)}, u32[]{:S(2)}) copy-start(bf16[512,512]{1,0:T(8,128)(2,1)} %wout_ref.2) | copy-start | bytes 1572868
  19.0 10.7 %copy-start.8 = (f32[512]{0:T(512)S(1)}, f32[512]{0:T(512)}, u32[]{:S(2)}) copy-start(f32[512]{0:T(512)} %param.16) | copy-start | bytes 6148
  35.8 32.2 %copy-start.4 = (bf16[512,1536]{1,0:T(8,128)(2,1)S(1)}, bf16[512,1536]{1,0:T(8,128)(2,1)}, u32[]{:S(2)}) copy-start(bf16[512,1536]{1,0:T(8,128)(2,1)} %wqkv_ref.3) | copy-start | bytes 4718596
  35.9 32.2 %copy-start.6 = (bf16[512,512]{1,0:T(8,128)(2,1)S(1)}, bf16[512,512]{1,0:T(8,128)(2,1)}, u32[]{:S(2)}) copy-start(bf16[512,512]{1,0:T(8,128)(2,1)} %wout_ref.3) | copy-start | bytes 1572868
  35.9 32.2 %copy-start.9 = (f32[512]{0:T(512)S(1)}, f32[512]{0:T(512)}, u32[]{:S(2)}) copy-start(f32[512]{0:T(512)} %param.19) | copy-start | bytes 6148

commit v3 on v2

v3 whole, which is shorter than its diff:
```python
import functools
import math

import jax
import jax.numpy as jnp
from jax import lax
from jax.experimental import pallas as pl
from jax.experimental.pallas import tpu as pltpu
from jax.sharding import PartitionSpec as P

HEADS = 16
WINDOW = 8
EXPAND = 512
FEATURES = 1024
LANES = 128
GROUP = 8
MIB = 1024 * 1024

NT = (((1,), (1,)), ((), ()))


def normalize(floats, scale_gain):
    center = floats - jnp.mean(floats, axis=-1, keepdims=True)
    spread = jnp.mean(center * center, axis=-1, keepdims=True)
    return center * lax.rsqrt(spread + 1e-05) * scale_gain


def gelu(v):
    inner = v * (math.sqrt(2 / math.pi) + (math.sqrt(2 / math.pi) * 0.044715) * (v * v))
    half = 0.5 * v
    return half + half * jnp.tanh(inner)


def tiles(value):
    return [value[:, t : t + LANES] for t in range(0, value.shape[1], LANES)]


def strided(ref, start, size, stride):
    return jnp.concatenate([ref[t, pl.ds(start, size, stride=stride), :] for t in range(ref.shape[0])], axis=1)


def by_place(tmp_ref, block, store):
    cols = block.shape[0]
    strips = cols // WINDOW
    for t, part in enumerate(tiles(block)):
        tmp_ref[t] = part
    for b in range(WINDOW):
        store(b * strips, strips, strided(tmp_ref, b, strips, WINDOW))


def expand_kernel(x_ref, gain_ref, w1_ref, out_ref, n_ref, tmp_ref):
    rows, cols, _ = x_ref.shape

    @pl.when(pl.program_id(0) == 0)
    def _():
        gain = gain_ref[...]
        for i in range(rows):

            def store(at, count, part):
                n_ref[i * cols + at : i * cols + at + count, :] = part.astype(jnp.bfloat16)

            by_place(tmp_ref, normalize(x_ref[i].astype(jnp.float32), gain), store)

    w1 = w1_ref[...]
    for i in range(rows):
        hidden = jnp.dot(n_ref[i * cols : (i + 1) * cols, :], w1, preferred_element_type=jnp.float32)
        out_ref[i] = gelu(hidden.astype(jnp.bfloat16)).reshape(out_ref.shape[1:])


def expand_own(tokens, gain, w_expand):
    rows, cols, channels = tokens.shape
    width = w_expand.shape[1]
    features = min(EXPAND, width)
    strips = cols // WINDOW
    return pl.pallas_call(
        expand_kernel,
        grid=(width // features,),
        out_shape=jax.ShapeDtypeStruct((rows, WINDOW, strips, width), jnp.bfloat16),
        in_specs=[
            pl.BlockSpec(tokens.shape, lambda f: (0, 0, 0)),
            pl.BlockSpec((1, channels), lambda f: (0, 0)),
            pl.BlockSpec((channels, features), lambda f: (0, f)),
        ],
        out_specs=pl.BlockSpec((rows, WINDOW, strips, features), lambda f: (0, 0, 0, f)),
        scratch_shapes=[
            pltpu.VMEM((rows * cols, channels), jnp.bfloat16),
            pltpu.VMEM((channels // LANES, cols, LANES), jnp.float32),
        ],
        compiler_params=pltpu.CompilerParams(dimension_semantics=("arbitrary",), vmem_limit_bytes=56 * MIB),
        cost_estimate=pl.CostEstimate(
            flops=2 * rows * cols * channels * width,
            bytes_accessed=2 * channels * width + 2 * rows * cols * (channels + width),
            transcendentals=rows * cols * width,
        ),
        name="expand_own",
    )(tokens, gain.reshape(1, channels), w_expand)


def conv_kernel(
    conv_steps, shape, x_ref, e_ref, ns0_ref, ns1_ref, ew0_ref, ew1_ref, gain_ref, w1_ref, dw_ref, w2_ref,
    block_gain_ref, wqkv_hbm, wout_hbm, out_ref, n_ref, tmp_ref, edge_ref, side_ref, acc_ref, wqkv_ref, wout_ref, sems
):
    step = pl.program_id(0)
    rows, cols, channels = x_ref.shape
    strips = cols // WINDOW
    features = w1_ref.shape[1]
    side_rows = ew0_ref.shape[0]
    side_count = side_rows + -side_rows % 16
    copies = [
        pltpu.make_async_copy(wqkv_hbm, wqkv_ref, sems.at[0]),
        pltpu.make_async_copy(wout_hbm, wout_ref, sems.at[1]),
    ]

    @pl.when(step == 0)
    def _():
        for copy in copies:
            copy.start()
        gain = gain_ref[...]

        def sorted_pair(first_ref, second_ref, axis):
            first, second = first_ref[...].astype(jnp.float32), second_ref[...].astype(jnp.float32)
            even = lax.rem(lax.axis_index(axis), 2) == 0
            return jnp.where(even, second, first), jnp.where(even, first, second)

        for k, block in enumerate(sorted_pair(ns0_ref, ns1_ref, "ns")):

            def store(at, count, part):
                n_ref[k * cols + at : k * cols + at + count, :] = part.astype(jnp.bfloat16)

            by_place(tmp_ref, normalize(block, gain), store)
        pad = jnp.zeros((side_count - side_rows, channels), jnp.float32)
        for k, block in enumerate(sorted_pair(ew0_ref, ew1_ref, "ew")):
            start = 2 * cols + k * side_count
            n_ref[start : start + side_count, :] = normalize(
                jnp.concatenate([block, pad], axis=0), gain
            ).astype(jnp.bfloat16)
        for i in range(rows):

            def keep(at, count, part):
                for t, piece in enumerate(tiles(part)):
                    acc_ref[t, i * cols + at : i * cols + at + count, :] = piece

            by_place(tmp_ref, x_ref[i].astype(jnp.float32), keep)

    @pl.when(step < conv_steps)
    def _():
        w2 = w2_ref[...]
        taps = [[dw_ref[3 * a + b : 3 * a + b + 1, :].astype(jnp.bfloat16) for b in range(3)] for a in range(3)]
        halo = gelu(
            jnp.dot(n_ref[...], w1_ref[...], preferred_element_type=jnp.float32).astype(jnp.bfloat16)
        )
        for k in range(2):
            edge_ref[k] = halo[k * cols : (k + 1) * cols].reshape(WINDOW, strips, features)
        sides = halo[2 * cols :].astype(jnp.float32)
        place_in_strip = lax.broadcasted_iota(jnp.int32, (strips, features), 0)

        def own(i, b):
            if i == 0:
                return edge_ref[0, b]
            if i == rows + 1:
                return edge_ref[1, b]
            return e_ref[i - 1, b]

        for i in range(rows + 2):
            last = pltpu.roll(own(i, WINDOW - 1).astype(jnp.float32), 1, axis=0)
            first = pltpu.roll(own(i, 0).astype(jnp.float32), strips - 1, axis=0)
            low = jnp.where(place_in_strip == 0, sides[i : i + 1], last)
            high = jnp.where(place_in_strip == strips - 1, sides[side_count + i : side_count + i + 1], first)
            side_ref[i, 0] = low.astype(jnp.bfloat16)
            side_ref[i, 1] = high.astype(jnp.bfloat16)

        def at(i, b):
            if b < 0:
                return side_ref[i, 0]
            if b >= WINDOW:
                return side_ref[i, 1]
            return own(i, b)

        for i in range(rows):
            pieces = []
            for b in range(WINDOW):
                sums = []
                for da in range(3):
                    t = [at(i + da, b + db - 1) * taps[da][db] for db in range(3)]
                    sums.append(t[0] + t[1] + t[2])
                pieces.append(gelu(sums[0] + sums[1] + sums[2]))
            active = jnp.concatenate(pieces, axis=0)
            for t, part in enumerate(tiles(jnp.dot(active, w2, preferred_element_type=jnp.float32))):
                acc_ref[t, i * cols : (i + 1) * cols, :] += part

    @pl.when(step == conv_steps)
    def _():
        for copy in copies:
            copy.wait()

    @pl.when(step >= conv_steps)
    def _():
        all_places, across = shape
        _, places, shares, parts, side, _ = out_ref.shape
        size = rows * WINDOW
        first = (step - conv_steps) * places
        x = jnp.concatenate(
            [
                strided(acc_ref, share * across + part * all_places + first + j, size, strips)
                for j in range(places)
                for share in range(shares)
                for part in range(parts)
            ],
            axis=0,
        ).astype(jnp.bfloat16)
        result = attend_windows(x.astype(jnp.float32), block_gain_ref[...], wqkv_ref, wout_ref)
        result = result.astype(jnp.bfloat16).reshape(places, shares, parts, size // side, side, channels)
        for j in range(places):
            for share in range(shares):
                for part in range(parts):
                    out_ref[:, j, share, part] = result[j, share, part]


def conv_and_windows(tokens, expanded, swaps, gain, w_expand, dw_kernel, w_project, block_gain, w_qkv, w_out, shape):
    rows, cols, channels = tokens.shape
    places, shares, parts = shape
    width = w_expand.shape[1]
    features = min(FEATURES, width)
    strips = cols // WINDOW
    conv_steps = width // features
    block_places = max(1, min(places, GROUP // (shares * parts)))
    side_rows = swaps[2].shape[0]
    side_count = side_rows + -side_rows % 16
    whole = lambda *shape: pl.BlockSpec(shape, lambda step: (0,) * len(shape))
    block_of = lambda step: jnp.minimum(step, conv_steps - 1)
    tokens_of = rows * cols
    return pl.pallas_call(
        functools.partial(conv_kernel, conv_steps, (places, strips // shares)),
        grid=(conv_steps + places // block_places,),
        out_shape=jax.ShapeDtypeStruct((rows, places, shares, parts, WINDOW, channels), jnp.bfloat16),
        in_specs=[
            whole(*tokens.shape),
            pl.BlockSpec((rows, WINDOW, strips, features), lambda step: (0, 0, 0, block_of(step))),
            *[whole(*swap.shape) for swap in swaps],
            whole(1, channels),
            pl.BlockSpec((channels, features), lambda step: (0, block_of(step))),
            pl.BlockSpec((9, features), lambda step: (0, block_of(step))),
            pl.BlockSpec((features, channels), lambda step: (block_of(step), 0)),
            whole(1, channels),
            pl.BlockSpec(memory_space=pl.ANY),
            pl.BlockSpec(memory_space=pl.ANY),
        ],
        out_specs=pl.BlockSpec(
            (rows, block_places, shares, parts, WINDOW, channels),
            lambda step: (0, jnp.maximum(step - conv_steps, 0), 0, 0, 0, 0),
        ),
        scratch_shapes=[
            pltpu.VMEM((2 * cols + 2 * side_count, channels), jnp.bfloat16),
            pltpu.VMEM((channels // LANES, cols, LANES), jnp.float32),
            pltpu.VMEM((2, WINDOW, strips, features), jnp.bfloat16),
            pltpu.VMEM((rows + 2, 2, strips, features), jnp.bfloat16),
            pltpu.VMEM((channels // LANES, tokens_of, LANES), jnp.float32),
            pltpu.VMEM(w_qkv.shape, jnp.bfloat16),
            pltpu.VMEM(w_out.shape, jnp.bfloat16),
            pltpu.SemaphoreType.DMA((2,)),
        ],
        compiler_params=pltpu.CompilerParams(dimension_semantics=("arbitrary",), vmem_limit_bytes=56 * MIB),
        cost_estimate=pl.CostEstimate(
            flops=2 * tokens_of * channels * (width + 8 * channels),
            bytes_accessed=4 * channels * width + 2 * tokens_of * (2 * channels + width),
            transcendentals=tokens_of * width,
        ),
        name="conv_and_windows",
    )(
        tokens,
        expanded,
        *swaps,
        gain.reshape(1, channels),
        w_expand,
        dw_kernel.reshape(9, width),
        w_project,
        block_gain.reshape(1, channels),
        w_qkv,
        w_out,
    )


def attend_windows(x, gain, wqkv_ref, wout_ref):
    tokens, channels = x.shape
    head_dim = channels // HEADS
    group = LANES // head_dim
    size = WINDOW * WINDOW
    two = 2 * head_dim
    pairs, groups = tokens // (2 * size), channels // LANES
    units = [(p, g) for p in range(pairs) for g in range(groups)]
    scale = math.log2(math.e) / math.sqrt(head_dim)
    normed = normalize(x, gain).astype(jnp.bfloat16)

    def project(first):
        return jnp.dot(normed, wqkv_ref[:, first : first + channels], preferred_element_type=jnp.float32)

    queries = (project(0) * scale).astype(jnp.bfloat16)
    keys = project(channels).astype(jnp.bfloat16)
    values = lax.dot_general(
        wqkv_ref[:, 2 * channels :].T, normed, NT, preferred_element_type=jnp.float32
    ).astype(jnp.bfloat16)
    lane = lax.broadcasted_iota(jnp.int32, (1, LANES), 1)
    head_lanes = [(lane // head_dim == h).astype(jnp.float32).astype(jnp.bfloat16) for h in range(group)]
    halves = [(lane // size == h).astype(jnp.float32).astype(jnp.bfloat16) for h in range(2)]
    pick = (
        (
            lax.broadcasted_iota(jnp.int32, (size, 2 * size), 0)
            == lax.broadcasted_iota(jnp.int32, (size, 2 * size), 1) % size
        )
        .astype(jnp.float32)
        .astype(jnp.bfloat16)
    )
    scores = {}
    for p, g in units:
        for odd in range(2):
            at = (2 * p + odd) * size
            q = queries[at : at + size, g * LANES : (g + 1) * LANES]
            k = keys[at : at + size, g * LANES : (g + 1) * LANES]
            q_heads = jnp.concatenate([q * m for m in head_lanes], axis=0)
            scores[p, g, odd] = lax.dot_general(k, q_heads, NT, preferred_element_type=jnp.float32)
    weights = {}
    for unit, s in scores.items():
        raised = jnp.exp2(s - jnp.max(s, axis=0, keepdims=True))
        weights[unit] = (raised * (1.0 / jnp.sum(raised, axis=0, keepdims=True))).astype(jnp.bfloat16)
    mixed = {}
    for p, g in units:
        both = jnp.concatenate([weights[p, g, 0], weights[p, g, 1]], axis=0)
        for t in range(group // 2):
            at = g * LANES + t * two
            v = values[at : at + two, p * 2 * size : (p + 1) * 2 * size]
            v_halves = jnp.concatenate([v * m for m in halves], axis=0)
            mixed[p, g, t] = jnp.dot(
                v_halves, both[:, t * 2 * size : (t + 1) * 2 * size], preferred_element_type=jnp.float32
            ).astype(jnp.bfloat16)
    parts = {}
    for p, g in units:
        own = [
            mixed[p, g, t][odd * two + h * head_dim : odd * two + (h + 1) * head_dim] * halves[h]
            for odd in range(2)
            for t in range(group // 2)
            for h in range(2)
        ]
        parts[p, g] = lax.dot_general(
            pick, jnp.concatenate(own, axis=0), NT, preferred_element_type=jnp.float32
        ).astype(jnp.bfloat16)
    blended = [
        jnp.concatenate([parts[p, g][:, odd * LANES : (odd + 1) * LANES] for g in range(groups)], axis=1)
        for p in range(pairs)
        for odd in range(2)
    ]
    return x + jnp.dot(jnp.concatenate(blended, axis=0), wout_ref[...], preferred_element_type=jnp.float32)


def grid_kernel(x_ref, gain_ref, wqkv_ref, wout_ref, out_ref, floats_ref):
    step = pl.program_id(0)
    tokens, channels = x_ref.shape
    size = WINDOW * WINDOW
    windows = tokens // size
    block = windows // pl.num_programs(0)

    @pl.when(step == 0)
    def _():
        for t, part in enumerate(tiles(x_ref[...])):
            floats_ref[t] = part.astype(jnp.float32)

    first = step * block
    x = jnp.concatenate([strided(floats_ref, first + w, size, windows) for w in range(block)], axis=0)
    result = attend_windows(x, gain_ref[...], wqkv_ref, wout_ref)
    for t, part in enumerate(tiles(result)):
        for w in range(block):
            floats_ref[t, pl.ds(first + w, size, stride=windows), :] = part[w * size : (w + 1) * size]

    @pl.when(step == pl.num_programs(0) - 1)
    def _():
        for t in range(floats_ref.shape[0]):
            out_ref[:, t * LANES : (t + 1) * LANES] = floats_ref[t].astype(jnp.bfloat16)


def grid_attention(x, gain, w_qkv, w_out):
    tokens, channels = x.shape
    windows = tokens // (WINDOW * WINDOW)
    whole = lambda *shape: pl.BlockSpec(shape, lambda step: (0,) * len(shape))
    return pl.pallas_call(
        grid_kernel,
        grid=(windows // min(GROUP, windows),),
        out_shape=jax.ShapeDtypeStruct((tokens, channels), jnp.bfloat16),
        in_specs=[whole(tokens, channels), whole(1, channels), whole(*w_qkv.shape), whole(*w_out.shape)],
        out_specs=whole(tokens, channels),
        scratch_shapes=[pltpu.VMEM((channels // LANES, tokens, LANES), jnp.float32)],
        compiler_params=pltpu.CompilerParams(dimension_semantics=("arbitrary",), vmem_limit_bytes=24 * MIB),
        cost_estimate=pl.CostEstimate(
            flops=16 * tokens * channels * channels,
            bytes_accessed=8 * channels * channels + 4 * tokens * channels,
            transcendentals=HEADS * tokens * WINDOW * WINDOW,
        ),
        name="grid_attention",
    )(x, gain.reshape(1, channels), w_qkv, w_out)


def swap(low_edge, high_edge, axis, first):
    pairs = [(a, a + 1) for a in range(first, lax.axis_size(axis) - 1, 2)]
    lower = lax.rem(lax.axis_index(axis), 2) == first
    return lax.ppermute(
        jnp.where(lower, high_edge, low_edge), axis, pairs + [(target, source) for source, target in pairs]
    )


def halo(tokens):
    rows, cols, _ = tokens.shape
    ns0, ns1 = [swap(tokens[0], tokens[rows - 1], "ns", first) for first in range(2)]
    even = lax.rem(lax.axis_index("ns"), 2) == 0

    def column(c):
        north, south = jnp.where(even, ns1[c], ns0[c]), jnp.where(even, ns0[c], ns1[c])
        return jnp.concatenate([north[None], tokens[:, c], south[None]])

    ew0, ew1 = [swap(column(0), column(cols - 1), "ew", first) for first in range(2)]
    return ns0, ns1, ew0, ew1


def exchange(x):
    bands, strips = lax.axis_size("ns"), lax.axis_size("ew")
    if bands == WINDOW:
        return lax.all_to_all(x, ("ns", "ew"), 0, 0, tiled=True)
    inner = bands // WINDOW
    groups = [[a * inner + p for a in range(WINDOW)] for p in range(inner)]
    shape = x.shape
    x = x.reshape(WINDOW, strips, *shape[1:])
    x = lax.all_to_all(x, "ns", 0, 0, axis_index_groups=groups, tiled=True)
    x = lax.all_to_all(x, "ew", 1, 1, tiled=True)
    return x.reshape(shape)


def on_device(
    tokens,
    conv_gain,
    w_expand,
    dw_kernel,
    w_project,
    block_gain,
    block_qkv,
    block_out,
    grid_gain,
    grid_qkv,
    grid_out,
):
    rows, cols, channels = tokens.shape
    shares = WINDOW // lax.axis_size("ew")
    group = WINDOW * lax.axis_size("ew")
    across = cols // shares // WINDOW
    places = group // rows
    parts = across // places
    expanded = expand_own(tokens, conv_gain, w_expand)
    sent = conv_and_windows(
        tokens,
        expanded,
        halo(tokens),
        conv_gain,
        w_expand,
        dw_kernel,
        w_project,
        block_gain,
        block_qkv,
        block_out,
        (places, shares, parts),
    )
    x = exchange(sent.reshape(group, -1, channels))
    y = grid_attention(x.reshape(-1, channels), grid_gain, grid_qkv, grid_out)
    returned = exchange(y.reshape(group, -1, channels)).reshape(rows, places, shares, parts, WINDOW, channels)
    return jnp.transpose(returned, (0, 2, 3, 1, 4, 5)).reshape(rows, cols, channels)


def solution(mesh):
    in_specs = (P("ns", "ew", None), P(), P(), P(), P(), P(), P(), P(), P(), P(), P())
    out_specs = P("ns", "ew", None)
    return jax.shard_map(
        on_device, mesh=mesh, in_specs=in_specs, out_specs=out_specs, check_vma=False
    )
```

time: 108 us -> 110 us (1.019)
  Pallas kernels: 24.7 us -> 32.4 us
  local copies, waits for them, and re-layouts: 8.07 us -> 3.35 us
    pallas_call x3, Pallas kernels: 24.7 us -> 32.4 us  [the longest x1 17.2 us: conv_and_windows(): pl.pallas_call(functools.partial(conv_kernel, conv_steps, (places, strips...]
    unnamed x20 -> x16, local copies, waits for them, and re-layouts: 5.12 us -> 0.62 us
    another operation x1 -> x0, local copies, waits for them, and re-layouts: 1.11 us -> none  [on_device(): jnp.stack(pieces)]
  transfers between devices with their start and end apart: 4 -> 4, of which waited for: 2 -> 0; matrix products, arithmetic and copies ran while one was open for 2% -> 1% of each run, Pallas kernels for 0% -> 7%
where the time goes in v3:
time: 110 us; the launch traced here: 108 us
  blocking collectives  61.1 us (56%)
  Pallas kernels  32.4 us (29%)
  starting transfers between devices  10.2 us (9%)
  local copies, waits for them, and re-layouts  3.35 us (3%)
    all_to_all x2, blocking collectives, exchange(): return lax.all_to_all(x, ('ns', 'ew'), 0, 0, tiled=True)  61.1 us
    pallas_call x1, Pallas kernels, conv_and_windows(): pl.pallas_call(functools.partial(conv_kernel, conv_steps, (places, strips...  17.2 us
    ppermute x4, starting transfers between devices, swap(): lax.ppermute(jnp.where(lower, high_edge, low_edge), axis, pairs + [(targe...  10.2 us
    pallas_call x1, Pallas kernels, grid_attention(): pl.pallas_call(grid_kernel, grid=(windows // min(GROUP, windows),), out_s...  7.93 us
    pallas_call x1, Pallas kernels, expand_own(): pl.pallas_call(expand_kernel, grid=(width // features,), out_shape=jax.Sh...  7.23 us
  transfers between devices with their start and end apart: 4, of which 0 were waited for; matrix products, arithmetic and copies ran while one was open for 1% of the time, Pallas kernels for 7%

profile of v3, /device:TPU:0, one launch (start us, length us, event | category | flops | bytes accessed | tf_op | source)
XLA Modules:
  0.0 108.2 jit_solution(8811588244629715733)
XLA Ops:
  0.0 1.0 select_bitcast_fusion
  1.0 0.7 collective-permute-start.1
  1.7 4.4 %collective-permute-start = (bf16[128,512]{1,0:T(8,128)(2,1)S(1)}, bf16[128,512]{1,0:T(8,128)(2,1)S(1)}, u32[]{:S(2)}, u32[]{:S(2)}) collective-permute-start(bf16[128,512]{1,0:T(8,128)(2,1)S(1)} %get-tuple-element.8), channel_id=1, source_target_pairs={{0,4},{8,12},{16,20},{24,28},{4,0},{12,8},{20,16},{28,24},{1,5},{9... | collective-permute-start | bytes 393224 | tf_op jit(solution)/shard_map/ppermute | solution.py:403
  6.0 0.9 fusion
  6.9 0.0 collective-permute-done.1.ns1_ref
  7.0 0.0 copy-start.4
  7.0 0.0 collective-permute-done.ns0_ref
  7.0 0.0 copy-start.5
  7.1 0.7 collective-permute-start.3
  7.7 4.5 %collective-permute-start.2 = (bf16[10,512]{1,0:T(8,128)(2,1)S(1)}, bf16[10,512]{1,0:T(8,128)(2,1)S(1)}, u32[]{:S(2)}, u32[]{:S(2)}) collective-permute-start(bf16[10,512]{1,0:T(8,128)(2,1)S(1)} %get-tuple-element.14), channel_id=1, source_target_pairs={{0,1},{2,3},{1,0},{3,2},{4,5},{6,7},{5,4},{7,6},{8,9},{10,11},{9,8... | collective-permute-start | bytes 30728 | tf_op jit(solution)/shard_map/ppermute | solution.py:403
  12.2 0.0 copy-start.3
  12.2 7.2 %expand_own.1.e_ref = bf16[8,8,16,2048]{3,2,1,0:T(8,128)(2,1)} custom-call(bf16[8,128,512]{2,1,0:T(8,128)(2,1)} %x_ref.3, f32[1,512]{1,0:T(1,128)} %bitcast.23, bf16[512,2048]{1,0:T(8,128)(2,1)} %w1_ref.3), custom_call_target="tpu_custom_call" | custom-call | flops 2147483648 | bytes 7340032 | tf_op jit(solution)/shard_map/expand_own/pallas_call | solution.py:75
  19.4 0.0 copy-done.4
  19.4 0.0 copy-done.5
  19.4 0.0 copy-done.3
  19.4 0.7 reshape.33.dw_ref
  20.2 0.0 collective-permute-done.3.ew1_ref
  20.2 0.0 copy-start.6
  20.2 0.0 collective-permute-done.2.ew0_ref
  20.2 0.0 copy-start.7
  20.2 0.6 copy-done.6
  20.8 0.0 copy-done.7
  20.8 17.2 %conv_and_windows.1 = bf16[8,4,2,2,8,512]{5,4,3,2,1,0:T(8,128)(2,1)} custom-call(bf16[8,128,512]{2,1,0:T(8,128)(2,1)} %x_ref.3, bf16[8,8,16,2048]{3,2,1,0:T(8,128)(2,1)} %expand_own.1.e_ref, bf16[128,512]{1,0:T(8,128)(2,1)} %copy-done.5, bf16[128,512]{1,0:T(8,128)(2,1)} %copy-done.4, bf16[10,512]{1,0:T(8,128)(2,1)} %copy-done.7, bf16[10,512]{1,0:T(8,128)(2,1)} %copy-done.6, ...), custom_call_target="tpu_custom_call" | custom-call | flops 6442450944 | bytes 10485760 | tf_op jit(solution)/shard_map/conv_and_windows/pallas_call | solution.py:232
  38.0 0.0 copy-start
  38.0 0.0 copy-start.1
  38.0 0.0 copy-start.2
  38.1 31.8 %all_to_all.10 = bf16[32,32,512]{2,1,0:T(8,128)(2,1)S(1)} all-to-all(bf16[32,32,512]{2,1,0:T(8,128)(2,1)} %bitcast.22), channel_id=1, replica_groups=mesh['ns'=8,'ew'=4] {'ns','ew'}, dimensions={0} | all-to-all | bytes 2097152 | tf_op jit(solution)/shard_map/all_to_all | solution.py:424
  69.8 0.0 copy-done
  69.8 0.0 copy-done.1
  69.8 0.0 copy-done.2
  69.8 7.9 %grid_attention.1 = bf16[1024,512]{1,0:T(8,128)(2,1)S(1)} custom-call(bf16[1024,512]{1,0:T(8,128)(2,1)S(1)} %bitcast.18, f32[1,512]{1,0:T(1,128)S(1)} %bitcast.20, bf16[512,1536]{1,0:T(8,128)(2,1)S(1)} %copy-done, bf16[512,512]{1,0:T(8,128)(2,1)S(1)} %copy-done.1), custom_call_target="tpu_custom_call" | custom-call | flops 4294967296 | bytes 4194304 | tf_op jit(solution)/shard_map/grid_attention/pallas_call | solution.py:383
  77.8 29.3 %all_to_all.11 = bf16[32,32,512]{2,1,0:T(8,128)(2,1)S(1)} all-to-all(bf16[32,32,512]{2,1,0:T(8,128)(2,1)S(1)} %bitcast.19), channel_id=1, replica_groups=mesh['ns'=8,'ew'=4] {'ns','ew'}, dimensions={0} | all-to-all | bytes 2097152 | tf_op jit(solution)/shard_map/all_to_all | solution.py:424
  107.1 1.1 %copy.14 = bf16[8,4,2,2,8,512]{5,4,1,3,2,0:T(8,128)(2,1)} copy(bf16[8,4,2,2,8,512]{5,4,3,2,1,0:T(8,128)(2,1)S(1)} %bitcast.21) | data formatting | bytes 2097152 | tf_op jit(solution)/shard_map/reshape | solution.py:469
  (3 shorter events, 0.0 us)
Async XLA Ops:
  1.0 6.0 %collective-permute-start.1 = (bf16[128,512]{1,0:T(8,128)(2,1)S(1)}, bf16[128,512]{1,0:T(8,128)(2,1)S(1)}, u32[]{:S(2)}, u32[]{:S(2)}) collective-permute-start(bf16[128,512]{1,0:T(8,128)(2,1)S(1)} %get-tuple-element.7), channel_id=1, source_target_pairs={{4,8},{12,16},{20,24},{8,4},{16,12},{24,20},{5,9},{13,17},{21,25},... | collective-permute-start | bytes 393224 | tf_op jit(solution)/shard_map/ppermute | solution.py:403
  1.7 5.3 %collective-permute-start = (bf16[128,512]{1,0:T(8,128)(2,1)S(1)}, bf16[128,512]{1,0:T(8,128)(2,1)S(1)}, u32[]{:S(2)}, u32[]{:S(2)}) collective-permute-start(bf16[128,512]{1,0:T(8,128)(2,1)S(1)} %get-tuple-element.8), channel_id=1, source_target_pairs={{0,4},{8,12},{16,20},{24,28},{4,0},{12,8},{20,16},{28,24},{1,5},{9... | collective-permute-start | bytes 393224 | tf_op jit(solution)/shard_map/ppermute | solution.py:403
  7.0 12.5 %copy-start.4 = (bf16[128,512]{1,0:T(8,128)(2,1)}, bf16[128,512]{1,0:T(8,128)(2,1)S(1)}, u32[]{:S(2)}) copy-start(bf16[128,512]{1,0:T(8,128)(2,1)S(1)} %collective-permute-done.1.ns1_ref) | copy-start | bytes 393220
  7.0 12.4 %copy-start.5 = (bf16[128,512]{1,0:T(8,128)(2,1)}, bf16[128,512]{1,0:T(8,128)(2,1)S(1)}, u32[]{:S(2)}) copy-start(bf16[128,512]{1,0:T(8,128)(2,1)S(1)} %collective-permute-done.ns0_ref) | copy-start | bytes 393220
  7.1 13.1 %collective-permute-start.3 = (bf16[10,512]{1,0:T(8,128)(2,1)S(1)}, bf16[10,512]{1,0:T(8,128)(2,1)S(1)}, u32[]{:S(2)}, u32[]{:S(2)}) collective-permute-start(bf16[10,512]{1,0:T(8,128)(2,1)S(1)} %get-tuple-element.13), channel_id=1, source_target_pairs={{1,2},{2,1},{5,6},{6,5},{9,10},{10,9},{13,14},{14,13},{17,18},{18,... | collective-permute-start | bytes 30728 | tf_op jit(solution)/shard_map/ppermute | solution.py:403
  7.7 12.4 %collective-permute-start.2 = (bf16[10,512]{1,0:T(8,128)(2,1)S(1)}, bf16[10,512]{1,0:T(8,128)(2,1)S(1)}, u32[]{:S(2)}, u32[]{:S(2)}) collective-permute-start(bf16[10,512]{1,0:T(8,128)(2,1)S(1)} %get-tuple-element.14), channel_id=1, source_target_pairs={{0,1},{2,3},{1,0},{3,2},{4,5},{6,7},{5,4},{7,6},{8,9},{10,11},{9,8... | collective-permute-start | bytes 30728 | tf_op jit(solution)/shard_map/ppermute | solution.py:403
  12.2 7.2 %copy-start.3 = (f32[3,3,2048]{2,1,0:T(4,128)S(1)}, f32[3,3,2048]{2,1,0:T(4,128)}, u32[]{:S(2)}) copy-start(f32[3,3,2048]{2,1,0:T(4,128)} %param.14) | copy-start | bytes 221188
  20.2 0.6 copy-start.6
  20.2 0.6 copy-start.7
  38.0 31.8 %copy-start = (bf16[512,1536]{1,0:T(8,128)(2,1)S(1)}, bf16[512,1536]{1,0:T(8,128)(2,1)}, u32[]{:S(2)}) copy-start(bf16[512,1536]{1,0:T(8,128)(2,1)} %wqkv_ref.1) | copy-start | bytes 4718596
  38.0 31.8 %copy-start.1 = (bf16[512,512]{1,0:T(8,128)(2,1)S(1)}, bf16[512,512]{1,0:T(8,128)(2,1)}, u32[]{:S(2)}) copy-start(bf16[512,512]{1,0:T(8,128)(2,1)} %wout_ref.1) | copy-start | bytes 1572868
  38.0 31.8 %copy-start.2 = (f32[512]{0:T(512)S(1)}, f32[512]{0:T(512)}, u32[]{:S(2)}) copy-start(f32[512]{0:T(512)} %param.19) | copy-start | bytes 6148

commit v4 on v3

--- a/solution.py
+++ b/solution.py
@@ -10,7 +10,6 @@
 
 HEADS = 16
 WINDOW = 8
-EXPAND = 512
 FEATURES = 1024
 LANES = 128
 GROUP = 8
@@ -48,140 +47,106 @@
         store(b * strips, strips, strided(tmp_ref, b, strips, WINDOW))
 
 
-def expand_kernel(x_ref, gain_ref, w1_ref, out_ref, n_ref, tmp_ref):
-    rows, cols, _ = x_ref.shape
-
-    @pl.when(pl.program_id(0) == 0)
-    def _():
-        gain = gain_ref[...]
-        for i in range(rows):
-
-            def store(at, count, part):
-                n_ref[i * cols + at : i * cols + at + count, :] = part.astype(jnp.bfloat16)
-
-            by_place(tmp_ref, normalize(x_ref[i].astype(jnp.float32), gain), store)
-
-    w1 = w1_ref[...]
-    for i in range(rows):
-        hidden = jnp.dot(n_ref[i * cols : (i + 1) * cols, :], w1, preferred_element_type=jnp.float32)
-        out_ref[i] = gelu(hidden.astype(jnp.bfloat16)).reshape(out_ref.shape[1:])
-
-
-def expand_own(tokens, gain, w_expand):
-    rows, cols, channels = tokens.shape
-    width = w_expand.shape[1]
-    features = min(EXPAND, width)
-    strips = cols // WINDOW
-    return pl.pallas_call(
-        expand_kernel,
-        grid=(width // features,),
-        out_shape=jax.ShapeDtypeStruct((rows, WINDOW, strips, width), jnp.bfloat16),
-        in_specs=[
-            pl.BlockSpec(tokens.shape, lambda f: (0, 0, 0)),
-            pl.BlockSpec((1, channels), lambda f: (0, 0)),
-            pl.BlockSpec((channels, features), lambda f: (0, f)),
-        ],
-        out_specs=pl.BlockSpec((rows, WINDOW, strips, features), lambda f: (0, 0, 0, f)),
-        scratch_shapes=[
-            pltpu.VMEM((rows * cols, channels), jnp.bfloat16),
-            pltpu.VMEM((channels // LANES, cols, LANES), jnp.float32),
-        ],
-        compiler_params=pltpu.CompilerParams(dimension_semantics=("arbitrary",), vmem_limit_bytes=56 * MIB),
-        cost_estimate=pl.CostEstimate(
-            flops=2 * rows * cols * channels * width,
-            bytes_accessed=2 * channels * width + 2 * rows * cols * (channels + width),
-            transcendentals=rows * cols * width,
-        ),
-        name="expand_own",
-    )(tokens, gain.reshape(1, channels), w_expand)
-
-
 def conv_kernel(
-    conv_steps, shape, x_ref, e_ref, ns0_ref, ns1_ref, ew0_ref, ew1_ref, gain_ref, w1_ref, dw_ref, w2_ref,
-    block_gain_ref, wqkv_hbm, wout_hbm, out_ref, n_ref, tmp_ref, edge_ref, side_ref, acc_ref, wqkv_ref, wout_ref, sems
+    conv_steps, shape, x_hbm, ns0_ref, ns1_ref, ew0_ref, ew1_ref, gain_ref, w1_hbm, dw_ref, w2_hbm, block_gain_ref,
+    wqkv_hbm, wout_hbm, out_ref, n_ref, tmp_ref, e_ref, acc_ref, x_ref, w1_ref, w2_ref, wqkv_ref, wout_ref, sems
 ):
     step = pl.program_id(0)
     rows, cols, channels = x_ref.shape
     strips = cols // WINDOW
-    features = w1_ref.shape[1]
+    features = w1_ref.shape[2]
     side_rows = ew0_ref.shape[0]
     side_count = side_rows + -side_rows % 16
-    copies = [
-        pltpu.make_async_copy(wqkv_hbm, wqkv_ref, sems.at[0]),
-        pltpu.make_async_copy(wout_hbm, wout_ref, sems.at[1]),
+    copy_x = pltpu.make_async_copy(x_hbm, x_ref, sems.at[0])
+    copies_late = [
+        pltpu.make_async_copy(wqkv_hbm, wqkv_ref, sems.at[1]),
+        pltpu.make_async_copy(wout_hbm, wout_ref, sems.at[2]),
     ]
+    copies_w1 = [
+        pltpu.make_async_copy(w1_hbm.at[:, f * features : (f + 1) * features], w1_ref.at[f], sems.at[3 + f])
+        for f in range(conv_steps)
+    ]
+    copies_w2 = [
+        pltpu.make_async_copy(w2_hbm.at[f * features : (f + 1) * features], w2_ref.at[f], sems.at[3 + conv_steps + f])
+        for f in range(conv_steps)
+    ]
 
     @pl.when(step == 0)
     def _():
-        for copy in copies:
+        copy_x.start()
+        for f in range(conv_steps):
+            copies_w1[f].start()
+            copies_w2[f].start()
+        for copy in copies_late:
             copy.start()
         gain = gain_ref[...]
+
+        def place(slot, block):
+            def store(at, count, part):
+                n_ref[slot * cols + at : slot * cols + at + count, :] = part.astype(jnp.bfloat16)
+
+            by_place(tmp_ref, normalize(block, gain), store)
 
         def sorted_pair(first_ref, second_ref, axis):
             first, second = first_ref[...].astype(jnp.float32), second_ref[...].astype(jnp.float32)
             even = lax.rem(lax.axis_index(axis), 2) == 0
             return jnp.where(even, second, first), jnp.where(even, first, second)
 
-        for k, block in enumerate(sorted_pair(ns0_ref, ns1_ref, "ns")):
-
-            def store(at, count, part):
-                n_ref[k * cols + at : k * cols + at + count, :] = part.astype(jnp.bfloat16)
-
-            by_place(tmp_ref, normalize(block, gain), store)
+        north, south = sorted_pair(ns0_ref, ns1_ref, "ns")
+        place(0, north)
+        place(rows + 1, south)
         pad = jnp.zeros((side_count - side_rows, channels), jnp.float32)
         for k, block in enumerate(sorted_pair(ew0_ref, ew1_ref, "ew")):
-            start = 2 * cols + k * side_count
+            start = (rows + 2) * cols + k * side_count
             n_ref[start : start + side_count, :] = normalize(
                 jnp.concatenate([block, pad], axis=0), gain
             ).astype(jnp.bfloat16)
+        copy_x.wait()
         for i in range(rows):
+            block = x_ref[i].astype(jnp.float32)
+            place(i + 1, block)
 
             def keep(at, count, part):
                 for t, piece in enumerate(tiles(part)):
                     acc_ref[t, i * cols + at : i * cols + at + count, :] = piece
 
-            by_place(tmp_ref, x_ref[i].astype(jnp.float32), keep)
+            by_place(tmp_ref, block, keep)
+
+    for f in range(conv_steps):
+
+        @pl.when(step == f)
+        def _():
+            copies_w1[f].wait()
+            copies_w2[f].wait()
 
     @pl.when(step < conv_steps)
     def _():
-        w2 = w2_ref[...]
-        taps = [[dw_ref[3 * a + b : 3 * a + b + 1, :].astype(jnp.bfloat16) for b in range(3)] for a in range(3)]
-        halo = gelu(
-            jnp.dot(n_ref[...], w1_ref[...], preferred_element_type=jnp.float32).astype(jnp.bfloat16)
-        )
-        for k in range(2):
-            edge_ref[k] = halo[k * cols : (k + 1) * cols].reshape(WINDOW, strips, features)
-        sides = halo[2 * cols :].astype(jnp.float32)
+        w1 = w1_ref[step]
+        w2 = w2_ref[step]
+        taps = [[dw_ref[a, b : b + 1, :].astype(jnp.bfloat16) for b in range(3)] for a in range(3)]
+
+        def hidden(first, count):
+            return gelu(
+                jnp.dot(n_ref[first : first + count, :], w1, preferred_element_type=jnp.float32).astype(jnp.bfloat16)
+            )
+
+        sides = hidden((rows + 2) * cols, 2 * side_count).astype(jnp.float32)
         place_in_strip = lax.broadcasted_iota(jnp.int32, (strips, features), 0)
-
-        def own(i, b):
-            if i == 0:
-                return edge_ref[0, b]
-            if i == rows + 1:
-                return edge_ref[1, b]
-            return e_ref[i - 1, b]
-
         for i in range(rows + 2):
-            last = pltpu.roll(own(i, WINDOW - 1).astype(jnp.float32), 1, axis=0)
-            first = pltpu.roll(own(i, 0).astype(jnp.float32), strips - 1, axis=0)
+            own = hidden(i * cols, cols)
+            e_ref[i, 1 : WINDOW + 1] = own.reshape(WINDOW, strips, features)
+            last = pltpu.roll(own[(WINDOW - 1) * strips :].astype(jnp.float32), 1, axis=0)
+            first = pltpu.roll(own[:strips].astype(jnp.float32), strips - 1, axis=0)
             low = jnp.where(place_in_strip == 0, sides[i : i + 1], last)
             high = jnp.where(place_in_strip == strips - 1, sides[side_count + i : side_count + i + 1], first)
-            side_ref[i, 0] = low.astype(jnp.bfloat16)
-            side_ref[i, 1] = high.astype(jnp.bfloat16)
-
-        def at(i, b):
-            if b < 0:
-                return side_ref[i, 0]
-            if b >= WINDOW:
-                return side_ref[i, 1]
-            return own(i, b)
-
+            e_ref[i, 0] = low.astype(jnp.bfloat16)
+            e_ref[i, WINDOW + 1] = high.astype(jnp.bfloat16)
         for i in range(rows):
             pieces = []
             for b in range(WINDOW):
                 sums = []
                 for da in range(3):
-                    t = [at(i + da, b + db - 1) * taps[da][db] for db in range(3)]
+                    t = [e_ref[i + da, b + db] * taps[da][db] for db in range(3)]
                     sums.append(t[0] + t[1] + t[2])
                 pieces.append(gelu(sums[0] + sums[1] + sums[2]))
             active = jnp.concatenate(pieces, axis=0)
@@ -190,7 +155,7 @@
 
     @pl.when(step == conv_steps)
     def _():
-        for copy in copies:
+        for copy in copies_late:
             copy.wait()
 
     @pl.when(step >= conv_steps)
@@ -216,7 +181,7 @@
                     out_ref[:, j, share, part] = result[j, share, part]
 
 
-def conv_and_windows(tokens, expanded, swaps, gain, w_expand, dw_kernel, w_project, block_gain, w_qkv, w_out, shape):
+def conv_and_windows(tokens, swaps, gain, w_expand, dw_kernel, w_project, block_gain, w_qkv, w_out, shape):
     rows, cols, channels = tokens.shape
     places, shares, parts = shape
     width = w_expand.shape[1]
@@ -227,52 +192,52 @@
     side_rows = swaps[2].shape[0]
     side_count = side_rows + -side_rows % 16
     whole = lambda *shape: pl.BlockSpec(shape, lambda step: (0,) * len(shape))
-    block_of = lambda step: jnp.minimum(step, conv_steps - 1)
+    anywhere = pl.BlockSpec(memory_space=pl.ANY)
     tokens_of = rows * cols
     return pl.pallas_call(
         functools.partial(conv_kernel, conv_steps, (places, strips // shares)),
         grid=(conv_steps + places // block_places,),
         out_shape=jax.ShapeDtypeStruct((rows, places, shares, parts, WINDOW, channels), jnp.bfloat16),
         in_specs=[
-            whole(*tokens.shape),
-            pl.BlockSpec((rows, WINDOW, strips, features), lambda step: (0, 0, 0, block_of(step))),
+            anywhere,
             *[whole(*swap.shape) for swap in swaps],
             whole(1, channels),
-            pl.BlockSpec((channels, features), lambda step: (0, block_of(step))),
-            pl.BlockSpec((9, features), lambda step: (0, block_of(step))),
-            pl.BlockSpec((features, channels), lambda step: (block_of(step), 0)),
+            anywhere,
+            pl.BlockSpec((3, 3, features), lambda step: (0, 0, jnp.minimum(step, conv_steps - 1))),
+            anywhere,
             whole(1, channels),
-            pl.BlockSpec(memory_space=pl.ANY),
-            pl.BlockSpec(memory_space=pl.ANY),
+            anywhere,
+            anywhere,
         ],
         out_specs=pl.BlockSpec(
             (rows, block_places, shares, parts, WINDOW, channels),
             lambda step: (0, jnp.maximum(step - conv_steps, 0), 0, 0, 0, 0),
         ),
         scratch_shapes=[
-            pltpu.VMEM((2 * cols + 2 * side_count, channels), jnp.bfloat16),
+            pltpu.VMEM(((rows + 2) * cols + 2 * side_count, channels), jnp.bfloat16),
             pltpu.VMEM((channels // LANES, cols, LANES), jnp.float32),
-            pltpu.VMEM((2, WINDOW, strips, features), jnp.bfloat16),
-            pltpu.VMEM((rows + 2, 2, strips, features), jnp.bfloat16),
+            pltpu.VMEM((rows + 2, WINDOW + 2, strips, features), jnp.bfloat16),
             pltpu.VMEM((channels // LANES, tokens_of, LANES), jnp.float32),
+            pltpu.VMEM(tokens.shape, jnp.bfloat16),
+            pltpu.VMEM((conv_steps, channels, features), jnp.bfloat16),
+            pltpu.VMEM((conv_steps, features, channels), jnp.bfloat16),
             pltpu.VMEM(w_qkv.shape, jnp.bfloat16),
             pltpu.VMEM(w_out.shape, jnp.bfloat16),
-            pltpu.SemaphoreType.DMA((2,)),
+            pltpu.SemaphoreType.DMA((3 + 2 * conv_steps,)),
         ],
         compiler_params=pltpu.CompilerParams(dimension_semantics=("arbitrary",), vmem_limit_bytes=56 * MIB),
         cost_estimate=pl.CostEstimate(
-            flops=2 * tokens_of * channels * (width + 8 * channels),
-            bytes_accessed=4 * channels * width + 2 * tokens_of * (2 * channels + width),
-            transcendentals=tokens_of * width,
+            flops=4 * tokens_of * channels * (width + 4 * channels),
+            bytes_accessed=4 * channels * (width + 2 * channels) + 4 * tokens_of * channels,
+            transcendentals=2 * tokens_of * width,
         ),
         name="conv_and_windows",
     )(
         tokens,
-        expanded,
         *swaps,
         gain.reshape(1, channels),
         w_expand,
-        dw_kernel.reshape(9, width),
+        dw_kernel,
         w_project,
         block_gain.reshape(1, channels),
         w_qkv,
@@ -450,10 +415,8 @@
     across = cols // shares // WINDOW
     places = group // rows
     parts = across // places
-    expanded = expand_own(tokens, conv_gain, w_expand)
     sent = conv_and_windows(
         tokens,
-        expanded,
         halo(tokens),
         conv_gain,
         w_expand,

time: 110 us -> 106 us (0.964)
  Pallas kernels: 32.4 us -> 26.8 us
  waiting for transfers between devices: 0.06 us -> 1.77 us
    pallas_call x1 -> x0, Pallas kernels: 7.23 us -> none  [expand_own(): pl.pallas_call(expand_kernel, grid=(width // features,), out_shape=jax.Sh...]
    ppermute x4, waiting for transfers between devices: 0.06 us -> 1.77 us  [swap(): lax.ppermute(jnp.where(lower, high_edge, low_edge), axis, pairs + [(targe...]
    pallas_call x1, Pallas kernels: 17.2 us -> 18.9 us  [conv_and_windows(): pl.pallas_call(functools.partial(conv_kernel, conv_steps, (places, strips...]
  transfers between devices with their start and end apart: 4 -> 4, of which waited for: 0 -> 1; matrix products, arithmetic and copies ran while one was open for 1% -> 1% of each run, Pallas kernels for 7% -> 0%
where the time goes in v4:
time: 106 us; the launch traced here: 104 us
  blocking collectives  61.7 us (58%)
  Pallas kernels  26.8 us (25%)
  starting transfers between devices  10.2 us (10%)
  local copies, waits for them, and re-layouts  2.64 us (2%)
  waiting for transfers between devices  1.77 us (2%)
    all_to_all x2, blocking collectives, exchange(): return lax.all_to_all(x, ('ns', 'ew'), 0, 0, tiled=True)  61.7 us
    pallas_call x1, Pallas kernels, conv_and_windows(): pl.pallas_call(functools.partial(conv_kernel, conv_steps, (places, strips...  18.9 us
    ppermute x4, starting transfers between devices, swap(): lax.ppermute(jnp.where(lower, high_edge, low_edge), axis, pairs + [(targe...  10.2 us
    pallas_call x1, Pallas kernels, grid_attention(): pl.pallas_call(grid_kernel, grid=(windows // min(GROUP, windows),), out_s...  7.93 us
  transfers between devices with their start and end apart: 4, of which 1 were waited for; matrix products, arithmetic and copies ran while one was open for 1% of the time, Pallas kernels for 0%

profile of v4, /device:TPU:0, one launch (start us, length us, event | category | flops | bytes accessed | tf_op | source)
XLA Modules:
  0.0 104.2 jit_solution(3662314564851230305)
XLA Ops:
  0.0 1.0 select_bitcast_fusion
  1.0 0.7 collective-permute-start.1
  1.7 4.4 %collective-permute-start = (bf16[128,512]{1,0:T(8,128)(2,1)S(1)}, bf16[128,512]{1,0:T(8,128)(2,1)S(1)}, u32[]{:S(2)}, u32[]{:S(2)}) collective-permute-start(bf16[128,512]{1,0:T(8,128)(2,1)S(1)} %get-tuple-element.8), channel_id=1, source_target_pairs={{0,4},{8,12},{16,20},{24,28},{4,0},{12,8},{20,16},{28,24},{1,5},{9... | collective-permute-start | bytes 393224 | tf_op jit(solution)/shard_map/ppermute | solution.py:368
  6.0 0.9 fusion
  6.9 0.0 collective-permute-done.1.ns1_ref
  7.0 0.0 copy-start.3
  7.0 0.0 collective-permute-done.ns0_ref
  7.0 0.0 copy-start.4
  7.1 0.7 collective-permute-start.3
  7.7 4.5 %collective-permute-start.2 = (bf16[10,512]{1,0:T(8,128)(2,1)S(1)}, bf16[10,512]{1,0:T(8,128)(2,1)S(1)}, u32[]{:S(2)}, u32[]{:S(2)}) collective-permute-start(bf16[10,512]{1,0:T(8,128)(2,1)S(1)} %get-tuple-element.14), channel_id=1, source_target_pairs={{0,1},{2,3},{1,0},{3,2},{4,5},{6,7},{5,4},{7,6},{8,9},{10,11},{9,8... | collective-permute-start | bytes 30728 | tf_op jit(solution)/shard_map/ppermute | solution.py:368
  12.2 0.0 collective-permute-done.3.ew1_ref
  12.2 0.0 copy-start.5
  12.2 1.7 %collective-permute-done.2.ew0_ref = bf16[10,512]{1,0:T(8,128)(2,1)S(1)} collective-permute-done((bf16[10,512]{1,0:T(8,128)(2,1)S(1)}, bf16[10,512]{1,0:T(8,128)(2,1)S(1)}, u32[]{:S(2)}, u32[]{:S(2)}) %collective-permute-start.2) | collective-permute-done | bytes 10272 | tf_op jit(solution)/shard_map/ppermute | solution.py:368
  13.9 0.0 copy-start.6
  13.9 0.0 copy-done.3
  13.9 0.0 copy-done.4
  13.9 0.0 copy-done.5
  13.9 0.6 copy-done.6
  14.5 18.9 %conv_and_windows.1 = bf16[8,4,2,2,8,512]{5,4,3,2,1,0:T(8,128)(2,1)} custom-call(bf16[8,128,512]{2,1,0:T(8,128)(2,1)} %x_hbm.1, bf16[128,512]{1,0:T(8,128)(2,1)} %copy-done.4, bf16[128,512]{1,0:T(8,128)(2,1)} %copy-done.3, bf16[10,512]{1,0:T(8,128)(2,1)} %copy-done.6, bf16[10,512]{1,0:T(8,128)(2,1)} %copy-done.5, f32[1,512]{1,0:T(1,128)} %bitcast.23, ...), custom_call_target="tpu_custom_call" | custom-call | flops 8589934592 | bytes 8388608 | tf_op jit(solution)/shard_map/conv_and_windows/pallas_call | solution.py:197
  33.4 0.0 copy-start
  33.4 0.0 copy-start.1
  33.4 0.0 copy-start.2
  33.4 32.4 %all_to_all.10 = bf16[32,32,512]{2,1,0:T(8,128)(2,1)S(1)} all-to-all(bf16[32,32,512]{2,1,0:T(8,128)(2,1)} %bitcast.22), channel_id=1, replica_groups=mesh['ns'=8,'ew'=4] {'ns','ew'}, dimensions={0} | all-to-all | bytes 2097152 | tf_op jit(solution)/shard_map/all_to_all | solution.py:389
  65.8 0.0 copy-done
  65.9 0.0 copy-done.1
  65.9 0.0 copy-done.2
  65.9 7.9 %grid_attention.1 = bf16[1024,512]{1,0:T(8,128)(2,1)S(1)} custom-call(bf16[1024,512]{1,0:T(8,128)(2,1)S(1)} %bitcast.18, f32[1,512]{1,0:T(1,128)S(1)} %bitcast.20, bf16[512,1536]{1,0:T(8,128)(2,1)S(1)} %copy-done, bf16[512,512]{1,0:T(8,128)(2,1)S(1)} %copy-done.1), custom_call_target="tpu_custom_call" | custom-call | flops 4294967296 | bytes 4194304 | tf_op jit(solution)/shard_map/grid_attention/pallas_call | solution.py:348
  73.8 29.3 %all_to_all.11 = bf16[32,32,512]{2,1,0:T(8,128)(2,1)S(1)} all-to-all(bf16[32,32,512]{2,1,0:T(8,128)(2,1)S(1)} %bitcast.19), channel_id=1, replica_groups=mesh['ns'=8,'ew'=4] {'ns','ew'}, dimensions={0} | all-to-all | bytes 2097152 | tf_op jit(solution)/shard_map/all_to_all | solution.py:389
  103.1 1.1 %copy.14 = bf16[8,4,2,2,8,512]{5,4,1,3,2,0:T(8,128)(2,1)} copy(bf16[8,4,2,2,8,512]{5,4,3,2,1,0:T(8,128)(2,1)S(1)} %bitcast.21) | data formatting | bytes 2097152 | tf_op jit(solution)/shard_map/reshape | solution.py:432
  (3 shorter events, 0.0 us)
Async XLA Ops:
  1.0 6.0 %collective-permute-start.1 = (bf16[128,512]{1,0:T(8,128)(2,1)S(1)}, bf16[128,512]{1,0:T(8,128)(2,1)S(1)}, u32[]{:S(2)}, u32[]{:S(2)}) collective-permute-start(bf16[128,512]{1,0:T(8,128)(2,1)S(1)} %get-tuple-element.7), channel_id=1, source_target_pairs={{4,8},{12,16},{20,24},{8,4},{16,12},{24,20},{5,9},{13,17},{21,25},... | collective-permute-start | bytes 393224 | tf_op jit(solution)/shard_map/ppermute | solution.py:368
  1.7 5.3 %collective-permute-start = (bf16[128,512]{1,0:T(8,128)(2,1)S(1)}, bf16[128,512]{1,0:T(8,128)(2,1)S(1)}, u32[]{:S(2)}, u32[]{:S(2)}) collective-permute-start(bf16[128,512]{1,0:T(8,128)(2,1)S(1)} %get-tuple-element.8), channel_id=1, source_target_pairs={{0,4},{8,12},{16,20},{24,28},{4,0},{12,8},{20,16},{28,24},{1,5},{9... | collective-permute-start | bytes 393224 | tf_op jit(solution)/shard_map/ppermute | solution.py:368
  7.0 7.0 %copy-start.3 = (bf16[128,512]{1,0:T(8,128)(2,1)}, bf16[128,512]{1,0:T(8,128)(2,1)S(1)}, u32[]{:S(2)}) copy-start(bf16[128,512]{1,0:T(8,128)(2,1)S(1)} %collective-permute-done.1.ns1_ref) | copy-start | bytes 393220
  7.0 6.9 %copy-start.4 = (bf16[128,512]{1,0:T(8,128)(2,1)}, bf16[128,512]{1,0:T(8,128)(2,1)S(1)}, u32[]{:S(2)}) copy-start(bf16[128,512]{1,0:T(8,128)(2,1)S(1)} %collective-permute-done.ns0_ref) | copy-start | bytes 393220
  7.1 5.1 %collective-permute-start.3 = (bf16[10,512]{1,0:T(8,128)(2,1)S(1)}, bf16[10,512]{1,0:T(8,128)(2,1)S(1)}, u32[]{:S(2)}, u32[]{:S(2)}) collective-permute-start(bf16[10,512]{1,0:T(8,128)(2,1)S(1)} %get-tuple-element.13), channel_id=1, source_target_pairs={{1,2},{2,1},{5,6},{6,5},{9,10},{10,9},{13,14},{14,13},{17,18},{18,... | collective-permute-start | bytes 30728 | tf_op jit(solution)/shard_map/ppermute | solution.py:368
  7.7 6.2 %collective-permute-start.2 = (bf16[10,512]{1,0:T(8,128)(2,1)S(1)}, bf16[10,512]{1,0:T(8,128)(2,1)S(1)}, u32[]{:S(2)}, u32[]{:S(2)}) collective-permute-start(bf16[10,512]{1,0:T(8,128)(2,1)S(1)} %get-tuple-element.14), channel_id=1, source_target_pairs={{0,1},{2,3},{1,0},{3,2},{4,5},{6,7},{5,4},{7,6},{8,9},{10,11},{9,8... | collective-permute-start | bytes 30728 | tf_op jit(solution)/shard_map/ppermute | solution.py:368
  12.2 1.7 %copy-start.5 = (bf16[10,512]{1,0:T(8,128)(2,1)}, bf16[10,512]{1,0:T(8,128)(2,1)S(1)}, u32[]{:S(2)}) copy-start(bf16[10,512]{1,0:T(8,128)(2,1)S(1)} %collective-permute-done.3.ew1_ref) | copy-start | bytes 30724
  13.9 0.6 copy-start.6
  33.4 32.5 %copy-start = (bf16[512,1536]{1,0:T(8,128)(2,1)S(1)}, bf16[512,1536]{1,0:T(8,128)(2,1)}, u32[]{:S(2)}) copy-start(bf16[512,1536]{1,0:T(8,128)(2,1)} %wqkv_ref.1) | copy-start | bytes 4718596
  33.4 32.4 %copy-start.1 = (bf16[512,512]{1,0:T(8,128)(2,1)S(1)}, bf16[512,512]{1,0:T(8,128)(2,1)}, u32[]{:S(2)}) copy-start(bf16[512,512]{1,0:T(8,128)(2,1)} %wout_ref.1) | copy-start | bytes 1572868
  33.4 32.4 %copy-start.2 = (f32[512]{0:T(512)S(1)}, f32[512]{0:T(512)}, u32[]{:S(2)}) copy-start(f32[512]{0:T(512)} %param.19) | copy-start | bytes 6148

commit v5 on v4

--- a/solution.py
+++ b/solution.py
@@ -14,6 +14,9 @@
 LANES = 128
 GROUP = 8
 MIB = 1024 * 1024
+NORM_LIMIT = 8
+NORM_COST = 10_000_000_000
+CONV_LIMIT = 32
 
 NT = (((1,), (1,)), ((), ()))
 
@@ -47,93 +50,87 @@
         store(b * strips, strips, strided(tmp_ref, b, strips, WINDOW))
 
 
+def norm_kernel(x_ref, gain_ref, normed_ref, moved_ref, tmp_ref):
+    rows, cols, _ = x_ref.shape
+    gain = gain_ref[...]
+    for i in range(rows):
+
+        block = x_ref[i].astype(jnp.float32)
+        for out_ref, value in ((normed_ref, normalize(block, gain)), (moved_ref, block)):
+
+            def store(at, count, part):
+                out_ref[i * cols + at : i * cols + at + count, :] = part.astype(jnp.bfloat16)
+
+            by_place(tmp_ref, value, store)
+
+
+def norm_own(tokens, gain):
+    rows, cols, channels = tokens.shape
+    return pl.pallas_call(
+        norm_kernel,
+        out_shape=[jax.ShapeDtypeStruct((rows * cols, channels), jnp.bfloat16)] * 2,
+        scratch_shapes=[pltpu.VMEM((channels // LANES, cols, LANES), jnp.float32)],
+        compiler_params=pltpu.CompilerParams(vmem_limit_bytes=NORM_LIMIT * MIB),
+        cost_estimate=pl.CostEstimate(flops=NORM_COST, bytes_accessed=4 * rows * cols * channels, transcendentals=0),
+        name="norm_own",
+    )(tokens, gain.reshape(1, channels))
+
+
 def conv_kernel(
-    conv_steps, shape, x_hbm, ns0_ref, ns1_ref, ew0_ref, ew1_ref, gain_ref, w1_hbm, dw_ref, w2_hbm, block_gain_ref,
-    wqkv_hbm, wout_hbm, out_ref, n_ref, tmp_ref, e_ref, acc_ref, x_ref, w1_ref, w2_ref, wqkv_ref, wout_ref, sems
+    conv_steps, shape, x_ref, own_ref, ns0_ref, ns1_ref, ew0_ref, ew1_ref, gain_ref, w1_ref, dw_ref, w2_ref,
+    block_gain_ref, wqkv_ref, wout_ref, out_ref, n_ref, tmp_ref, e_ref, acc_ref
 ):
     step = pl.program_id(0)
-    rows, cols, channels = x_ref.shape
+    tokens, channels = x_ref.shape
+    rows = out_ref.shape[0]
+    cols = tokens // rows
     strips = cols // WINDOW
-    features = w1_ref.shape[2]
+    features = w1_ref.shape[1] // conv_steps
     side_rows = ew0_ref.shape[0]
     side_count = side_rows + -side_rows % 16
-    copy_x = pltpu.make_async_copy(x_hbm, x_ref, sems.at[0])
-    copies_late = [
-        pltpu.make_async_copy(wqkv_hbm, wqkv_ref, sems.at[1]),
-        pltpu.make_async_copy(wout_hbm, wout_ref, sems.at[2]),
-    ]
-    copies_w1 = [
-        pltpu.make_async_copy(w1_hbm.at[:, f * features : (f + 1) * features], w1_ref.at[f], sems.at[3 + f])
-        for f in range(conv_steps)
-    ]
-    copies_w2 = [
-        pltpu.make_async_copy(w2_hbm.at[f * features : (f + 1) * features], w2_ref.at[f], sems.at[3 + conv_steps + f])
-        for f in range(conv_steps)
-    ]
 
     @pl.when(step == 0)
     def _():
-        copy_x.start()
-        for f in range(conv_steps):
-            copies_w1[f].start()
-            copies_w2[f].start()
-        for copy in copies_late:
-            copy.start()
         gain = gain_ref[...]
-
-        def place(slot, block):
-            def store(at, count, part):
-                n_ref[slot * cols + at : slot * cols + at + count, :] = part.astype(jnp.bfloat16)
-
-            by_place(tmp_ref, normalize(block, gain), store)
 
         def sorted_pair(first_ref, second_ref, axis):
             first, second = first_ref[...].astype(jnp.float32), second_ref[...].astype(jnp.float32)
             even = lax.rem(lax.axis_index(axis), 2) == 0
             return jnp.where(even, second, first), jnp.where(even, first, second)
 
-        north, south = sorted_pair(ns0_ref, ns1_ref, "ns")
-        place(0, north)
-        place(rows + 1, south)
+        for k, block in enumerate(sorted_pair(ns0_ref, ns1_ref, "ns")):
+
+            def store(at, count, part):
+                n_ref[k * cols + at : k * cols + at + count, :] = part.astype(jnp.bfloat16)
+
+            by_place(tmp_ref, normalize(block, gain), store)
         pad = jnp.zeros((side_count - side_rows, channels), jnp.float32)
         for k, block in enumerate(sorted_pair(ew0_ref, ew1_ref, "ew")):
-            start = (rows + 2) * cols + k * side_count
+            start = 2 * cols + k * side_count
             n_ref[start : start + side_count, :] = normalize(
                 jnp.concatenate([block, pad], axis=0), gain
             ).astype(jnp.bfloat16)
-        copy_x.wait()
-        for i in range(rows):
-            block = x_ref[i].astype(jnp.float32)
-            place(i + 1, block)
-
-            def keep(at, count, part):
-                for t, piece in enumerate(tiles(part)):
-                    acc_ref[t, i * cols + at : i * cols + at + count, :] = piece
-
-            by_place(tmp_ref, block, keep)
-
-    for f in range(conv_steps):
-
-        @pl.when(step == f)
-        def _():
-            copies_w1[f].wait()
-            copies_w2[f].wait()
+        for t in range(channels // LANES):
+            acc_ref[t] = x_ref[:, t * LANES : (t + 1) * LANES].astype(jnp.float32)
 
     @pl.when(step < conv_steps)
     def _():
-        w1 = w1_ref[step]
-        w2 = w2_ref[step]
+        block = pl.ds(pl.multiple_of(step * features, features), features)
+        w1 = w1_ref[:, block]
+        w2 = w2_ref[block, :]
         taps = [[dw_ref[a, b : b + 1, :].astype(jnp.bfloat16) for b in range(3)] for a in range(3)]
 
-        def hidden(first, count):
-            return gelu(
-                jnp.dot(n_ref[first : first + count, :], w1, preferred_element_type=jnp.float32).astype(jnp.bfloat16)
-            )
-
-        sides = hidden((rows + 2) * cols, 2 * side_count).astype(jnp.float32)
+        def hidden(normed):
+            return gelu(jnp.dot(normed, w1, preferred_element_type=jnp.float32).astype(jnp.bfloat16))
+
+        sides = hidden(n_ref[2 * cols :, :]).astype(jnp.float32)
         place_in_strip = lax.broadcasted_iota(jnp.int32, (strips, features), 0)
         for i in range(rows + 2):
-            own = hidden(i * cols, cols)
+            if i in (0, rows + 1):
+                edge = i // (rows + 1)
+                own = hidden(n_ref[edge * cols : (edge + 1) * cols, :])
+            else:
+                own = hidden(own_ref[(i - 1) * cols : i * cols, :])
             e_ref[i, 1 : WINDOW + 1] = own.reshape(WINDOW, strips, features)
             last = pltpu.roll(own[(WINDOW - 1) * strips :].astype(jnp.float32), 1, axis=0)
             first = pltpu.roll(own[:strips].astype(jnp.float32), strips - 1, axis=0)
@@ -152,11 +149,6 @@
             active = jnp.concatenate(pieces, axis=0)
             for t, part in enumerate(tiles(jnp.dot(active, w2, preferred_element_type=jnp.float32))):
                 acc_ref[t, i * cols : (i + 1) * cols, :] += part
-
-    @pl.when(step == conv_steps)
-    def _():
-        for copy in copies_late:
-            copy.wait()
 
     @pl.when(step >= conv_steps)
     def _():
@@ -181,8 +173,9 @@
                     out_ref[:, j, share, part] = result[j, share, part]
 
 
-def conv_and_windows(tokens, swaps, gain, w_expand, dw_kernel, w_project, block_gain, w_qkv, w_out, shape):
-    rows, cols, channels = tokens.shape
+def conv_and_windows(moved, own, swaps, gain, w_expand, dw_kernel, w_project, block_gain, w_qkv, w_out, rows, shape):
+    tokens, channels = moved.shape
+    cols = tokens // rows
     places, shares, parts = shape
     width = w_expand.shape[1]
     features = min(FEATURES, width)
@@ -191,49 +184,43 @@
     block_places = max(1, min(places, GROUP // (shares * parts)))
     side_rows = swaps[2].shape[0]
     side_count = side_rows + -side_rows % 16
-    whole = lambda *shape: pl.BlockSpec(shape, lambda step: (0,) * len(shape))
-    anywhere = pl.BlockSpec(memory_space=pl.ANY)
-    tokens_of = rows * cols
+    vmem = pl.BlockSpec(memory_space=pltpu.VMEM)
     return pl.pallas_call(
         functools.partial(conv_kernel, conv_steps, (places, strips // shares)),
         grid=(conv_steps + places // block_places,),
         out_shape=jax.ShapeDtypeStruct((rows, places, shares, parts, WINDOW, channels), jnp.bfloat16),
         in_specs=[
-            anywhere,
-            *[whole(*swap.shape) for swap in swaps],
-            whole(1, channels),
-            anywhere,
+            vmem,
+            vmem,
+            *[vmem for swap in swaps],
+            vmem,
+            vmem,
             pl.BlockSpec((3, 3, features), lambda step: (0, 0, jnp.minimum(step, conv_steps - 1))),
-            anywhere,
-            whole(1, channels),
-            anywhere,
-            anywhere,
+            vmem,
+            vmem,
+            vmem,
+            vmem,
         ],
         out_specs=pl.BlockSpec(
             (rows, block_places, shares, parts, WINDOW, channels),
             lambda step: (0, jnp.maximum(step - conv_steps, 0), 0, 0, 0, 0),
         ),
         scratch_shapes=[
-            pltpu.VMEM(((rows + 2) * cols + 2 * side_count, channels), jnp.bfloat16),
+            pltpu.VMEM((2 * cols + 2 * side_count, channels), jnp.bfloat16),
             pltpu.VMEM((channels // LANES, cols, LANES), jnp.float32),
             pltpu.VMEM((rows + 2, WINDOW + 2, strips, features), jnp.bfloat16),
-            pltpu.VMEM((channels // LANES, tokens_of, LANES), jnp.float32),
-            pltpu.VMEM(tokens.shape, jnp.bfloat16),
-            pltpu.VMEM((conv_steps, channels, features), jnp.bfloat16),
-            pltpu.VMEM((conv_steps, features, channels), jnp.bfloat16),
-            pltpu.VMEM(w_qkv.shape, jnp.bfloat16),
-            pltpu.VMEM(w_out.shape, jnp.bfloat16),
-            pltpu.SemaphoreType.DMA((3 + 2 * conv_steps,)),
+            pltpu.VMEM((channels // LANES, tokens, LANES), jnp.float32),
         ],
-        compiler_params=pltpu.CompilerParams(dimension_semantics=("arbitrary",), vmem_limit_bytes=56 * MIB),
+        compiler_params=pltpu.CompilerParams(dimension_semantics=("arbitrary",), vmem_limit_bytes=CONV_LIMIT * MIB),
         cost_estimate=pl.CostEstimate(
-            flops=4 * tokens_of * channels * (width + 4 * channels),
-            bytes_accessed=4 * channels * (width + 2 * channels) + 4 * tokens_of * channels,
-            transcendentals=2 * tokens_of * width,
+            flops=4 * tokens * channels * (width + 4 * channels),
+            bytes_accessed=4 * channels * (width + 2 * channels) + 4 * tokens * channels,
+            transcendentals=2 * tokens * width,
         ),
         name="conv_and_windows",
     )(
-        tokens,
+        moved,
+        own,
         *swaps,
         gain.reshape(1, channels),
         w_expand,
@@ -370,17 +357,15 @@
     )
 
 
-def halo(tokens):
-    rows, cols, _ = tokens.shape
-    ns0, ns1 = [swap(tokens[0], tokens[rows - 1], "ns", first) for first in range(2)]
+def swap_columns(tokens, ns0, ns1):
+    cols = tokens.shape[1]
     even = lax.rem(lax.axis_index("ns"), 2) == 0
 
     def column(c):
         north, south = jnp.where(even, ns1[c], ns0[c]), jnp.where(even, ns0[c], ns1[c])
         return jnp.concatenate([north[None], tokens[:, c], south[None]])
 
-    ew0, ew1 = [swap(column(0), column(cols - 1), "ew", first) for first in range(2)]
-    return ns0, ns1, ew0, ew1
+    return [swap(column(0), column(cols - 1), "ew", first) for first in range(2)]
 
 
 def exchange(x):
@@ -415,9 +400,14 @@
     across = cols // shares // WINDOW
     places = group // rows
     parts = across // places
+    ns0, ns1 = [swap(tokens[0], tokens[rows - 1], "ns", first) for first in range(2)]
+    own, moved = norm_own(tokens, conv_gain)
+    tokens, own, moved = lax.optimization_barrier((tokens, own, moved))
+    ew0, ew1 = swap_columns(tokens, ns0, ns1)
     sent = conv_and_windows(
-        tokens,
-        halo(tokens),
+        moved,
+        own,
+        (ns0, ns1, ew0, ew1),
         conv_gain,
         w_expand,
         dw_kernel,
@@ -425,6 +415,7 @@
         block_gain,
         block_qkv,
         block_out,
+        rows,
         (places, shares, parts),
     )
     x = exchange(sent.reshape(group, -1, channels))

time: 106 us -> 102 us (0.962)
  blocking collectives: 61.7 us -> 58.3 us
  Pallas kernels: 26.8 us -> 25 us
    all_to_all x2, blocking collectives: 61.7 us -> 58.3 us  [exchange(): return lax.all_to_all(x, ('ns', 'ew'), 0, 0, tiled=True)]
    pallas_call x1, Pallas kernels: 18.9 us -> 15.6 us  [conv_and_windows(): pl.pallas_call(functools.partial(conv_kernel, conv_steps, (places, strips...]
    pallas_call x0 -> x1, Pallas kernels: none -> 1.41 us  [norm_own(): pl.pallas_call(norm_kernel, out_shape=[jax.ShapeDtypeStruct((rows * cols,...]
    unnamed x14 -> x26, local copies, waits for them, and re-layouts: 0.62 us -> 1.96 us
  transfers between devices with their start and end apart: 4 -> 4, of which waited for: 1 -> 1; matrix products, arithmetic and copies ran while one was open for 1% -> 1% of each run, Pallas kernels for 0% -> 1%
where the time goes in v5:
time: 102 us; the launch traced here: 100 us
  blocking collectives  58.3 us (57%)
  Pallas kernels  25 us (25%)
  starting transfers between devices  10.3 us (10%)
  local copies, waits for them, and re-layouts  3.66 us (4%)
  waiting for transfers between devices  1.72 us (2%)
  other arithmetic  1.03 us (1%)
    all_to_all x2, blocking collectives, exchange(): return lax.all_to_all(x, ('ns', 'ew'), 0, 0, tiled=True)  58.3 us
    pallas_call x1, Pallas kernels, conv_and_windows(): pl.pallas_call(functools.partial(conv_kernel, conv_steps, (places, strips...  15.6 us
    ppermute x4, starting transfers between devices, swap(): lax.ppermute(jnp.where(lower, high_edge, low_edge), axis, pairs + [(targe...  10.3 us
    pallas_call x1, Pallas kernels, grid_attention(): pl.pallas_call(grid_kernel, grid=(windows // min(GROUP, windows),), out_s...  7.93 us
  transfers between devices with their start and end apart: 4, of which 1 were waited for; matrix products, arithmetic and copies ran while one was open for 1% of the time, Pallas kernels for 1%

profile of v5, /device:TPU:0, one launch (start us, length us, event | category | flops | bytes accessed | tf_op | source)
XLA Modules:
  0.0 100.2 jit_solution(9750965923812194832)
XLA Ops:
  0.0 1.0 select_bitcast_fusion
  1.0 0.7 collective-permute-start.1
  1.7 4.4 %collective-permute-start = (bf16[128,512]{1,0:T(8,128)(2,1)S(1)}, bf16[128,512]{1,0:T(8,128)(2,1)S(1)}, u32[]{:S(2)}, u32[]{:S(2)}) collective-permute-start(bf16[128,512]{1,0:T(8,128)(2,1)S(1)} %get-tuple-element.18), channel_id=1, source_target_pairs={{0,4},{8,12},{16,20},{24,28},{4,0},{12,8},{20,16},{28,24},{1,5},{9... | collective-permute-start | bytes 393224 | tf_op jit(solution)/shard_map/ppermute | solution.py:355
  6.0 0.0 copy-start
  6.0 1.2 %copy-done = bf16[8,128,512]{2,1,0:T(8,128)(2,1)S(1)} copy-done((bf16[8,128,512]{2,1,0:T(8,128)(2,1)S(1)}, bf16[8,128,512]{2,1,0:T(8,128)(2,1)}, u32[]{:S(2)}) %copy-start) | copy-done | bytes 1048600
  7.3 0.0 copy-start.9
  7.3 0.7 copy-done.9
  7.9 0.0 copy-start.1
  7.9 0.0 copy-start.3
  7.9 0.0 copy-start.4
  7.9 0.0 copy-start.6
  7.9 1.4 %norm_own.1 = (bf16[1024,512]{1,0:T(8,128)(2,1)S(1)}, bf16[1024,512]{1,0:T(8,128)(2,1)S(1)}) custom-call(bf16[8,128,512]{2,1,0:T(8,128)(2,1)S(1)} %copy-done, f32[1,512]{1,0:T(1,128)S(1)} %bitcast.21), custom_call_target="tpu_custom_call" | custom-call | flops 10000000000 | bytes 2097152 | tf_op jit(solution)/shard_map/norm_own/pallas_call | solution.py:69
  9.4 0.0 copy-start.2
  9.4 0.0 copy-start.8
  9.4 0.0 copy-start.10
  9.4 0.0 copy-start.11
  9.4 0.0 copy-done.1
  9.4 0.6 copy.12
  10.0 0.0 collective-permute-done.1.ns1_ref
  10.0 0.0 collective-permute-done.ns0_ref
  10.1 0.8 collective-permute-start.3
  10.9 4.5 %collective-permute-start.2 = (bf16[10,512]{1,0:T(8,128)(2,1)S(1)}, bf16[10,512]{1,0:T(8,128)(2,1)S(1)}, u32[]{:S(2)}, u32[]{:S(2)}) collective-permute-start(bf16[10,512]{1,0:T(8,128)(2,1)S(1)} %get-tuple-element.24), channel_id=1, source_target_pairs={{0,1},{2,3},{1,0},{3,2},{4,5},{6,7},{5,4},{7,6},{8,9},{10,11},{9,8... | collective-permute-start | bytes 30728 | tf_op jit(solution)/shard_map/ppermute | solution.py:355
  15.4 0.0 collective-permute-done.3.ew1_ref
  15.4 1.7 %collective-permute-done.2.ew0_ref = bf16[10,512]{1,0:T(8,128)(2,1)S(1)} collective-permute-done((bf16[10,512]{1,0:T(8,128)(2,1)S(1)}, bf16[10,512]{1,0:T(8,128)(2,1)S(1)}, u32[]{:S(2)}, u32[]{:S(2)}) %collective-permute-start.2) | collective-permute-done | bytes 10272 | tf_op jit(solution)/shard_map/ppermute | solution.py:355
  17.1 0.0 copy-done.3
  17.1 0.0 copy-done.4
  17.1 0.0 copy-done.6
  17.1 0.0 copy-done.2
  17.1 0.0 copy-done.8
  17.1 0.0 copy-done.10
  17.1 0.0 copy-done.11
  17.1 15.6 %conv_and_windows.1 = bf16[8,4,2,2,8,512]{5,4,3,2,1,0:T(8,128)(2,1)S(1)} custom-call(bf16[1024,512]{1,0:T(8,128)(2,1)S(1)} %get-tuple-element.12.x_ref, bf16[1024,512]{1,0:T(8,128)(2,1)S(1)} %get-tuple-element.13.own_ref, bf16[128,512]{1,0:T(8,128)(2,1)S(1)} %collective-permute-done.ns0_ref, bf16[128,512]{1,0:T(8,128)(2,1)S(1)} %collective-permute-done.1.ns1_ref, ...), custom_call_target="tpu_custom_call" | custom-call | flops 8589934592 | bytes 8388608 | tf_op jit(solution)/shard_map/conv_and_windows/pallas_call | solution.py:188
  32.8 0.0 copy-start.5
  32.8 0.0 copy-start.7
  32.8 0.0 copy-start.12
  32.8 29.0 %all_to_all.10 = bf16[32,32,512]{2,1,0:T(8,128)(2,1)S(1)} all-to-all(bf16[32,32,512]{2,1,0:T(8,128)(2,1)S(1)} %bitcast.18), channel_id=1, replica_groups=mesh['ns'=8,'ew'=4] {'ns','ew'}, dimensions={0} | all-to-all | bytes 2097152 | tf_op jit(solution)/shard_map/all_to_all | solution.py:374
  61.8 0.0 copy-done.5
  61.8 0.0 copy-done.7
  61.8 0.0 copy-done.12
  61.8 7.9 %grid_attention.1 = bf16[1024,512]{1,0:T(8,128)(2,1)S(1)} custom-call(bf16[1024,512]{1,0:T(8,128)(2,1)S(1)} %bitcast.19, f32[1,512]{1,0:T(1,128)S(1)} %bitcast.24, bf16[512,1536]{1,0:T(8,128)(2,1)S(1)} %copy-done.5, bf16[512,512]{1,0:T(8,128)(2,1)S(1)} %copy-done.7), custom_call_target="tpu_custom_call" | custom-call | flops 4294967296 | bytes 4194304 | tf_op jit(solution)/shard_map/grid_attention/pallas_call | solution.py:335
  69.8 29.3 %all_to_all.11 = bf16[32,32,512]{2,1,0:T(8,128)(2,1)S(1)} all-to-all(bf16[32,32,512]{2,1,0:T(8,128)(2,1)S(1)} %bitcast.20), channel_id=1, replica_groups=mesh['ns'=8,'ew'=4] {'ns','ew'}, dimensions={0} | all-to-all | bytes 2097152 | tf_op jit(solution)/shard_map/all_to_all | solution.py:374
  99.1 1.1 %copy.14 = bf16[8,4,2,2,8,512]{5,4,1,3,2,0:T(8,128)(2,1)} copy(bf16[8,4,2,2,8,512]{5,4,3,2,1,0:T(8,128)(2,1)S(1)} %bitcast.25) | data formatting | bytes 2097152 | tf_op jit(solution)/shard_map/reshape | solution.py:423
  (3 shorter events, 0.0 us)
Async XLA Ops:
  1.0 9.0 %collective-permute-start.1 = (bf16[128,512]{1,0:T(8,128)(2,1)S(1)}, bf16[128,512]{1,0:T(8,128)(2,1)S(1)}, u32[]{:S(2)}, u32[]{:S(2)}) collective-permute-start(bf16[128,512]{1,0:T(8,128)(2,1)S(1)} %get-tuple-element.17), channel_id=1, source_target_pairs={{4,8},{12,16},{20,24},{8,4},{16,12},{24,20},{5,9},{13,17},{21,25},... | collective-permute-start | bytes 393224 | tf_op jit(solution)/shard_map/ppermute | solution.py:355
  1.7 8.4 %collective-permute-start = (bf16[128,512]{1,0:T(8,128)(2,1)S(1)}, bf16[128,512]{1,0:T(8,128)(2,1)S(1)}, u32[]{:S(2)}, u32[]{:S(2)}) collective-permute-start(bf16[128,512]{1,0:T(8,128)(2,1)S(1)} %get-tuple-element.18), channel_id=1, source_target_pairs={{0,4},{8,12},{16,20},{24,28},{4,0},{12,8},{20,16},{28,24},{1,5},{9... | collective-permute-start | bytes 393224 | tf_op jit(solution)/shard_map/ppermute | solution.py:355
  6.0 1.2 %copy-start = (bf16[8,128,512]{2,1,0:T(8,128)(2,1)S(1)}, bf16[8,128,512]{2,1,0:T(8,128)(2,1)}, u32[]{:S(2)}) copy-start(bf16[8,128,512]{2,1,0:T(8,128)(2,1)} %x_ref.1) | copy-start | bytes 3145732
  7.3 0.7 copy-start.9
  7.9 1.5 %copy-start.1 = (bf16[8,128,512]{2,1,0:T(8,128)(2,1)S(1)}, bf16[8,128,512]{2,1,0:T(8,128)(2,1)}, u32[]{:S(2)}) copy-start(bf16[8,128,512]{2,1,0:T(8,128)(2,1)} %x_ref.1) | copy-start | bytes 3145732
  7.9 9.1 %copy-start.3 = (bf16[2048,512]{1,0:T(8,128)(2,1)S(1)}, bf16[2048,512]{1,0:T(8,128)(2,1)}, u32[]{:S(2)}) copy-start(bf16[2048,512]{1,0:T(8,128)(2,1)} %w2_ref.1) | copy-start | bytes 6291460
  7.9 9.1 %copy-start.4 = (bf16[512,1536]{1,0:T(8,128)(2,1)S(1)}, bf16[512,1536]{1,0:T(8,128)(2,1)}, u32[]{:S(2)}) copy-start(bf16[512,1536]{1,0:T(8,128)(2,1)} %wqkv_ref.2) | copy-start | bytes 4718596
  7.9 9.1 %copy-start.6 = (bf16[512,512]{1,0:T(8,128)(2,1)S(1)}, bf16[512,512]{1,0:T(8,128)(2,1)}, u32[]{:S(2)}) copy-start(bf16[512,512]{1,0:T(8,128)(2,1)} %wout_ref.2) | copy-start | bytes 1572868
  9.4 7.7 %copy-start.2 = (bf16[512,2048]{1,0:T(8,128)(2,1)S(1)}, bf16[512,2048]{1,0:T(8,128)(2,1)}, u32[]{:S(2)}) copy-start(bf16[512,2048]{1,0:T(8,128)(2,1)} %w1_ref.1) | copy-start | bytes 6291460
  9.4 7.7 %copy-start.8 = (f32[3,3,2048]{2,1,0:T(4,128)S(1)}, f32[3,3,2048]{2,1,0:T(4,128)}, u32[]{:S(2)}) copy-start(f32[3,3,2048]{2,1,0:T(4,128)} %dw_ref.1) | copy-start | bytes 221188
  9.4 7.7 %copy-start.10 = (f32[512]{0:T(512)S(1)}, f32[512]{0:T(512)}, u32[]{:S(2)}) copy-start(f32[512]{0:T(512)} %param.12) | copy-start | bytes 6148
  9.4 7.7 %copy-start.11 = (f32[512]{0:T(512)S(1)}, f32[512]{0:T(512)}, u32[]{:S(2)}) copy-start(f32[512]{0:T(512)} %param.16) | copy-start | bytes 6148
  10.1 5.3 %collective-permute-start.3 = (bf16[10,512]{1,0:T(8,128)(2,1)S(1)}, bf16[10,512]{1,0:T(8,128)(2,1)S(1)}, u32[]{:S(2)}, u32[]{:S(2)}) collective-permute-start(bf16[10,512]{1,0:T(8,128)(2,1)S(1)} %get-tuple-element.23), channel_id=1, source_target_pairs={{1,2},{2,1},{5,6},{6,5},{9,10},{10,9},{13,14},{14,13},{17,18},{18,... | collective-permute-start | bytes 30728 | tf_op jit(solution)/shard_map/ppermute | solution.py:355
  10.9 6.2 %collective-permute-start.2 = (bf16[10,512]{1,0:T(8,128)(2,1)S(1)}, bf16[10,512]{1,0:T(8,128)(2,1)S(1)}, u32[]{:S(2)}, u32[]{:S(2)}) collective-permute-start(bf16[10,512]{1,0:T(8,128)(2,1)S(1)} %get-tuple-element.24), channel_id=1, source_target_pairs={{0,1},{2,3},{1,0},{3,2},{4,5},{6,7},{5,4},{7,6},{8,9},{10,11},{9,8... | collective-permute-start | bytes 30728 | tf_op jit(solution)/shard_map/ppermute | solution.py:355
  32.8 29.1 %copy-start.5 = (bf16[512,1536]{1,0:T(8,128)(2,1)S(1)}, bf16[512,1536]{1,0:T(8,128)(2,1)}, u32[]{:S(2)}) copy-start(bf16[512,1536]{1,0:T(8,128)(2,1)} %wqkv_ref.3) | copy-start | bytes 4718596
  32.8 29.1 %copy-start.7 = (bf16[512,512]{1,0:T(8,128)(2,1)S(1)}, bf16[512,512]{1,0:T(8,128)(2,1)}, u32[]{:S(2)}) copy-start(bf16[512,512]{1,0:T(8,128)(2,1)} %wout_ref.3) | copy-start | bytes 1572868
  32.8 29.0 %copy-start.12 = (f32[512]{0:T(512)S(1)}, f32[512]{0:T(512)}, u32[]{:S(2)}) copy-start(f32[512]{0:T(512)} %param.19) | copy-start | bytes 6148

commit v6 on v5

--- a/solution.py
+++ b/solution.py
@@ -10,11 +10,12 @@
 
 HEADS = 16
 WINDOW = 8
-FEATURES = 1024
+FEATURES = 2048
 LANES = 128
-GROUP = 8
+GROUP = 16
 MIB = 1024 * 1024
 NORM_LIMIT = 8
+EDGE_LIMIT = 12
 NORM_COST = 10_000_000_000
 CONV_LIMIT = 32
 
@@ -76,9 +77,53 @@
     )(tokens, gain.reshape(1, channels))
 
 
+def sorted_pair(first_ref, second_ref, axis):
+    first, second = first_ref[...].astype(jnp.float32), second_ref[...].astype(jnp.float32)
+    even = lax.rem(lax.axis_index(axis), 2) == 0
+    return jnp.where(even, second, first), jnp.where(even, first, second)
+
+
+def edge_kernel(ns0_ref, ns1_ref, gain_ref, w1_ref, out_ref, n_ref, tmp_ref):
+    cols = ns0_ref.shape[0]
+    gain = gain_ref[...]
+    for k, block in enumerate(sorted_pair(ns0_ref, ns1_ref, "ns")):
+
+        def store(at, count, part):
+            n_ref[k * cols + at : k * cols + at + count, :] = part.astype(jnp.bfloat16)
+
+        by_place(tmp_ref, normalize(block, gain), store)
+    for k in range(2):
+        normed = n_ref[k * cols : (k + 1) * cols, :]
+        hidden = jnp.dot(normed, w1_ref[...], preferred_element_type=jnp.float32)
+        out_ref[k] = gelu(hidden.astype(jnp.bfloat16)).reshape(out_ref.shape[1:])
+
+
+def expand_edges(ns0, ns1, gain, w_expand):
+    cols, channels = ns0.shape
+    width = w_expand.shape[1]
+    vmem = pl.BlockSpec(memory_space=pltpu.VMEM)
+    return pl.pallas_call(
+        edge_kernel,
+        out_shape=jax.ShapeDtypeStruct((2, WINDOW, cols // WINDOW, width), jnp.bfloat16),
+        in_specs=[vmem] * 4,
+        out_specs=vmem,
+        scratch_shapes=[
+            pltpu.VMEM((2 * cols, channels), jnp.bfloat16),
+            pltpu.VMEM((channels // LANES, cols, LANES), jnp.float32),
+        ],
+        compiler_params=pltpu.CompilerParams(vmem_limit_bytes=EDGE_LIMIT * MIB),
+        cost_estimate=pl.CostEstimate(
+            flops=4 * cols * channels * width,
+            bytes_accessed=2 * channels * width + 4 * cols * (channels + width),
+            transcendentals=2 * cols * width,
+        ),
+        name="expand_edges",
+    )(ns0, ns1, gain.reshape(1, channels), w_expand)
+
+
 def conv_kernel(
-    conv_steps, shape, x_ref, own_ref, ns0_ref, ns1_ref, ew0_ref, ew1_ref, gain_ref, w1_ref, dw_ref, w2_ref,
-    block_gain_ref, wqkv_ref, wout_ref, out_ref, n_ref, tmp_ref, e_ref, acc_ref
+    conv_steps, shape, x_ref, own_ref, edge_ref, ew0_ref, ew1_ref, gain_ref, w1_ref, dw_ref, w2_ref,
+    block_gain_ref, wqkv_ref, wout_ref, out_ref, n_ref, e_ref, acc_ref
 ):
     step = pl.program_id(0)
     tokens, channels = x_ref.shape
@@ -93,20 +138,9 @@
     def _():
         gain = gain_ref[...]
 
-        def sorted_pair(first_ref, second_ref, axis):
-            first, second = first_ref[...].astype(jnp.float32), second_ref[...].astype(jnp.float32)
-            even = lax.rem(lax.axis_index(axis), 2) == 0
-            return jnp.where(even, second, first), jnp.where(even, first, second)
-
-        for k, block in enumerate(sorted_pair(ns0_ref, ns1_ref, "ns")):
-
-            def store(at, count, part):
-                n_ref[k * cols + at : k * cols + at + count, :] = part.astype(jnp.bfloat16)
-
-            by_place(tmp_ref, normalize(block, gain), store)
         pad = jnp.zeros((side_count - side_rows, channels), jnp.float32)
         for k, block in enumerate(sorted_pair(ew0_ref, ew1_ref, "ew")):
-            start = 2 * cols + k * side_count
+            start = k * side_count
             n_ref[start : start + side_count, :] = normalize(
                 jnp.concatenate([block, pad], axis=0), gain
             ).astype(jnp.bfloat16)
@@ -123,17 +157,16 @@
         def hidden(normed):
             return gelu(jnp.dot(normed, w1, preferred_element_type=jnp.float32).astype(jnp.bfloat16))
 
-        sides = hidden(n_ref[2 * cols :, :]).astype(jnp.float32)
+        sides = hidden(n_ref[...]).astype(jnp.float32)
         place_in_strip = lax.broadcasted_iota(jnp.int32, (strips, features), 0)
         for i in range(rows + 2):
             if i in (0, rows + 1):
-                edge = i // (rows + 1)
-                own = hidden(n_ref[edge * cols : (edge + 1) * cols, :])
+                own = edge_ref[i // (rows + 1), :, :, block]
             else:
-                own = hidden(own_ref[(i - 1) * cols : i * cols, :])
-            e_ref[i, 1 : WINDOW + 1] = own.reshape(WINDOW, strips, features)
-            last = pltpu.roll(own[(WINDOW - 1) * strips :].astype(jnp.float32), 1, axis=0)
-            first = pltpu.roll(own[:strips].astype(jnp.float32), strips - 1, axis=0)
+                own = hidden(own_ref[(i - 1) * cols : i * cols, :]).reshape(WINDOW, strips, features)
+            e_ref[i, 1 : WINDOW + 1] = own
+            last = pltpu.roll(own[WINDOW - 1].astype(jnp.float32), 1, axis=0)
+            first = pltpu.roll(own[0].astype(jnp.float32), strips - 1, axis=0)
             low = jnp.where(place_in_strip == 0, sides[i : i + 1], last)
             high = jnp.where(place_in_strip == strips - 1, sides[side_count + i : side_count + i + 1], first)
             e_ref[i, 0] = low.astype(jnp.bfloat16)
@@ -152,8 +185,8 @@
 
     @pl.when(step >= conv_steps)
     def _():
-        all_places, across = shape
-        _, places, shares, parts, side, _ = out_ref.shape
+        places, across = shape
+        _, all_places, shares, parts, side, _ = out_ref.shape
         size = rows * WINDOW
         first = (step - conv_steps) * places
         x = jnp.concatenate(
@@ -170,10 +203,10 @@
         for j in range(places):
             for share in range(shares):
                 for part in range(parts):
-                    out_ref[:, j, share, part] = result[j, share, part]
-
-
-def conv_and_windows(moved, own, swaps, gain, w_expand, dw_kernel, w_project, block_gain, w_qkv, w_out, rows, shape):
+                    out_ref[:, first + j, share, part] = result[j, share, part]
+
+
+def conv_and_windows(moved, own, edges, ew0, ew1, gain, w_expand, dw_kernel, w_project, block_gain, w_qkv, w_out, rows, shape):
     tokens, channels = moved.shape
     cols = tokens // rows
     places, shares, parts = shape
@@ -182,17 +215,15 @@
     strips = cols // WINDOW
     conv_steps = width // features
     block_places = max(1, min(places, GROUP // (shares * parts)))
-    side_rows = swaps[2].shape[0]
+    side_rows = ew0.shape[0]
     side_count = side_rows + -side_rows % 16
     vmem = pl.BlockSpec(memory_space=pltpu.VMEM)
     return pl.pallas_call(
-        functools.partial(conv_kernel, conv_steps, (places, strips // shares)),
+        functools.partial(conv_kernel, conv_steps, (block_places, strips // shares)),
         grid=(conv_steps + places // block_places,),
         out_shape=jax.ShapeDtypeStruct((rows, places, shares, parts, WINDOW, channels), jnp.bfloat16),
         in_specs=[
-            vmem,
-            vmem,
-            *[vmem for swap in swaps],
+            *[vmem] * 5,
             vmem,
             vmem,
             pl.BlockSpec((3, 3, features), lambda step: (0, 0, jnp.minimum(step, conv_steps - 1))),
@@ -201,13 +232,9 @@
             vmem,
             vmem,
         ],
-        out_specs=pl.BlockSpec(
-            (rows, block_places, shares, parts, WINDOW, channels),
-            lambda step: (0, jnp.maximum(step - conv_steps, 0), 0, 0, 0, 0),
-        ),
+        out_specs=vmem,
         scratch_shapes=[
-            pltpu.VMEM((2 * cols + 2 * side_count, channels), jnp.bfloat16),
-            pltpu.VMEM((channels // LANES, cols, LANES), jnp.float32),
+            pltpu.VMEM((2 * side_count, channels), jnp.bfloat16),
             pltpu.VMEM((rows + 2, WINDOW + 2, strips, features), jnp.bfloat16),
             pltpu.VMEM((channels // LANES, tokens, LANES), jnp.float32),
         ],
@@ -221,7 +248,9 @@
     )(
         moved,
         own,
-        *swaps,
+        edges,
+        ew0,
+        ew1,
         gain.reshape(1, channels),
         w_expand,
         dw_kernel,
@@ -331,13 +360,13 @@
 def grid_attention(x, gain, w_qkv, w_out):
     tokens, channels = x.shape
     windows = tokens // (WINDOW * WINDOW)
-    whole = lambda *shape: pl.BlockSpec(shape, lambda step: (0,) * len(shape))
+    vmem = pl.BlockSpec(memory_space=pltpu.VMEM)
     return pl.pallas_call(
         grid_kernel,
         grid=(windows // min(GROUP, windows),),
         out_shape=jax.ShapeDtypeStruct((tokens, channels), jnp.bfloat16),
-        in_specs=[whole(tokens, channels), whole(1, channels), whole(*w_qkv.shape), whole(*w_out.shape)],
-        out_specs=whole(tokens, channels),
+        in_specs=[vmem] * 4,
+        out_specs=vmem,
         scratch_shapes=[pltpu.VMEM((channels // LANES, tokens, LANES), jnp.float32)],
         compiler_params=pltpu.CompilerParams(dimension_semantics=("arbitrary",), vmem_limit_bytes=24 * MIB),
         cost_estimate=pl.CostEstimate(
@@ -357,15 +386,15 @@
     )
 
 
-def swap_columns(tokens, ns0, ns1):
-    cols = tokens.shape[1]
+def swap_columns(tokens, corners0, corners1):
     even = lax.rem(lax.axis_index("ns"), 2) == 0
 
-    def column(c):
-        north, south = jnp.where(even, ns1[c], ns0[c]), jnp.where(even, ns0[c], ns1[c])
+    def column(c, k):
+        north, south = jnp.where(even, corners1[k], corners0[k]), jnp.where(even, corners0[k], corners1[k])
         return jnp.concatenate([north[None], tokens[:, c], south[None]])
 
-    return [swap(column(0), column(cols - 1), "ew", first) for first in range(2)]
+    low, high = column(0, 0), column(tokens.shape[1] - 1, 1)
+    return [swap(low, high, "ew", first) for first in range(2)]
 
 
 def exchange(x):
@@ -402,12 +431,15 @@
     parts = across // places
     ns0, ns1 = [swap(tokens[0], tokens[rows - 1], "ns", first) for first in range(2)]
     own, moved = norm_own(tokens, conv_gain)
-    tokens, own, moved = lax.optimization_barrier((tokens, own, moved))
-    ew0, ew1 = swap_columns(tokens, ns0, ns1)
+    corners = [jnp.concatenate([ns[:1], ns[cols - 1 :]]) for ns in (ns0, ns1)]
+    corners, own, moved = lax.optimization_barrier((corners, own, moved))
+    ew0, ew1 = swap_columns(tokens, *corners)
     sent = conv_and_windows(
         moved,
         own,
-        (ns0, ns1, ew0, ew1),
+        expand_edges(ns0, ns1, conv_gain, w_expand),
+        ew0,
+        ew1,
         conv_gain,
         w_expand,
         dw_kernel,

time: 102 us -> 100 us (0.980)
  waiting for transfers between devices: 1.72 us -> 0.57 us
    ppermute x4, waiting for transfers between devices: 1.72 us -> 0.57 us  [swap(): lax.ppermute(jnp.where(lower, high_edge, low_edge), axis, pairs + [(targe...]
    pallas_call x1 -> x2, Pallas kernels: 15.6 us -> 15.6 us  [the longest x1 14.5 us: conv_and_windows(): pl.pallas_call(functools.partial(conv_kernel, conv_steps, (block_places,...]
  transfers between devices with their start and end apart: 4 -> 4, of which waited for: 1 -> 1; matrix products, arithmetic and copies ran while one was open for 1% -> 1% of each run, Pallas kernels for 1% -> 3%
where the time goes in v6:
time: 100 us; the launch traced here: 98.7 us
  blocking collectives  58.1 us (58%)
  Pallas kernels  24.5 us (24%)
  starting transfers between devices  10.3 us (10%)
  local copies, waits for them, and re-layouts  3.99 us (4%)
  other arithmetic  1.05 us (1%)
    all_to_all x2, blocking collectives, exchange(): return lax.all_to_all(x, ('ns', 'ew'), 0, 0, tiled=True)  58.1 us
    pallas_call x1, Pallas kernels, conv_and_windows(): pl.pallas_call(functools.partial(conv_kernel, conv_steps, (block_places,...  14.5 us
    ppermute x4, starting transfers between devices, swap(): lax.ppermute(jnp.where(lower, high_edge, low_edge), axis, pairs + [(targe...  10.3 us
    pallas_call x1, Pallas kernels, grid_attention(): pl.pallas_call(grid_kernel, grid=(windows // min(GROUP, windows),), out_s...  7.44 us
  transfers between devices with their start and end apart: 4, of which 1 were waited for; matrix products, arithmetic and copies ran while one was open for 1% of the time, Pallas kernels for 3%

profile of v6, /device:TPU:0, one launch (start us, length us, event | category | flops | bytes accessed | tf_op | source)
XLA Modules:
  0.0 98.7 jit_solution(14928082534724284901)
XLA Ops:
  0.0 1.0 %select_bitcast_fusion = (bf16[128,512]{1,0:T(8,128)(2,1)S(1)}, bf16[128,512]{1,0:T(8,128)(2,1)S(1)}) fusion(pred[]{:T(512)S(6)} %eq.14, bf16[8,128,512]{2,1,0:T(8,128)(2,1)} %x_ref.1, pred[]{:T(512)S(6)} %eq.13), kind=kLoop, calls=%fused_computation | loop fusion | flops 131072 | bytes 524290 | tf_op jit(solution)/shard_map/jit(_where)/select_n | solution.py:385
  1.0 0.7 collective-permute-start.1
  1.7 4.4 %collective-permute-start = (bf16[128,512]{1,0:T(8,128)(2,1)S(1)}, bf16[128,512]{1,0:T(8,128)(2,1)S(1)}, u32[]{:S(2)}, u32[]{:S(2)}) collective-permute-start(bf16[128,512]{1,0:T(8,128)(2,1)S(1)} %get-tuple-element.20), channel_id=1, source_target_pairs={{0,4},{8,12},{16,20},{24,28},{4,0},{12,8},{20,16},{28,24},{1,5},{9... | collective-permute-start | bytes 393224 | tf_op jit(solution)/shard_map/ppermute | solution.py:384
  6.0 0.9 fusion
  6.9 0.0 copy-start.1
  6.9 1.2 %copy-done.1 = bf16[8,128,512]{2,1,0:T(8,128)(2,1)S(1)} copy-done((bf16[8,128,512]{2,1,0:T(8,128)(2,1)S(1)}, bf16[8,128,512]{2,1,0:T(8,128)(2,1)}, u32[]{:S(2)}) %copy-start.1) | copy-done | bytes 1048600
  8.2 0.0 copy-start.2
  8.2 0.7 copy-done.2
  8.8 0.0 copy-start
  8.8 0.0 copy-start.3
  8.8 0.0 copy-start.5
  8.8 1.4 %norm_own.1 = (bf16[1024,512]{1,0:T(8,128)(2,1)S(1)}, bf16[1024,512]{1,0:T(8,128)(2,1)S(1)}) custom-call(bf16[8,128,512]{2,1,0:T(8,128)(2,1)S(1)} %copy-done.1, f32[1,512]{1,0:T(1,128)S(1)} %bitcast.21), custom_call_target="tpu_custom_call" | custom-call | flops 10000000000 | bytes 2097152 | tf_op jit(solution)/shard_map/norm_own/pallas_call | solution.py:70
  10.3 0.0 copy-start.4
  10.3 0.0 copy-start.7
  10.3 0.0 copy-start.9
  10.3 0.0 copy-start.10
  10.3 0.0 collective-permute-done.1.ns1_ref
  10.3 0.0 collective-permute-done.ns0_ref
  10.5 0.8 collective-permute-start.3
  11.3 4.5 %collective-permute-start.2 = (bf16[10,512]{1,0:T(8,128)(2,1)S(1)}, bf16[10,512]{1,0:T(8,128)(2,1)S(1)}, u32[]{:S(2)}, u32[]{:S(2)}) collective-permute-start(bf16[10,512]{1,0:T(8,128)(2,1)S(1)} %get-tuple-element.26), channel_id=1, source_target_pairs={{0,1},{2,3},{1,0},{3,2},{4,5},{6,7},{5,4},{7,6},{8,9},{10,11},{9,8... | collective-permute-start | bytes 30728 | tf_op jit(solution)/shard_map/ppermute | solution.py:384
  15.7 0.0 copy-done
  15.7 0.0 copy-done.3
  15.7 1.1 %expand_edges.1.edge_ref = bf16[2,8,16,2048]{3,2,1,0:T(8,128)(2,1)S(1)} custom-call(bf16[128,512]{1,0:T(8,128)(2,1)S(1)} %collective-permute-done.ns0_ref, bf16[128,512]{1,0:T(8,128)(2,1)S(1)} %collective-permute-done.1.ns1_ref, f32[1,512]{1,0:T(1,128)S(1)} %bitcast.22, bf16[512,2048]{1,0:T(8,128)(2,1)S(1)} %copy-done), custom_call_target="tpu_custom_call" | custom-call | flops 536870912 | bytes 3407872 | tf_op jit(solution)/shard_map/expand_edges/pallas_call | solution.py:105
  16.9 0.0 collective-permute-done.3.ew1_ref
  16.9 0.6 collective-permute-done.2.ew0_ref
  17.4 0.0 copy-done.5
  17.4 0.0 copy-done.4
  17.4 0.0 copy-done.7
  17.5 0.0 copy-done.9
  17.5 0.0 copy-done.10
  17.5 14.5 %conv_and_windows.1 = bf16[8,4,2,2,8,512]{5,4,3,2,1,0:T(8,128)(2,1)S(1)} custom-call(bf16[1024,512]{1,0:T(8,128)(2,1)S(1)} %get-tuple-element.13.x_ref, bf16[1024,512]{1,0:T(8,128)(2,1)S(1)} %get-tuple-element.14.own_ref, bf16[2,8,16,2048]{3,2,1,0:T(8,128)(2,1)S(1)} %expand_edges.1.edge_ref, bf16[10,512]{1,0:T(8,128)(2,1)S(1)} %collective-permute-done.2.ew0_ref, ...), custom_call_target="tpu_custom_call" | custom-call | flops 8589934592 | bytes 8388608 | tf_op jit(solution)/shard_map/conv_and_windows/pallas_call | solution.py:221
  32.0 0.0 copy-start.6
  32.0 0.0 copy-start.8
  32.0 0.0 copy-start.11
  32.0 28.8 %all_to_all.10 = bf16[32,32,512]{2,1,0:T(8,128)(2,1)S(1)} all-to-all(bf16[32,32,512]{2,1,0:T(8,128)(2,1)S(1)} %bitcast.18), channel_id=1, replica_groups=mesh['ns'=8,'ew'=4] {'ns','ew'}, dimensions={0} | all-to-all | bytes 2097152 | tf_op jit(solution)/shard_map/all_to_all | solution.py:403
  60.8 0.0 copy-done.6
  60.8 0.0 copy-done.8
  60.8 0.0 copy-done.11
  60.8 7.4 %grid_attention.1 = bf16[1024,512]{1,0:T(8,128)(2,1)S(1)} custom-call(bf16[1024,512]{1,0:T(8,128)(2,1)S(1)} %bitcast.19, f32[1,512]{1,0:T(1,128)S(1)} %bitcast.25, bf16[512,1536]{1,0:T(8,128)(2,1)S(1)} %copy-done.6, bf16[512,512]{1,0:T(8,128)(2,1)S(1)} %copy-done.8), custom_call_target="tpu_custom_call" | custom-call | flops 4294967296 | bytes 4194304 | tf_op jit(solution)/shard_map/grid_attention/pallas_call | solution.py:364
  68.2 29.3 %all_to_all.11 = bf16[32,32,512]{2,1,0:T(8,128)(2,1)S(1)} all-to-all(bf16[32,32,512]{2,1,0:T(8,128)(2,1)S(1)} %bitcast.20), channel_id=1, replica_groups=mesh['ns'=8,'ew'=4] {'ns','ew'}, dimensions={0} | all-to-all | bytes 2097152 | tf_op jit(solution)/shard_map/all_to_all | solution.py:403
  97.6 1.1 %copy.14 = bf16[8,4,2,2,8,512]{5,4,1,3,2,0:T(8,128)(2,1)} copy(bf16[8,4,2,2,8,512]{5,4,3,2,1,0:T(8,128)(2,1)S(1)} %bitcast.26) | data formatting | bytes 2097152 | tf_op jit(solution)/shard_map/reshape | solution.py:455
  (6 shorter events, 0.1 us)
Async XLA Ops:
  1.0 9.3 %collective-permute-start.1 = (bf16[128,512]{1,0:T(8,128)(2,1)S(1)}, bf16[128,512]{1,0:T(8,128)(2,1)S(1)}, u32[]{:S(2)}, u32[]{:S(2)}) collective-permute-start(bf16[128,512]{1,0:T(8,128)(2,1)S(1)} %get-tuple-element.19), channel_id=1, source_target_pairs={{4,8},{12,16},{20,24},{8,4},{16,12},{24,20},{5,9},{13,17},{21,25},... | collective-permute-start | bytes 393224 | tf_op jit(solution)/shard_map/ppermute | solution.py:384
  1.7 8.7 %collective-permute-start = (bf16[128,512]{1,0:T(8,128)(2,1)S(1)}, bf16[128,512]{1,0:T(8,128)(2,1)S(1)}, u32[]{:S(2)}, u32[]{:S(2)}) collective-permute-start(bf16[128,512]{1,0:T(8,128)(2,1)S(1)} %get-tuple-element.20), channel_id=1, source_target_pairs={{0,4},{8,12},{16,20},{24,28},{4,0},{12,8},{20,16},{28,24},{1,5},{9... | collective-permute-start | bytes 393224 | tf_op jit(solution)/shard_map/ppermute | solution.py:384
  6.9 1.2 %copy-start.1 = (bf16[8,128,512]{2,1,0:T(8,128)(2,1)S(1)}, bf16[8,128,512]{2,1,0:T(8,128)(2,1)}, u32[]{:S(2)}) copy-start(bf16[8,128,512]{2,1,0:T(8,128)(2,1)} %x_ref.1) | copy-start | bytes 3145732
  8.2 0.7 copy-start.2
  8.8 6.9 %copy-start = (bf16[512,2048]{1,0:T(8,128)(2,1)S(1)}, bf16[512,2048]{1,0:T(8,128)(2,1)}, u32[]{:S(2)}) copy-start(bf16[512,2048]{1,0:T(8,128)(2,1)} %w1_ref.3) | copy-start | bytes 6291460
  8.8 6.9 %copy-start.3 = (f32[512]{0:T(512)S(1)}, f32[512]{0:T(512)}, u32[]{:S(2)}) copy-start(f32[512]{0:T(512)} %param.12) | copy-start | bytes 6148
  8.8 8.6 %copy-start.5 = (bf16[512,1536]{1,0:T(8,128)(2,1)S(1)}, bf16[512,1536]{1,0:T(8,128)(2,1)}, u32[]{:S(2)}) copy-start(bf16[512,1536]{1,0:T(8,128)(2,1)} %wqkv_ref.2) | copy-start | bytes 4718596
  10.3 7.2 %copy-start.4 = (bf16[2048,512]{1,0:T(8,128)(2,1)S(1)}, bf16[2048,512]{1,0:T(8,128)(2,1)}, u32[]{:S(2)}) copy-start(bf16[2048,512]{1,0:T(8,128)(2,1)} %w2_ref.1) | copy-start | bytes 6291460
  10.3 7.2 %copy-start.7 = (bf16[512,512]{1,0:T(8,128)(2,1)S(1)}, bf16[512,512]{1,0:T(8,128)(2,1)}, u32[]{:S(2)}) copy-start(bf16[512,512]{1,0:T(8,128)(2,1)} %wout_ref.2) | copy-start | bytes 1572868
  10.3 7.2 %copy-start.9 = (f32[3,3,2048]{2,1,0:T(4,128)S(1)}, f32[3,3,2048]{2,1,0:T(4,128)}, u32[]{:S(2)}) copy-start(f32[3,3,2048]{2,1,0:T(4,128)} %dw_ref.1) | copy-start | bytes 221188
  10.3 7.2 %copy-start.10 = (f32[512]{0:T(512)S(1)}, f32[512]{0:T(512)}, u32[]{:S(2)}) copy-start(f32[512]{0:T(512)} %param.16) | copy-start | bytes 6148
  10.5 6.4 %collective-permute-start.3 = (bf16[10,512]{1,0:T(8,128)(2,1)S(1)}, bf16[10,512]{1,0:T(8,128)(2,1)S(1)}, u32[]{:S(2)}, u32[]{:S(2)}) collective-permute-start(bf16[10,512]{1,0:T(8,128)(2,1)S(1)} %get-tuple-element.25), channel_id=1, source_target_pairs={{1,2},{2,1},{5,6},{6,5},{9,10},{10,9},{13,14},{14,13},{17,18},{18,... | collective-permute-start | bytes 30728 | tf_op jit(solution)/shard_map/ppermute | solution.py:384
  11.3 6.2 %collective-permute-start.2 = (bf16[10,512]{1,0:T(8,128)(2,1)S(1)}, bf16[10,512]{1,0:T(8,128)(2,1)S(1)}, u32[]{:S(2)}, u32[]{:S(2)}) collective-permute-start(bf16[10,512]{1,0:T(8,128)(2,1)S(1)} %get-tuple-element.26), channel_id=1, source_target_pairs={{0,1},{2,3},{1,0},{3,2},{4,5},{6,7},{5,4},{7,6},{8,9},{10,11},{9,8... | collective-permute-start | bytes 30728 | tf_op jit(solution)/shard_map/ppermute | solution.py:384
  32.0 28.8 %copy-start.6 = (bf16[512,1536]{1,0:T(8,128)(2,1)S(1)}, bf16[512,1536]{1,0:T(8,128)(2,1)}, u32[]{:S(2)}) copy-start(bf16[512,1536]{1,0:T(8,128)(2,1)} %wqkv_ref.3) | copy-start | bytes 4718596
  32.0 28.8 %copy-start.8 = (bf16[512,512]{1,0:T(8,128)(2,1)S(1)}, bf16[512,512]{1,0:T(8,128)(2,1)}, u32[]{:S(2)}) copy-start(bf16[512,512]{1,0:T(8,128)(2,1)} %wout_ref.3) | copy-start | bytes 1572868
  32.0 28.8 %copy-start.11 = (f32[512]{0:T(512)S(1)}, f32[512]{0:T(512)}, u32[]{:S(2)}) copy-start(f32[512]{0:T(512)} %param.19) | copy-start | bytes 6148

commit v7 on v6

--- a/solution.py
+++ b/solution.py
@@ -275,30 +275,33 @@
     def project(first):
         return jnp.dot(normed, wqkv_ref[:, first : first + channels], preferred_element_type=jnp.float32)
 
-    queries = (project(0) * scale).astype(jnp.bfloat16)
+    queries = lax.dot_general(wqkv_ref[:, :channels].T, normed, NT, preferred_element_type=jnp.float32) * scale
     keys = project(channels).astype(jnp.bfloat16)
     values = lax.dot_general(
         wqkv_ref[:, 2 * channels :].T, normed, NT, preferred_element_type=jnp.float32
     ).astype(jnp.bfloat16)
     lane = lax.broadcasted_iota(jnp.int32, (1, LANES), 1)
-    head_lanes = [(lane // head_dim == h).astype(jnp.float32).astype(jnp.bfloat16) for h in range(group)]
     halves = [(lane // size == h).astype(jnp.float32).astype(jnp.bfloat16) for h in range(2)]
-    pick = (
-        (
-            lax.broadcasted_iota(jnp.int32, (size, 2 * size), 0)
-            == lax.broadcasted_iota(jnp.int32, (size, 2 * size), 1) % size
-        )
-        .astype(jnp.float32)
-        .astype(jnp.bfloat16)
-    )
     scores = {}
+    zeros = jnp.zeros((two, 2 * size), jnp.bfloat16)
     for p, g in units:
+        own = queries[g * LANES : (g + 1) * LANES, p * 2 * size : (p + 1) * 2 * size]
+        turned = pltpu.roll(own, size, axis=1).astype(jnp.bfloat16)
+        own = own.astype(jnp.bfloat16)
         for odd in range(2):
             at = (2 * p + odd) * size
-            q = queries[at : at + size, g * LANES : (g + 1) * LANES]
             k = keys[at : at + size, g * LANES : (g + 1) * LANES]
-            q_heads = jnp.concatenate([q * m for m in head_lanes], axis=0)
-            scores[p, g, odd] = lax.dot_general(k, q_heads, NT, preferred_element_type=jnp.float32)
+            columns = []
+            for t in range(group // 2):
+                heads = []
+                for h in range(2):
+                    source = own if h == odd else turned
+                    row = t * two + h * head_dim
+                    heads.append(source[row : row + head_dim] * halves[h])
+                column = [zeros] * (group // 2)
+                column[t] = jnp.concatenate(heads, axis=0)
+                columns.append(jnp.concatenate(column, axis=0))
+            scores[p, g, odd] = jnp.dot(k, jnp.concatenate(columns, axis=1), preferred_element_type=jnp.float32)
     weights = {}
     for unit, s in scores.items():
         raised = jnp.exp2(s - jnp.max(s, axis=0, keepdims=True))
@@ -312,23 +315,18 @@
             v_halves = jnp.concatenate([v * m for m in halves], axis=0)
             mixed[p, g, t] = jnp.dot(
                 v_halves, both[:, t * 2 * size : (t + 1) * 2 * size], preferred_element_type=jnp.float32
-            ).astype(jnp.bfloat16)
-    parts = {}
-    for p, g in units:
-        own = [
-            mixed[p, g, t][odd * two + h * head_dim : odd * two + (h + 1) * head_dim] * halves[h]
-            for odd in range(2)
-            for t in range(group // 2)
-            for h in range(2)
-        ]
-        parts[p, g] = lax.dot_general(
-            pick, jnp.concatenate(own, axis=0), NT, preferred_element_type=jnp.float32
-        ).astype(jnp.bfloat16)
-    blended = [
-        jnp.concatenate([parts[p, g][:, odd * LANES : (odd + 1) * LANES] for g in range(groups)], axis=1)
-        for p in range(pairs)
-        for odd in range(2)
-    ]
+            )
+    even_head = lane // head_dim % 2 == 0
+    blended = []
+    for p in range(pairs):
+        for odd in range(2):
+            parts = []
+            for g in range(groups):
+                turned = jnp.concatenate(
+                    [mixed[p, g, t][odd * two : (odd + 1) * two] for t in range(group // 2)], axis=0
+                ).T
+                parts.append(jnp.where(even_head, turned[:size], turned[size:]).astype(jnp.bfloat16))
+            blended.append(jnp.concatenate(parts, axis=1))
     return x + jnp.dot(jnp.concatenate(blended, axis=0), wout_ref[...], preferred_element_type=jnp.float32)
 
 

time: 100 us -> 97.7 us (0.977)
  Pallas kernels: 24.5 us -> 22.1 us
    pallas_call x1, Pallas kernels: 14.5 us -> 13.2 us  [conv_and_windows(): pl.pallas_call(functools.partial(conv_kernel, conv_steps, (block_places,...]
    pallas_call x1, Pallas kernels: 7.44 us -> 6.32 us  [grid_attention(): pl.pallas_call(grid_kernel, grid=(windows // min(GROUP, windows),), out_s...]
where the time goes in v7:
time: 97.7 us; the launch traced here: 96.3 us
  blocking collectives  58.1 us (59%)
  Pallas kernels  22.1 us (23%)
  starting transfers between devices  10.3 us (11%)
  local copies, waits for them, and re-layouts  3.99 us (4%)
  other arithmetic  1.05 us (1%)
    all_to_all x2, blocking collectives, exchange(): return lax.all_to_all(x, ('ns', 'ew'), 0, 0, tiled=True)  58.1 us
    pallas_call x1, Pallas kernels, conv_and_windows(): pl.pallas_call(functools.partial(conv_kernel, conv_steps, (block_places,...  13.2 us
    ppermute x4, starting transfers between devices, swap(): lax.ppermute(jnp.where(lower, high_edge, low_edge), axis, pairs + [(targe...  10.3 us
    pallas_call x1, Pallas kernels, grid_attention(): pl.pallas_call(grid_kernel, grid=(windows // min(GROUP, windows),), out_s...  6.32 us
    unnamed x24, local copies, waits for them, and re-layouts  1.96 us
  transfers between devices with their start and end apart: 4, of which 1 were waited for; matrix products, arithmetic and copies ran while one was open for 1% of the time, Pallas kernels for 3%

profile of v7, /device:TPU:0, one launch (start us, length us, event | category | flops | bytes accessed | tf_op | source)
XLA Modules:
  0.0 96.3 jit_solution(18386784486507541814)
XLA Ops:
  0.0 1.0 %select_bitcast_fusion = (bf16[128,512]{1,0:T(8,128)(2,1)S(1)}, bf16[128,512]{1,0:T(8,128)(2,1)S(1)}) fusion(pred[]{:T(512)S(6)} %eq.14, bf16[8,128,512]{2,1,0:T(8,128)(2,1)} %x_ref.1, pred[]{:T(512)S(6)} %eq.13), kind=kLoop, calls=%fused_computation | loop fusion | flops 131072 | bytes 524290 | tf_op jit(solution)/shard_map/jit(_where)/select_n | solution.py:383
  1.0 0.7 collective-permute-start.1
  1.7 4.4 %collective-permute-start = (bf16[128,512]{1,0:T(8,128)(2,1)S(1)}, bf16[128,512]{1,0:T(8,128)(2,1)S(1)}, u32[]{:S(2)}, u32[]{:S(2)}) collective-permute-start(bf16[128,512]{1,0:T(8,128)(2,1)S(1)} %get-tuple-element.20), channel_id=1, source_target_pairs={{0,4},{8,12},{16,20},{24,28},{4,0},{12,8},{20,16},{28,24},{1,5},{9... | collective-permute-start | bytes 393224 | tf_op jit(solution)/shard_map/ppermute | solution.py:382
  6.0 0.9 fusion
  6.9 0.0 copy-start.1
  6.9 1.2 %copy-done.1 = bf16[8,128,512]{2,1,0:T(8,128)(2,1)S(1)} copy-done((bf16[8,128,512]{2,1,0:T(8,128)(2,1)S(1)}, bf16[8,128,512]{2,1,0:T(8,128)(2,1)}, u32[]{:S(2)}) %copy-start.1) | copy-done | bytes 1048600
  8.2 0.0 copy-start.2
  8.2 0.7 copy-done.2
  8.8 0.0 copy-start
  8.8 0.0 copy-start.3
  8.8 0.0 copy-start.5
  8.8 1.4 %norm_own.1 = (bf16[1024,512]{1,0:T(8,128)(2,1)S(1)}, bf16[1024,512]{1,0:T(8,128)(2,1)S(1)}) custom-call(bf16[8,128,512]{2,1,0:T(8,128)(2,1)S(1)} %copy-done.1, f32[1,512]{1,0:T(1,128)S(1)} %bitcast.21), custom_call_target="tpu_custom_call" | custom-call | flops 10000000000 | bytes 2097152 | tf_op jit(solution)/shard_map/norm_own/pallas_call | solution.py:70
  10.3 0.0 copy-start.4
  10.3 0.0 copy-start.7
  10.3 0.0 copy-start.9
  10.3 0.0 copy-start.10
  10.3 0.0 collective-permute-done.1.ns1_ref
  10.3 0.0 collective-permute-done.ns0_ref
  10.5 0.8 collective-permute-start.3
  11.3 4.5 %collective-permute-start.2 = (bf16[10,512]{1,0:T(8,128)(2,1)S(1)}, bf16[10,512]{1,0:T(8,128)(2,1)S(1)}, u32[]{:S(2)}, u32[]{:S(2)}) collective-permute-start(bf16[10,512]{1,0:T(8,128)(2,1)S(1)} %get-tuple-element.26), channel_id=1, source_target_pairs={{0,1},{2,3},{1,0},{3,2},{4,5},{6,7},{5,4},{7,6},{8,9},{10,11},{9,8... | collective-permute-start | bytes 30728 | tf_op jit(solution)/shard_map/ppermute | solution.py:382
  15.7 0.0 copy-done
  15.7 0.0 copy-done.3
  15.7 1.1 %expand_edges.1.edge_ref = bf16[2,8,16,2048]{3,2,1,0:T(8,128)(2,1)S(1)} custom-call(bf16[128,512]{1,0:T(8,128)(2,1)S(1)} %collective-permute-done.ns0_ref, bf16[128,512]{1,0:T(8,128)(2,1)S(1)} %collective-permute-done.1.ns1_ref, f32[1,512]{1,0:T(1,128)S(1)} %bitcast.22, bf16[512,2048]{1,0:T(8,128)(2,1)S(1)} %copy-done), custom_call_target="tpu_custom_call" | custom-call | flops 536870912 | bytes 3407872 | tf_op jit(solution)/shard_map/expand_edges/pallas_call | solution.py:105
  16.9 0.0 collective-permute-done.3.ew1_ref
  16.9 0.6 collective-permute-done.2.ew0_ref
  17.4 0.0 copy-done.5
  17.4 0.0 copy-done.4
  17.4 0.0 copy-done.7
  17.5 0.0 copy-done.9
  17.5 0.0 copy-done.10
  17.5 13.2 %conv_and_windows.1 = bf16[8,4,2,2,8,512]{5,4,3,2,1,0:T(8,128)(2,1)S(1)} custom-call(bf16[1024,512]{1,0:T(8,128)(2,1)S(1)} %get-tuple-element.13.x_ref, bf16[1024,512]{1,0:T(8,128)(2,1)S(1)} %get-tuple-element.14.own_ref, bf16[2,8,16,2048]{3,2,1,0:T(8,128)(2,1)S(1)} %expand_edges.1.edge_ref, bf16[10,512]{1,0:T(8,128)(2,1)S(1)} %collective-permute-done.2.ew0_ref, ...), custom_call_target="tpu_custom_call" | custom-call | flops 8589934592 | bytes 8388608 | tf_op jit(solution)/shard_map/conv_and_windows/pallas_call | solution.py:221
  30.7 0.0 copy-start.6
  30.7 0.0 copy-start.8
  30.7 0.0 copy-start.11
  30.7 28.8 %all_to_all.10 = bf16[32,32,512]{2,1,0:T(8,128)(2,1)S(1)} all-to-all(bf16[32,32,512]{2,1,0:T(8,128)(2,1)S(1)} %bitcast.18), channel_id=1, replica_groups=mesh['ns'=8,'ew'=4] {'ns','ew'}, dimensions={0} | all-to-all | bytes 2097152 | tf_op jit(solution)/shard_map/all_to_all | solution.py:401
  59.5 0.0 copy-done.6
  59.5 0.0 copy-done.8
  59.5 0.0 copy-done.11
  59.5 6.3 %grid_attention.1 = bf16[1024,512]{1,0:T(8,128)(2,1)S(1)} custom-call(bf16[1024,512]{1,0:T(8,128)(2,1)S(1)} %bitcast.19, f32[1,512]{1,0:T(1,128)S(1)} %bitcast.25, bf16[512,1536]{1,0:T(8,128)(2,1)S(1)} %copy-done.6, bf16[512,512]{1,0:T(8,128)(2,1)S(1)} %copy-done.8), custom_call_target="tpu_custom_call" | custom-call | flops 4294967296 | bytes 4194304 | tf_op jit(solution)/shard_map/grid_attention/pallas_call | solution.py:362
  65.8 29.3 %all_to_all.11 = bf16[32,32,512]{2,1,0:T(8,128)(2,1)S(1)} all-to-all(bf16[32,32,512]{2,1,0:T(8,128)(2,1)S(1)} %bitcast.20), channel_id=1, replica_groups=mesh['ns'=8,'ew'=4] {'ns','ew'}, dimensions={0} | all-to-all | bytes 2097152 | tf_op jit(solution)/shard_map/all_to_all | solution.py:401
  95.2 1.1 %copy.14 = bf16[8,4,2,2,8,512]{5,4,1,3,2,0:T(8,128)(2,1)} copy(bf16[8,4,2,2,8,512]{5,4,3,2,1,0:T(8,128)(2,1)S(1)} %bitcast.26) | data formatting | bytes 2097152 | tf_op jit(solution)/shard_map/reshape | solution.py:453
  (6 shorter events, 0.1 us)
Async XLA Ops:
  1.0 9.3 %collective-permute-start.1 = (bf16[128,512]{1,0:T(8,128)(2,1)S(1)}, bf16[128,512]{1,0:T(8,128)(2,1)S(1)}, u32[]{:S(2)}, u32[]{:S(2)}) collective-permute-start(bf16[128,512]{1,0:T(8,128)(2,1)S(1)} %get-tuple-element.19), channel_id=1, source_target_pairs={{4,8},{12,16},{20,24},{8,4},{16,12},{24,20},{5,9},{13,17},{21,25},... | collective-permute-start | bytes 393224 | tf_op jit(solution)/shard_map/ppermute | solution.py:382
  1.7 8.7 %collective-permute-start = (bf16[128,512]{1,0:T(8,128)(2,1)S(1)}, bf16[128,512]{1,0:T(8,128)(2,1)S(1)}, u32[]{:S(2)}, u32[]{:S(2)}) collective-permute-start(bf16[128,512]{1,0:T(8,128)(2,1)S(1)} %get-tuple-element.20), channel_id=1, source_target_pairs={{0,4},{8,12},{16,20},{24,28},{4,0},{12,8},{20,16},{28,24},{1,5},{9... | collective-permute-start | bytes 393224 | tf_op jit(solution)/shard_map/ppermute | solution.py:382
  6.9 1.2 %copy-start.1 = (bf16[8,128,512]{2,1,0:T(8,128)(2,1)S(1)}, bf16[8,128,512]{2,1,0:T(8,128)(2,1)}, u32[]{:S(2)}) copy-start(bf16[8,128,512]{2,1,0:T(8,128)(2,1)} %x_ref.1) | copy-start | bytes 3145732
  8.2 0.7 copy-start.2
  8.8 6.9 %copy-start = (bf16[512,2048]{1,0:T(8,128)(2,1)S(1)}, bf16[512,2048]{1,0:T(8,128)(2,1)}, u32[]{:S(2)}) copy-start(bf16[512,2048]{1,0:T(8,128)(2,1)} %w1_ref.3) | copy-start | bytes 6291460
  8.8 6.9 %copy-start.3 = (f32[512]{0:T(512)S(1)}, f32[512]{0:T(512)}, u32[]{:S(2)}) copy-start(f32[512]{0:T(512)} %param.12) | copy-start | bytes 6148
  8.8 8.6 %copy-start.5 = (bf16[512,1536]{1,0:T(8,128)(2,1)S(1)}, bf16[512,1536]{1,0:T(8,128)(2,1)}, u32[]{:S(2)}) copy-start(bf16[512,1536]{1,0:T(8,128)(2,1)} %wqkv_ref.2) | copy-start | bytes 4718596
  10.3 7.2 %copy-start.4 = (bf16[2048,512]{1,0:T(8,128)(2,1)S(1)}, bf16[2048,512]{1,0:T(8,128)(2,1)}, u32[]{:S(2)}) copy-start(bf16[2048,512]{1,0:T(8,128)(2,1)} %w2_ref.1) | copy-start | bytes 6291460
  10.3 7.2 %copy-start.7 = (bf16[512,512]{1,0:T(8,128)(2,1)S(1)}, bf16[512,512]{1,0:T(8,128)(2,1)}, u32[]{:S(2)}) copy-start(bf16[512,512]{1,0:T(8,128)(2,1)} %wout_ref.2) | copy-start | bytes 1572868
  10.3 7.2 %copy-start.9 = (f32[3,3,2048]{2,1,0:T(4,128)S(1)}, f32[3,3,2048]{2,1,0:T(4,128)}, u32[]{:S(2)}) copy-start(f32[3,3,2048]{2,1,0:T(4,128)} %dw_ref.1) | copy-start | bytes 221188
  10.3 7.2 %copy-start.10 = (f32[512]{0:T(512)S(1)}, f32[512]{0:T(512)}, u32[]{:S(2)}) copy-start(f32[512]{0:T(512)} %param.16) | copy-start | bytes 6148
  10.5 6.4 %collective-permute-start.3 = (bf16[10,512]{1,0:T(8,128)(2,1)S(1)}, bf16[10,512]{1,0:T(8,128)(2,1)S(1)}, u32[]{:S(2)}, u32[]{:S(2)}) collective-permute-start(bf16[10,512]{1,0:T(8,128)(2,1)S(1)} %get-tuple-element.25), channel_id=1, source_target_pairs={{1,2},{2,1},{5,6},{6,5},{9,10},{10,9},{13,14},{14,13},{17,18},{18,... | collective-permute-start | bytes 30728 | tf_op jit(solution)/shard_map/ppermute | solution.py:382
  11.3 6.2 %collective-permute-start.2 = (bf16[10,512]{1,0:T(8,128)(2,1)S(1)}, bf16[10,512]{1,0:T(8,128)(2,1)S(1)}, u32[]{:S(2)}, u32[]{:S(2)}) collective-permute-start(bf16[10,512]{1,0:T(8,128)(2,1)S(1)} %get-tuple-element.26), channel_id=1, source_target_pairs={{0,1},{2,3},{1,0},{3,2},{4,5},{6,7},{5,4},{7,6},{8,9},{10,11},{9,8... | collective-permute-start | bytes 30728 | tf_op jit(solution)/shard_map/ppermute | solution.py:382
  30.7 28.8 %copy-start.6 = (bf16[512,1536]{1,0:T(8,128)(2,1)S(1)}, bf16[512,1536]{1,0:T(8,128)(2,1)}, u32[]{:S(2)}) copy-start(bf16[512,1536]{1,0:T(8,128)(2,1)} %wqkv_ref.3) | copy-start | bytes 4718596
  30.7 28.8 %copy-start.8 = (bf16[512,512]{1,0:T(8,128)(2,1)S(1)}, bf16[512,512]{1,0:T(8,128)(2,1)}, u32[]{:S(2)}) copy-start(bf16[512,512]{1,0:T(8,128)(2,1)} %wout_ref.3) | copy-start | bytes 1572868
  30.7 28.8 %copy-start.11 = (f32[512]{0:T(512)S(1)}, f32[512]{0:T(512)}, u32[]{:S(2)}) copy-start(f32[512]{0:T(512)} %param.19) | copy-start | bytes 6148

commit v8 on v7

--- a/solution.py
+++ b/solution.py
@@ -28,9 +28,9 @@
     return center * lax.rsqrt(spread + 1e-05) * scale_gain
 
 
-def gelu(v):
-    inner = v * (math.sqrt(2 / math.pi) + (math.sqrt(2 / math.pi) * 0.044715) * (v * v))
-    half = 0.5 * v
+def gelu_of_double(half):
+    root = math.sqrt(2 / math.pi)
+    inner = half * (2 * root + (8 * root * 0.044715) * (half * half))
     return half + half * jnp.tanh(inner)
 
 
@@ -46,14 +46,14 @@
     cols = block.shape[0]
     strips = cols // WINDOW
     for t, part in enumerate(tiles(block)):
-        tmp_ref[t] = part
+        tmp_ref[t, :cols] = part
     for b in range(WINDOW):
         store(b * strips, strips, strided(tmp_ref, b, strips, WINDOW))
 
 
 def norm_kernel(x_ref, gain_ref, normed_ref, moved_ref, tmp_ref):
     rows, cols, _ = x_ref.shape
-    gain = gain_ref[...]
+    gain = 0.5 * gain_ref[...]
     for i in range(rows):
 
         block = x_ref[i].astype(jnp.float32)
@@ -70,7 +70,7 @@
     return pl.pallas_call(
         norm_kernel,
         out_shape=[jax.ShapeDtypeStruct((rows * cols, channels), jnp.bfloat16)] * 2,
-        scratch_shapes=[pltpu.VMEM((channels // LANES, cols, LANES), jnp.float32)],
+        scratch_shapes=[pltpu.VMEM((channels // LANES, cols + WINDOW, LANES), jnp.float32)],
         compiler_params=pltpu.CompilerParams(vmem_limit_bytes=NORM_LIMIT * MIB),
         cost_estimate=pl.CostEstimate(flops=NORM_COST, bytes_accessed=4 * rows * cols * channels, transcendentals=0),
         name="norm_own",
@@ -85,7 +85,7 @@
 
 def edge_kernel(ns0_ref, ns1_ref, gain_ref, w1_ref, out_ref, n_ref, tmp_ref):
     cols = ns0_ref.shape[0]
-    gain = gain_ref[...]
+    gain = 0.5 * gain_ref[...]
     for k, block in enumerate(sorted_pair(ns0_ref, ns1_ref, "ns")):
 
         def store(at, count, part):
@@ -95,7 +95,7 @@
     for k in range(2):
         normed = n_ref[k * cols : (k + 1) * cols, :]
         hidden = jnp.dot(normed, w1_ref[...], preferred_element_type=jnp.float32)
-        out_ref[k] = gelu(hidden.astype(jnp.bfloat16)).reshape(out_ref.shape[1:])
+        out_ref[k] = gelu_of_double(hidden.astype(jnp.bfloat16)).reshape(out_ref.shape[1:])
 
 
 def expand_edges(ns0, ns1, gain, w_expand):
@@ -109,7 +109,7 @@
         out_specs=vmem,
         scratch_shapes=[
             pltpu.VMEM((2 * cols, channels), jnp.bfloat16),
-            pltpu.VMEM((channels // LANES, cols, LANES), jnp.float32),
+            pltpu.VMEM((channels // LANES, cols + WINDOW, LANES), jnp.float32),
         ],
         compiler_params=pltpu.CompilerParams(vmem_limit_bytes=EDGE_LIMIT * MIB),
         cost_estimate=pl.CostEstimate(
@@ -136,7 +136,7 @@
 
     @pl.when(step == 0)
     def _():
-        gain = gain_ref[...]
+        gain = 0.5 * gain_ref[...]
 
         pad = jnp.zeros((side_count - side_rows, channels), jnp.float32)
         for k, block in enumerate(sorted_pair(ew0_ref, ew1_ref, "ew")):
@@ -145,17 +145,17 @@
                 jnp.concatenate([block, pad], axis=0), gain
             ).astype(jnp.bfloat16)
         for t in range(channels // LANES):
-            acc_ref[t] = x_ref[:, t * LANES : (t + 1) * LANES].astype(jnp.float32)
+            acc_ref[t, :tokens] = x_ref[:, t * LANES : (t + 1) * LANES].astype(jnp.float32)
 
     @pl.when(step < conv_steps)
     def _():
         block = pl.ds(pl.multiple_of(step * features, features), features)
         w1 = w1_ref[:, block]
         w2 = w2_ref[block, :]
-        taps = [[dw_ref[a, b : b + 1, :].astype(jnp.bfloat16) for b in range(3)] for a in range(3)]
+        taps = [[(0.5 * dw_ref[a, b : b + 1, :]).astype(jnp.bfloat16) for b in range(3)] for a in range(3)]
 
         def hidden(normed):
-            return gelu(jnp.dot(normed, w1, preferred_element_type=jnp.float32).astype(jnp.bfloat16))
+            return gelu_of_double(jnp.dot(normed, w1, preferred_element_type=jnp.float32).astype(jnp.bfloat16))
 
         sides = hidden(n_ref[...]).astype(jnp.float32)
         place_in_strip = lax.broadcasted_iota(jnp.int32, (strips, features), 0)
@@ -178,7 +178,7 @@
                 for da in range(3):
                     t = [e_ref[i + da, b + db] * taps[da][db] for db in range(3)]
                     sums.append(t[0] + t[1] + t[2])
-                pieces.append(gelu(sums[0] + sums[1] + sums[2]))
+                pieces.append(gelu_of_double(sums[0] + sums[1] + sums[2]))
             active = jnp.concatenate(pieces, axis=0)
             for t, part in enumerate(tiles(jnp.dot(active, w2, preferred_element_type=jnp.float32))):
                 acc_ref[t, i * cols : (i + 1) * cols, :] += part
@@ -236,7 +236,7 @@
         scratch_shapes=[
             pltpu.VMEM((2 * side_count, channels), jnp.bfloat16),
             pltpu.VMEM((rows + 2, WINDOW + 2, strips, features), jnp.bfloat16),
-            pltpu.VMEM((channels // LANES, tokens, LANES), jnp.float32),
+            pltpu.VMEM((channels // LANES, tokens + strips, LANES), jnp.float32),
         ],
         compiler_params=pltpu.CompilerParams(dimension_semantics=("arbitrary",), vmem_limit_bytes=CONV_LIMIT * MIB),
         cost_estimate=pl.CostEstimate(
@@ -340,7 +340,7 @@
     @pl.when(step == 0)
     def _():
         for t, part in enumerate(tiles(x_ref[...])):
-            floats_ref[t] = part.astype(jnp.float32)
+            floats_ref[t, :tokens] = part.astype(jnp.float32)
 
     first = step * block
     x = jnp.concatenate([strided(floats_ref, first + w, size, windows) for w in range(block)], axis=0)
@@ -352,7 +352,7 @@
     @pl.when(step == pl.num_programs(0) - 1)
     def _():
         for t in range(floats_ref.shape[0]):
-            out_ref[:, t * LANES : (t + 1) * LANES] = floats_ref[t].astype(jnp.bfloat16)
+            out_ref[:, t * LANES : (t + 1) * LANES] = floats_ref[t, :tokens].astype(jnp.bfloat16)
 
 
 def grid_attention(x, gain, w_qkv, w_out):
@@ -365,7 +365,7 @@
         out_shape=jax.ShapeDtypeStruct((tokens, channels), jnp.bfloat16),
         in_specs=[vmem] * 4,
         out_specs=vmem,
-        scratch_shapes=[pltpu.VMEM((channels // LANES, tokens, LANES), jnp.float32)],
+        scratch_shapes=[pltpu.VMEM((channels // LANES, tokens + windows, LANES), jnp.float32)],
         compiler_params=pltpu.CompilerParams(dimension_semantics=("arbitrary",), vmem_limit_bytes=24 * MIB),
         cost_estimate=pl.CostEstimate(
             flops=16 * tokens * channels * channels,

time: 97.7 us -> 97.5 us (level)
  no operation moved by 1% of the time
where the time goes in v8:
time: 97.5 us; the launch traced here: 96.1 us
  blocking collectives  58.1 us (60%)
  Pallas kernels  21.9 us (22%)
  starting transfers between devices  10.3 us (11%)
  local copies, waits for them, and re-layouts  3.99 us (4%)
  other arithmetic  1.05 us (1%)
    all_to_all x2, blocking collectives, exchange(): return lax.all_to_all(x, ('ns', 'ew'), 0, 0, tiled=True)  58.1 us
    pallas_call x1, Pallas kernels, conv_and_windows(): pl.pallas_call(functools.partial(conv_kernel, conv_steps, (block_places,...  13.1 us
    ppermute x4, starting transfers between devices, swap(): lax.ppermute(jnp.where(lower, high_edge, low_edge), axis, pairs + [(targe...  10.3 us
    pallas_call x1, Pallas kernels, grid_attention(): pl.pallas_call(grid_kernel, grid=(windows // min(GROUP, windows),), out_s...  6.33 us
    unnamed x24, local copies, waits for them, and re-layouts  1.96 us
  transfers between devices with their start and end apart: 4, of which 1 were waited for; matrix products, arithmetic and copies ran while one was open for 1% of the time, Pallas kernels for 3%

profile of v8, /device:TPU:0, one launch (start us, length us, event | category | flops | bytes accessed | tf_op | source)
XLA Modules:
  0.0 96.1 jit_solution(7751465910385209546)
XLA Ops:
  0.0 1.0 %select_bitcast_fusion = (bf16[128,512]{1,0:T(8,128)(2,1)S(1)}, bf16[128,512]{1,0:T(8,128)(2,1)S(1)}) fusion(pred[]{:T(512)S(6)} %eq.14, bf16[8,128,512]{2,1,0:T(8,128)(2,1)} %x_ref.1, pred[]{:T(512)S(6)} %eq.13), kind=kLoop, calls=%fused_computation | loop fusion | flops 131072 | bytes 524290 | tf_op jit(solution)/shard_map/jit(_where)/select_n | solution.py:383
  1.0 0.7 collective-permute-start.1
  1.7 4.4 %collective-permute-start = (bf16[128,512]{1,0:T(8,128)(2,1)S(1)}, bf16[128,512]{1,0:T(8,128)(2,1)S(1)}, u32[]{:S(2)}, u32[]{:S(2)}) collective-permute-start(bf16[128,512]{1,0:T(8,128)(2,1)S(1)} %get-tuple-element.20), channel_id=1, source_target_pairs={{0,4},{8,12},{16,20},{24,28},{4,0},{12,8},{20,16},{28,24},{1,5},{9... | collective-permute-start | bytes 393224 | tf_op jit(solution)/shard_map/ppermute | solution.py:382
  6.0 0.9 fusion
  6.9 0.0 copy-start.1
  6.9 1.2 %copy-done.1 = bf16[8,128,512]{2,1,0:T(8,128)(2,1)S(1)} copy-done((bf16[8,128,512]{2,1,0:T(8,128)(2,1)S(1)}, bf16[8,128,512]{2,1,0:T(8,128)(2,1)}, u32[]{:S(2)}) %copy-start.1) | copy-done | bytes 1048600
  8.2 0.0 copy-start.2
  8.2 0.7 copy-done.2
  8.8 0.0 copy-start
  8.8 0.0 copy-start.3
  8.8 0.0 copy-start.5
  8.8 1.4 %norm_own.1 = (bf16[1024,512]{1,0:T(8,128)(2,1)S(1)}, bf16[1024,512]{1,0:T(8,128)(2,1)S(1)}) custom-call(bf16[8,128,512]{2,1,0:T(8,128)(2,1)S(1)} %copy-done.1, f32[1,512]{1,0:T(1,128)S(1)} %bitcast.21), custom_call_target="tpu_custom_call" | custom-call | flops 10000000000 | bytes 2097152 | tf_op jit(solution)/shard_map/norm_own/pallas_call | solution.py:70
  10.2 0.0 copy-start.4
  10.3 0.0 copy-start.7
  10.3 0.0 copy-start.9
  10.3 0.0 copy-start.10
  10.3 0.0 collective-permute-done.1.ns1_ref
  10.3 0.0 collective-permute-done.ns0_ref
  10.4 0.8 collective-permute-start.3
  11.2 4.5 %collective-permute-start.2 = (bf16[10,512]{1,0:T(8,128)(2,1)S(1)}, bf16[10,512]{1,0:T(8,128)(2,1)S(1)}, u32[]{:S(2)}, u32[]{:S(2)}) collective-permute-start(bf16[10,512]{1,0:T(8,128)(2,1)S(1)} %get-tuple-element.26), channel_id=1, source_target_pairs={{0,1},{2,3},{1,0},{3,2},{4,5},{6,7},{5,4},{7,6},{8,9},{10,11},{9,8... | collective-permute-start | bytes 30728 | tf_op jit(solution)/shard_map/ppermute | solution.py:382
  15.7 0.0 copy-done
  15.7 0.0 copy-done.3
  15.7 1.1 %expand_edges.1.edge_ref = bf16[2,8,16,2048]{3,2,1,0:T(8,128)(2,1)S(1)} custom-call(bf16[128,512]{1,0:T(8,128)(2,1)S(1)} %collective-permute-done.ns0_ref, bf16[128,512]{1,0:T(8,128)(2,1)S(1)} %collective-permute-done.1.ns1_ref, f32[1,512]{1,0:T(1,128)S(1)} %bitcast.22, bf16[512,2048]{1,0:T(8,128)(2,1)S(1)} %copy-done), custom_call_target="tpu_custom_call" | custom-call | flops 536870912 | bytes 3407872 | tf_op jit(solution)/shard_map/expand_edges/pallas_call | solution.py:105
  16.8 0.0 collective-permute-done.3.ew1_ref
  16.8 0.6 collective-permute-done.2.ew0_ref
  17.4 0.0 copy-done.5
  17.4 0.0 copy-done.4
  17.4 0.0 copy-done.7
  17.4 0.0 copy-done.9
  17.4 0.0 copy-done.10
  17.5 13.1 %conv_and_windows.1 = bf16[8,4,2,2,8,512]{5,4,3,2,1,0:T(8,128)(2,1)S(1)} custom-call(bf16[1024,512]{1,0:T(8,128)(2,1)S(1)} %get-tuple-element.13.x_ref, bf16[1024,512]{1,0:T(8,128)(2,1)S(1)} %get-tuple-element.14.own_ref, bf16[2,8,16,2048]{3,2,1,0:T(8,128)(2,1)S(1)} %expand_edges.1.edge_ref, bf16[10,512]{1,0:T(8,128)(2,1)S(1)} %collective-permute-done.2.ew0_ref, ...), custom_call_target="tpu_custom_call" | custom-call | flops 8589934592 | bytes 8388608 | tf_op jit(solution)/shard_map/conv_and_windows/pallas_call | solution.py:221
  30.6 0.0 copy-start.6
  30.6 0.0 copy-start.8
  30.6 0.0 copy-start.11
  30.6 28.7 %all_to_all.10 = bf16[32,32,512]{2,1,0:T(8,128)(2,1)S(1)} all-to-all(bf16[32,32,512]{2,1,0:T(8,128)(2,1)S(1)} %bitcast.18), channel_id=1, replica_groups=mesh['ns'=8,'ew'=4] {'ns','ew'}, dimensions={0} | all-to-all | bytes 2097152 | tf_op jit(solution)/shard_map/all_to_all | solution.py:401
  59.4 0.0 copy-done.6
  59.4 0.0 copy-done.8
  59.4 0.0 copy-done.11
  59.4 6.3 %grid_attention.1 = bf16[1024,512]{1,0:T(8,128)(2,1)S(1)} custom-call(bf16[1024,512]{1,0:T(8,128)(2,1)S(1)} %bitcast.19, f32[1,512]{1,0:T(1,128)S(1)} %bitcast.25, bf16[512,1536]{1,0:T(8,128)(2,1)S(1)} %copy-done.6, bf16[512,512]{1,0:T(8,128)(2,1)S(1)} %copy-done.8), custom_call_target="tpu_custom_call" | custom-call | flops 4294967296 | bytes 4194304 | tf_op jit(solution)/shard_map/grid_attention/pallas_call | solution.py:362
  65.7 29.3 %all_to_all.11 = bf16[32,32,512]{2,1,0:T(8,128)(2,1)S(1)} all-to-all(bf16[32,32,512]{2,1,0:T(8,128)(2,1)S(1)} %bitcast.20), channel_id=1, replica_groups=mesh['ns'=8,'ew'=4] {'ns','ew'}, dimensions={0} | all-to-all | bytes 2097152 | tf_op jit(solution)/shard_map/all_to_all | solution.py:401
  95.0 1.1 %copy.14 = bf16[8,4,2,2,8,512]{5,4,1,3,2,0:T(8,128)(2,1)} copy(bf16[8,4,2,2,8,512]{5,4,3,2,1,0:T(8,128)(2,1)S(1)} %bitcast.26) | data formatting | bytes 2097152 | tf_op jit(solution)/shard_map/reshape | solution.py:453
  (6 shorter events, 0.1 us)
Async XLA Ops:
  1.0 9.3 %collective-permute-start.1 = (bf16[128,512]{1,0:T(8,128)(2,1)S(1)}, bf16[128,512]{1,0:T(8,128)(2,1)S(1)}, u32[]{:S(2)}, u32[]{:S(2)}) collective-permute-start(bf16[128,512]{1,0:T(8,128)(2,1)S(1)} %get-tuple-element.19), channel_id=1, source_target_pairs={{4,8},{12,16},{20,24},{8,4},{16,12},{24,20},{5,9},{13,17},{21,25},... | collective-permute-start | bytes 393224 | tf_op jit(solution)/shard_map/ppermute | solution.py:382
  1.7 8.7 %collective-permute-start = (bf16[128,512]{1,0:T(8,128)(2,1)S(1)}, bf16[128,512]{1,0:T(8,128)(2,1)S(1)}, u32[]{:S(2)}, u32[]{:S(2)}) collective-permute-start(bf16[128,512]{1,0:T(8,128)(2,1)S(1)} %get-tuple-element.20), channel_id=1, source_target_pairs={{0,4},{8,12},{16,20},{24,28},{4,0},{12,8},{20,16},{28,24},{1,5},{9... | collective-permute-start | bytes 393224 | tf_op jit(solution)/shard_map/ppermute | solution.py:382
  6.9 1.2 %copy-start.1 = (bf16[8,128,512]{2,1,0:T(8,128)(2,1)S(1)}, bf16[8,128,512]{2,1,0:T(8,128)(2,1)}, u32[]{:S(2)}) copy-start(bf16[8,128,512]{2,1,0:T(8,128)(2,1)} %x_ref.1) | copy-start | bytes 3145732
  8.2 0.7 copy-start.2
  8.8 6.9 %copy-start = (bf16[512,2048]{1,0:T(8,128)(2,1)S(1)}, bf16[512,2048]{1,0:T(8,128)(2,1)}, u32[]{:S(2)}) copy-start(bf16[512,2048]{1,0:T(8,128)(2,1)} %w1_ref.3) | copy-start | bytes 6291460
  8.8 6.9 %copy-start.3 = (f32[512]{0:T(512)S(1)}, f32[512]{0:T(512)}, u32[]{:S(2)}) copy-start(f32[512]{0:T(512)} %param.12) | copy-start | bytes 6148
  8.8 8.6 %copy-start.5 = (bf16[512,1536]{1,0:T(8,128)(2,1)S(1)}, bf16[512,1536]{1,0:T(8,128)(2,1)}, u32[]{:S(2)}) copy-start(bf16[512,1536]{1,0:T(8,128)(2,1)} %wqkv_ref.2) | copy-start | bytes 4718596
  10.2 7.2 %copy-start.4 = (bf16[2048,512]{1,0:T(8,128)(2,1)S(1)}, bf16[2048,512]{1,0:T(8,128)(2,1)}, u32[]{:S(2)}) copy-start(bf16[2048,512]{1,0:T(8,128)(2,1)} %w2_ref.1) | copy-start | bytes 6291460
  10.3 7.2 %copy-start.7 = (bf16[512,512]{1,0:T(8,128)(2,1)S(1)}, bf16[512,512]{1,0:T(8,128)(2,1)}, u32[]{:S(2)}) copy-start(bf16[512,512]{1,0:T(8,128)(2,1)} %wout_ref.2) | copy-start | bytes 1572868
  10.3 7.2 %copy-start.9 = (f32[3,3,2048]{2,1,0:T(4,128)S(1)}, f32[3,3,2048]{2,1,0:T(4,128)}, u32[]{:S(2)}) copy-start(f32[3,3,2048]{2,1,0:T(4,128)} %dw_ref.1) | copy-start | bytes 221188
  10.3 7.2 %copy-start.10 = (f32[512]{0:T(512)S(1)}, f32[512]{0:T(512)}, u32[]{:S(2)}) copy-start(f32[512]{0:T(512)} %param.16) | copy-start | bytes 6148
  10.4 6.4 %collective-permute-start.3 = (bf16[10,512]{1,0:T(8,128)(2,1)S(1)}, bf16[10,512]{1,0:T(8,128)(2,1)S(1)}, u32[]{:S(2)}, u32[]{:S(2)}) collective-permute-start(bf16[10,512]{1,0:T(8,128)(2,1)S(1)} %get-tuple-element.25), channel_id=1, source_target_pairs={{1,2},{2,1},{5,6},{6,5},{9,10},{10,9},{13,14},{14,13},{17,18},{18,... | collective-permute-start | bytes 30728 | tf_op jit(solution)/shard_map/ppermute | solution.py:382
  11.2 6.2 %collective-permute-start.2 = (bf16[10,512]{1,0:T(8,128)(2,1)S(1)}, bf16[10,512]{1,0:T(8,128)(2,1)S(1)}, u32[]{:S(2)}, u32[]{:S(2)}) collective-permute-start(bf16[10,512]{1,0:T(8,128)(2,1)S(1)} %get-tuple-element.26), channel_id=1, source_target_pairs={{0,1},{2,3},{1,0},{3,2},{4,5},{6,7},{5,4},{7,6},{8,9},{10,11},{9,8... | collective-permute-start | bytes 30728 | tf_op jit(solution)/shard_map/ppermute | solution.py:382
  30.6 28.8 %copy-start.6 = (bf16[512,1536]{1,0:T(8,128)(2,1)S(1)}, bf16[512,1536]{1,0:T(8,128)(2,1)}, u32[]{:S(2)}) copy-start(bf16[512,1536]{1,0:T(8,128)(2,1)} %wqkv_ref.3) | copy-start | bytes 4718596
  30.6 28.8 %copy-start.8 = (bf16[512,512]{1,0:T(8,128)(2,1)S(1)}, bf16[512,512]{1,0:T(8,128)(2,1)}, u32[]{:S(2)}) copy-start(bf16[512,512]{1,0:T(8,128)(2,1)} %wout_ref.3) | copy-start | bytes 1572868
  30.6 28.8 %copy-start.11 = (f32[512]{0:T(512)S(1)}, f32[512]{0:T(512)}, u32[]{:S(2)}) copy-start(f32[512]{0:T(512)} %param.19) | copy-start | bytes 6148

commit v9 on v8

--- a/solution.py
+++ b/solution.py
@@ -144,8 +144,9 @@
             n_ref[start : start + side_count, :] = normalize(
                 jnp.concatenate([block, pad], axis=0), gain
             ).astype(jnp.bfloat16)
-        for t in range(channels // LANES):
-            acc_ref[t, :tokens] = x_ref[:, t * LANES : (t + 1) * LANES].astype(jnp.float32)
+        if conv_steps > 1:
+            for t in range(channels // LANES):
+                acc_ref[t, :tokens] = x_ref[:, t * LANES : (t + 1) * LANES].astype(jnp.float32)
 
     @pl.when(step < conv_steps)
     def _():
@@ -181,7 +182,13 @@
                 pieces.append(gelu_of_double(sums[0] + sums[1] + sums[2]))
             active = jnp.concatenate(pieces, axis=0)
             for t, part in enumerate(tiles(jnp.dot(active, w2, preferred_element_type=jnp.float32))):
-                acc_ref[t, i * cols : (i + 1) * cols, :] += part
+                own_rows = slice(i * cols, (i + 1) * cols)
+                if conv_steps > 1:
+                    acc_ref[t, own_rows, :] += part
+                else:
+                    acc_ref[t, own_rows, :] = (
+                        x_ref[own_rows, t * LANES : (t + 1) * LANES].astype(jnp.float32) + part
+                    )
 
     @pl.when(step >= conv_steps)
     def _():

time: 97.5 us -> 97.5 us (level)
  no operation moved by 1% of the time
where the time goes in v9:
time: 97.5 us; the launch traced here: 96.2 us
  blocking collectives  58.1 us (60%)
  Pallas kernels  21.9 us (22%)
  starting transfers between devices  10.3 us (11%)
  local copies, waits for them, and re-layouts  3.99 us (4%)
  other arithmetic  1.05 us (1%)
    all_to_all x2, blocking collectives, exchange(): return lax.all_to_all(x, ('ns', 'ew'), 0, 0, tiled=True)  58.1 us
    pallas_call x1, Pallas kernels, conv_and_windows(): pl.pallas_call(functools.partial(conv_kernel, conv_steps, (block_places,...  13.1 us
    ppermute x4, starting transfers between devices, swap(): lax.ppermute(jnp.where(lower, high_edge, low_edge), axis, pairs + [(targe...  10.3 us
    pallas_call x1, Pallas kernels, grid_attention(): pl.pallas_call(grid_kernel, grid=(windows // min(GROUP, windows),), out_s...  6.33 us
    unnamed x24, local copies, waits for them, and re-layouts  1.96 us
  transfers between devices with their start and end apart: 4, of which 1 were waited for; matrix products, arithmetic and copies ran while one was open for 1% of the time, Pallas kernels for 3%

profile of v9, /device:TPU:0, one launch (start us, length us, event | category | flops | bytes accessed | tf_op | source)
XLA Modules:
  0.0 96.2 jit_solution(13123357103372752350)
XLA Ops:
  0.0 1.0 %select_bitcast_fusion = (bf16[128,512]{1,0:T(8,128)(2,1)S(1)}, bf16[128,512]{1,0:T(8,128)(2,1)S(1)}) fusion(pred[]{:T(512)S(6)} %eq.14, bf16[8,128,512]{2,1,0:T(8,128)(2,1)} %x_ref.1, pred[]{:T(512)S(6)} %eq.13), kind=kLoop, calls=%fused_computation | loop fusion | flops 131072 | bytes 524290 | tf_op jit(solution)/shard_map/jit(_where)/select_n | solution.py:390
  1.0 0.7 collective-permute-start.1
  1.7 4.4 %collective-permute-start = (bf16[128,512]{1,0:T(8,128)(2,1)S(1)}, bf16[128,512]{1,0:T(8,128)(2,1)S(1)}, u32[]{:S(2)}, u32[]{:S(2)}) collective-permute-start(bf16[128,512]{1,0:T(8,128)(2,1)S(1)} %get-tuple-element.20), channel_id=1, source_target_pairs={{0,4},{8,12},{16,20},{24,28},{4,0},{12,8},{20,16},{28,24},{1,5},{9... | collective-permute-start | bytes 393224 | tf_op jit(solution)/shard_map/ppermute | solution.py:389
  6.0 0.9 fusion
  6.9 0.0 copy-start.1
  6.9 1.2 %copy-done.1 = bf16[8,128,512]{2,1,0:T(8,128)(2,1)S(1)} copy-done((bf16[8,128,512]{2,1,0:T(8,128)(2,1)S(1)}, bf16[8,128,512]{2,1,0:T(8,128)(2,1)}, u32[]{:S(2)}) %copy-start.1) | copy-done | bytes 1048600
  8.2 0.0 copy-start.2
  8.2 0.7 copy-done.2
  8.8 0.0 copy-start
  8.8 0.0 copy-start.3
  8.8 0.0 copy-start.5
  8.8 1.4 %norm_own.1 = (bf16[1024,512]{1,0:T(8,128)(2,1)S(1)}, bf16[1024,512]{1,0:T(8,128)(2,1)S(1)}) custom-call(bf16[8,128,512]{2,1,0:T(8,128)(2,1)S(1)} %copy-done.1, f32[1,512]{1,0:T(1,128)S(1)} %bitcast.21), custom_call_target="tpu_custom_call" | custom-call | flops 10000000000 | bytes 2097152 | tf_op jit(solution)/shard_map/norm_own/pallas_call | solution.py:70
  10.2 0.0 copy-start.4
  10.3 0.0 copy-start.7
  10.3 0.0 copy-start.9
  10.3 0.0 copy-start.10
  10.3 0.0 collective-permute-done.1.ns1_ref
  10.3 0.0 collective-permute-done.ns0_ref
  10.4 0.8 collective-permute-start.3
  11.2 4.5 %collective-permute-start.2 = (bf16[10,512]{1,0:T(8,128)(2,1)S(1)}, bf16[10,512]{1,0:T(8,128)(2,1)S(1)}, u32[]{:S(2)}, u32[]{:S(2)}) collective-permute-start(bf16[10,512]{1,0:T(8,128)(2,1)S(1)} %get-tuple-element.26), channel_id=1, source_target_pairs={{0,1},{2,3},{1,0},{3,2},{4,5},{6,7},{5,4},{7,6},{8,9},{10,11},{9,8... | collective-permute-start | bytes 30728 | tf_op jit(solution)/shard_map/ppermute | solution.py:389
  15.7 0.0 copy-done
  15.7 0.0 copy-done.3
  15.7 1.1 %expand_edges.1.edge_ref = bf16[2,8,16,2048]{3,2,1,0:T(8,128)(2,1)S(1)} custom-call(bf16[128,512]{1,0:T(8,128)(2,1)S(1)} %collective-permute-done.ns0_ref, bf16[128,512]{1,0:T(8,128)(2,1)S(1)} %collective-permute-done.1.ns1_ref, f32[1,512]{1,0:T(1,128)S(1)} %bitcast.22, bf16[512,2048]{1,0:T(8,128)(2,1)S(1)} %copy-done), custom_call_target="tpu_custom_call" | custom-call | flops 536870912 | bytes 3407872 | tf_op jit(solution)/shard_map/expand_edges/pallas_call | solution.py:105
  16.8 0.0 collective-permute-done.3.ew1_ref
  16.8 0.6 collective-permute-done.2.ew0_ref
  17.4 0.0 copy-done.5
  17.4 0.0 copy-done.4
  17.4 0.0 copy-done.7
  17.4 0.0 copy-done.9
  17.4 0.0 copy-done.10
  17.5 13.1 %conv_and_windows.1 = bf16[8,4,2,2,8,512]{5,4,3,2,1,0:T(8,128)(2,1)S(1)} custom-call(bf16[1024,512]{1,0:T(8,128)(2,1)S(1)} %get-tuple-element.13.x_ref, bf16[1024,512]{1,0:T(8,128)(2,1)S(1)} %get-tuple-element.14.own_ref, bf16[2,8,16,2048]{3,2,1,0:T(8,128)(2,1)S(1)} %expand_edges.1.edge_ref, bf16[10,512]{1,0:T(8,128)(2,1)S(1)} %collective-permute-done.2.ew0_ref, ...), custom_call_target="tpu_custom_call" | custom-call | flops 8589934592 | bytes 8388608 | tf_op jit(solution)/shard_map/conv_and_windows/pallas_call | solution.py:228
  30.6 0.0 copy-start.6
  30.6 0.0 copy-start.8
  30.6 0.0 copy-start.11
  30.6 28.8 %all_to_all.10 = bf16[32,32,512]{2,1,0:T(8,128)(2,1)S(1)} all-to-all(bf16[32,32,512]{2,1,0:T(8,128)(2,1)S(1)} %bitcast.18), channel_id=1, replica_groups=mesh['ns'=8,'ew'=4] {'ns','ew'}, dimensions={0} | all-to-all | bytes 2097152 | tf_op jit(solution)/shard_map/all_to_all | solution.py:408
  59.4 0.0 copy-done.6
  59.4 0.0 copy-done.8
  59.4 0.0 copy-done.11
  59.4 6.3 %grid_attention.1 = bf16[1024,512]{1,0:T(8,128)(2,1)S(1)} custom-call(bf16[1024,512]{1,0:T(8,128)(2,1)S(1)} %bitcast.19, f32[1,512]{1,0:T(1,128)S(1)} %bitcast.25, bf16[512,1536]{1,0:T(8,128)(2,1)S(1)} %copy-done.6, bf16[512,512]{1,0:T(8,128)(2,1)S(1)} %copy-done.8), custom_call_target="tpu_custom_call" | custom-call | flops 4294967296 | bytes 4194304 | tf_op jit(solution)/shard_map/grid_attention/pallas_call | solution.py:369
  65.7 29.3 %all_to_all.11 = bf16[32,32,512]{2,1,0:T(8,128)(2,1)S(1)} all-to-all(bf16[32,32,512]{2,1,0:T(8,128)(2,1)S(1)} %bitcast.20), channel_id=1, replica_groups=mesh['ns'=8,'ew'=4] {'ns','ew'}, dimensions={0} | all-to-all | bytes 2097152 | tf_op jit(solution)/shard_map/all_to_all | solution.py:408
  95.0 1.1 %copy.14 = bf16[8,4,2,2,8,512]{5,4,1,3,2,0:T(8,128)(2,1)} copy(bf16[8,4,2,2,8,512]{5,4,3,2,1,0:T(8,128)(2,1)S(1)} %bitcast.26) | data formatting | bytes 2097152 | tf_op jit(solution)/shard_map/reshape | solution.py:460
  (6 shorter events, 0.1 us)
Async XLA Ops:
  1.0 9.3 %collective-permute-start.1 = (bf16[128,512]{1,0:T(8,128)(2,1)S(1)}, bf16[128,512]{1,0:T(8,128)(2,1)S(1)}, u32[]{:S(2)}, u32[]{:S(2)}) collective-permute-start(bf16[128,512]{1,0:T(8,128)(2,1)S(1)} %get-tuple-element.19), channel_id=1, source_target_pairs={{4,8},{12,16},{20,24},{8,4},{16,12},{24,20},{5,9},{13,17},{21,25},... | collective-permute-start | bytes 393224 | tf_op jit(solution)/shard_map/ppermute | solution.py:389
  1.7 8.7 %collective-permute-start = (bf16[128,512]{1,0:T(8,128)(2,1)S(1)}, bf16[128,512]{1,0:T(8,128)(2,1)S(1)}, u32[]{:S(2)}, u32[]{:S(2)}) collective-permute-start(bf16[128,512]{1,0:T(8,128)(2,1)S(1)} %get-tuple-element.20), channel_id=1, source_target_pairs={{0,4},{8,12},{16,20},{24,28},{4,0},{12,8},{20,16},{28,24},{1,5},{9... | collective-permute-start | bytes 393224 | tf_op jit(solution)/shard_map/ppermute | solution.py:389
  6.9 1.2 %copy-start.1 = (bf16[8,128,512]{2,1,0:T(8,128)(2,1)S(1)}, bf16[8,128,512]{2,1,0:T(8,128)(2,1)}, u32[]{:S(2)}) copy-start(bf16[8,128,512]{2,1,0:T(8,128)(2,1)} %x_ref.1) | copy-start | bytes 3145732
  8.2 0.7 copy-start.2
  8.8 6.9 %copy-start = (bf16[512,2048]{1,0:T(8,128)(2,1)S(1)}, bf16[512,2048]{1,0:T(8,128)(2,1)}, u32[]{:S(2)}) copy-start(bf16[512,2048]{1,0:T(8,128)(2,1)} %w1_ref.3) | copy-start | bytes 6291460
  8.8 6.9 %copy-start.3 = (f32[512]{0:T(512)S(1)}, f32[512]{0:T(512)}, u32[]{:S(2)}) copy-start(f32[512]{0:T(512)} %param.12) | copy-start | bytes 6148
  8.8 8.6 %copy-start.5 = (bf16[512,1536]{1,0:T(8,128)(2,1)S(1)}, bf16[512,1536]{1,0:T(8,128)(2,1)}, u32[]{:S(2)}) copy-start(bf16[512,1536]{1,0:T(8,128)(2,1)} %wqkv_ref.2) | copy-start | bytes 4718596
  10.2 7.2 %copy-start.4 = (bf16[2048,512]{1,0:T(8,128)(2,1)S(1)}, bf16[2048,512]{1,0:T(8,128)(2,1)}, u32[]{:S(2)}) copy-start(bf16[2048,512]{1,0:T(8,128)(2,1)} %w2_ref.1) | copy-start | bytes 6291460
  10.3 7.2 %copy-start.7 = (bf16[512,512]{1,0:T(8,128)(2,1)S(1)}, bf16[512,512]{1,0:T(8,128)(2,1)}, u32[]{:S(2)}) copy-start(bf16[512,512]{1,0:T(8,128)(2,1)} %wout_ref.2) | copy-start | bytes 1572868
  10.3 7.2 %copy-start.9 = (f32[3,3,2048]{2,1,0:T(4,128)S(1)}, f32[3,3,2048]{2,1,0:T(4,128)}, u32[]{:S(2)}) copy-start(f32[3,3,2048]{2,1,0:T(4,128)} %dw_ref.1) | copy-start | bytes 221188
  10.3 7.2 %copy-start.10 = (f32[512]{0:T(512)S(1)}, f32[512]{0:T(512)}, u32[]{:S(2)}) copy-start(f32[512]{0:T(512)} %param.16) | copy-start | bytes 6148
  10.4 6.4 %collective-permute-start.3 = (bf16[10,512]{1,0:T(8,128)(2,1)S(1)}, bf16[10,512]{1,0:T(8,128)(2,1)S(1)}, u32[]{:S(2)}, u32[]{:S(2)}) collective-permute-start(bf16[10,512]{1,0:T(8,128)(2,1)S(1)} %get-tuple-element.25), channel_id=1, source_target_pairs={{1,2},{2,1},{5,6},{6,5},{9,10},{10,9},{13,14},{14,13},{17,18},{18,... | collective-permute-start | bytes 30728 | tf_op jit(solution)/shard_map/ppermute | solution.py:389
  11.2 6.2 %collective-permute-start.2 = (bf16[10,512]{1,0:T(8,128)(2,1)S(1)}, bf16[10,512]{1,0:T(8,128)(2,1)S(1)}, u32[]{:S(2)}, u32[]{:S(2)}) collective-permute-start(bf16[10,512]{1,0:T(8,128)(2,1)S(1)} %get-tuple-element.26), channel_id=1, source_target_pairs={{0,1},{2,3},{1,0},{3,2},{4,5},{6,7},{5,4},{7,6},{8,9},{10,11},{9,8... | collective-permute-start | bytes 30728 | tf_op jit(solution)/shard_map/ppermute | solution.py:389
  30.6 28.8 %copy-start.6 = (bf16[512,1536]{1,0:T(8,128)(2,1)S(1)}, bf16[512,1536]{1,0:T(8,128)(2,1)}, u32[]{:S(2)}) copy-start(bf16[512,1536]{1,0:T(8,128)(2,1)} %wqkv_ref.3) | copy-start | bytes 4718596
  30.6 28.8 %copy-start.8 = (bf16[512,512]{1,0:T(8,128)(2,1)S(1)}, bf16[512,512]{1,0:T(8,128)(2,1)}, u32[]{:S(2)}) copy-start(bf16[512,512]{1,0:T(8,128)(2,1)} %wout_ref.3) | copy-start | bytes 1572868
  30.6 28.8 %copy-start.11 = (f32[512]{0:T(512)S(1)}, f32[512]{0:T(512)}, u32[]{:S(2)}) copy-start(f32[512]{0:T(512)} %param.19) | copy-start | bytes 6148
